TPU v7x, 32 devices: a whole 2x2x4 slice. The times are simulated.
32 devices in a mesh: dp: 8 (over z, x), rep: 4 (over y, core).
Axes of the slice: x: 2, y: 2, z: 4, core: 2. Of those that a mesh axis runs over, the one named last changes fastest.
Arguments:
- hidden_in: bfloat16 [64, 256, 1152], P(('dp', 'rep')), may hold values from -6 to 6
- condition: bfloat16 [64, 1152], P(('dp', 'rep')), may hold values from -6 to 6
- patch_mask: int32 [64, 256], P(('dp', 'rep')), may hold values from 0 to 1, as said below
- image_counts: int32 [32], P(('dp', 'rep')), may hold values from 1 to 2, as said below
- modulation_weight: bfloat16 [1152, 6912], P('dp'), may hold values from -0.1875 to 0.1875
- modulation_bias: bfloat16 [6912], P('dp'), may hold values from -3 to 3
- attend_weight: bfloat16 [1152, 3456], P('dp'), may hold values from -0.1875 to 0.1875
- attend_bias: bfloat16 [2, 1152], P(None, 'dp'), may hold values from -3 to 3
- output_weight: bfloat16 [1152, 1152], P('dp'), may hold values from -0.75 to 0.75
- output_bias: bfloat16 [1152], P('dp'), may hold values from -3 to 3
- expand_weight: bfloat16 [1152, 4608], P('dp'), may hold values from -0.1875 to 0.1875
- expand_bias: bfloat16 [4608], P('dp'), may hold values from -3 to 3
- shrink_weight: bfloat16 [4608, 1152], P('dp'), may hold values from -0.09375 to 0.09375
- shrink_bias: bfloat16 [1152], P('dp'), may hold values from -3 to 3
- cotangent: bfloat16 [64, 256, 1152], P(('dp', 'rep')), may hold values from -6 to 6
Outputs:
- layer_out: bfloat16 [64, 256, 1152], P(('dp', 'rep'))
- gradient_hidden: float32 [64, 256, 1152], P(('dp', 'rep'))
- gradient_condition: float32 [64, 1152], P(('dp', 'rep'))
- gradient_modulation_weight: float32 [1152, 6912], P('dp')
- gradient_modulation_bias: float32 [6912], P('dp')
- gradient_attend_weight: float32 [1152, 3456], P('dp')
- gradient_attend_bias: float32 [2, 1152], P(None, 'dp')
- gradient_output_weight: float32 [1152, 1152], P('dp')
- gradient_output_bias: float32 [1152], P('dp')
- gradient_expand_weight: float32 [1152, 4608], P('dp')
- gradient_expand_bias: float32 [4608], P('dp')
- gradient_shrink_weight: float32 [4608, 1152], P('dp')
- gradient_shrink_bias: float32 [1152], P('dp')
Inputs may be any that keep to these rules, and one draw needn't show every extreme that they name: `patch_mask`: in each image the valid patches form a prefix of 128 patches or more; some image has exactly 128. `image_counts`: each device holds 1 to 2 images in its first slots; some device holds 2 and some device holds 1.
All inputs are finite; a program needn't handle non-finite values.
Results may differ from a plain program's by a relative error of at most 0.015.
The roundings to bfloat16 on the way count: a program that leaves them out, or rounds other values in their place, can miss the bound.
Values may be sent and summed in bfloat16 or wider, within the bound.
No kernel may reach another device: no remote copies, remote signals or barrier semaphores. Data moves between devices by JAX's collectives and lax.ppermute only.
A program may use at most 384 MiB of HBM per device.

v0:
```python
from functools import partial

import jax
import jax.numpy as jnp
from jax import lax
from jax.sharding import PartitionSpec as P

HEADS = 16


epsilon = 1e-06
masked_score = -1e30


def layer_norm(values):
    centered = values - jnp.mean(values, -1, keepdims=True)
    variance = jnp.mean(centered * centered, -1, keepdims=True)
    return centered * lax.rsqrt(variance + epsilon)


def modulate(values, shift_part, scale_part):
    return layer_norm(values) * (1.0 + scale_part) + shift_part


def inner_rows(left_side, right_side):
    return lax.dot_general(
        left_side, right_side, (((0,), (0,)), ((), ())), preferred_element_type=jnp.float32
    )


def times_transposed(left_side, right_side):
    return lax.dot_general(
        left_side, right_side, (((1,), (1,)), ((), ())), preferred_element_type=jnp.float32
    )


def per_device(
    hidden_in,
    condition,
    patch_mask,
    image_counts,
    modulation_weight,
    modulation_bias,
    attend_weight,
    attend_bias,
    output_weight,
    output_bias,
    expand_weight,
    expand_bias,
    shrink_weight,
    shrink_bias,
    cotangent,
):
    slot_count, patch_count, model_width = hidden_in.shape
    head_count = HEADS
    head_dim = model_width // head_count
    row_count = slot_count * patch_count
    score_scale = head_dim ** (-0.5)
    key_valid = (patch_mask > 0)[:, None, None, :]
    live_images = (jnp.arange(slot_count) < image_counts[0]).astype(jnp.float32)
    (
        modulation_full,
        modulation_bias_full,
        attend_full,
        attend_bias_full,
        output_full,
        output_bias_full,
    ) = (
        lax.all_gather(modulation_weight, "dp", axis=0, tiled=True),
        lax.all_gather(modulation_bias, "dp", axis=0, tiled=True),
        lax.all_gather(attend_weight, "dp", axis=0, tiled=True),
        lax.all_gather(attend_bias, "dp", axis=1, tiled=True),
        lax.all_gather(output_weight, "dp", axis=0, tiled=True),
        lax.all_gather(output_bias, "dp", axis=0, tiled=True),
    )
    hidden = hidden_in.astype(jnp.float32)
    condition_f = condition.astype(jnp.float32)
    cond_act, silu_back = jax.vjp(jax.nn.silu, condition_f)
    cond_low = cond_act.astype(jnp.bfloat16)
    modulation = (
        jnp.dot(cond_low, modulation_full, preferred_element_type=jnp.float32)
        + modulation_bias_full
    )
    pieces = modulation.reshape(slot_count, 6, 1, model_width)
    shift_one = pieces[:, 0]
    scale_one = pieces[:, 1]
    gate_one = pieces[:, 2]
    shift_two = pieces[:, 3]
    scale_two = pieces[:, 4]
    gate_two = pieces[:, 5]
    normed_value, back_one = jax.vjp(modulate, hidden, shift_one, scale_one)
    normed_one = normed_value.astype(jnp.bfloat16).reshape(row_count, model_width)
    bias_full = jnp.concatenate(
        [
            attend_bias_full[0].astype(jnp.float32),
            jnp.zeros((model_width,), jnp.float32),
            attend_bias_full[1].astype(jnp.float32),
        ]
    )
    triple = jnp.dot(normed_one, attend_full, preferred_element_type=jnp.float32) + bias_full
    triple_low = triple.astype(jnp.bfloat16).reshape(
        slot_count, patch_count, 3, head_count, head_dim
    )
    queries = triple_low[:, :, 0]
    keys_all = triple_low[:, :, 1]
    values_all = triple_low[:, :, 2]

    def attention_scores(query_low, key_low):
        raw = (
            jnp.einsum("sqhd,skhd->shqk", query_low, key_low, preferred_element_type=jnp.float32)
            * score_scale
        )
        return jnp.where(key_valid, raw, masked_score)

    scores = attention_scores(queries, keys_all)
    row_peak = jnp.max(scores, -1, keepdims=True)
    exponent = jnp.exp(scores - row_peak)
    row_total = jnp.sum(exponent, -1, keepdims=True)
    probs_low = (exponent / row_total).astype(jnp.bfloat16)
    log_total = row_peak + jnp.log(row_total)
    attended = jnp.einsum(
        "shqk,skhd->sqhd", probs_low, values_all, preferred_element_type=jnp.float32
    )
    attended_low = attended.reshape(row_count, model_width).astype(jnp.bfloat16)
    branch = (
        jnp.dot(attended_low, output_full, preferred_element_type=jnp.float32) + output_bias_full
    )
    branch = branch.reshape(slot_count, patch_count, model_width)
    middle = hidden + gate_one * branch
    expand_full, expand_bias_full, shrink_full, shrink_bias_full = (
        lax.all_gather(expand_weight, "dp", axis=0, tiled=True),
        lax.all_gather(expand_bias, "dp", axis=0, tiled=True),
        lax.all_gather(shrink_weight, "dp", axis=0, tiled=True),
        lax.all_gather(shrink_bias, "dp", axis=0, tiled=True),
    )
    normed_two_value, back_two = jax.vjp(modulate, middle, shift_two, scale_two)
    normed_two = normed_two_value.astype(jnp.bfloat16).reshape(row_count, model_width)
    inner = jnp.dot(normed_two, expand_full, preferred_element_type=jnp.float32) + expand_bias_full
    active, gelu_back = jax.vjp(partial(jax.nn.gelu, approximate=True), inner)
    active_low = active.astype(jnp.bfloat16)
    mlp_out = (
        jnp.dot(active_low, shrink_full, preferred_element_type=jnp.float32) + shrink_bias_full
    )
    mlp_out = mlp_out.reshape(slot_count, patch_count, model_width)
    layer_out = (live_images[:, None, None] * (middle + gate_two * mlp_out)).astype(jnp.bfloat16)
    slope = cotangent.astype(jnp.float32) * live_images[:, None, None]
    shrink_slope = (slope * gate_two).astype(jnp.bfloat16).reshape(row_count, model_width)
    gate_two_slope = jnp.sum(slope * mlp_out, axis=1)
    expand_back, shrink_back = (
        lax.all_gather(expand_weight, "dp", axis=0, tiled=True),
        lax.all_gather(shrink_weight, "dp", axis=0, tiled=True),
    )
    active_slope = times_transposed(shrink_slope, shrink_back)
    inner_low = gelu_back(active_slope)[0].astype(jnp.bfloat16)
    feed_parts = (
        lax.psum_scatter(inner_rows(normed_two, inner_low), "dp", scatter_dimension=0, tiled=True),
        lax.psum_scatter(
            jnp.sum(inner_low, 0, dtype=jnp.float32), "dp", scatter_dimension=0, tiled=True
        ),
        lax.psum_scatter(
            inner_rows(active_low, shrink_slope), "dp", scatter_dimension=0, tiled=True
        ),
        lax.psum_scatter(
            jnp.sum(shrink_slope, 0, dtype=jnp.float32), "dp", scatter_dimension=0, tiled=True
        ),
    )
    normed_two_slope = times_transposed(inner_low, expand_back).reshape(
        slot_count, patch_count, model_width
    )
    middle_extra, shift_two_slope, scale_two_slope = back_two(normed_two_slope)
    middle_slope = slope + middle_extra
    gate_one_slope = jnp.sum(middle_slope * branch, axis=1)
    branch_low = (middle_slope * gate_one).astype(jnp.bfloat16).reshape(row_count, model_width)
    modulation_back, attend_back, output_back = (
        lax.all_gather(modulation_weight, "dp", axis=0, tiled=True),
        lax.all_gather(attend_weight, "dp", axis=0, tiled=True),
        lax.all_gather(output_weight, "dp", axis=0, tiled=True),
    )
    attended_slope = times_transposed(branch_low, output_back).astype(jnp.bfloat16)
    attended_slope = attended_slope.reshape(slot_count, patch_count, head_count, head_dim)
    probs_again = jnp.exp(attention_scores(queries, keys_all) - log_total)
    again_low = probs_again.astype(jnp.bfloat16)
    prob_slope = jnp.einsum(
        "sqhd,skhd->shqk", attended_slope, values_all, preferred_element_type=jnp.float32
    )
    value_slope = jnp.einsum(
        "shqk,sqhd->skhd", again_low, attended_slope, preferred_element_type=jnp.float32
    )
    score_slope = (
        probs_again * (prob_slope - jnp.sum(probs_again * prob_slope, -1, keepdims=True))
    ).astype(jnp.bfloat16)
    query_slope = (
        jnp.einsum("shqk,skhd->sqhd", score_slope, keys_all, preferred_element_type=jnp.float32)
        * score_scale
    )
    key_slope = (
        jnp.einsum("shqk,sqhd->skhd", score_slope, queries, preferred_element_type=jnp.float32)
        * score_scale
    )
    triple_slope = jnp.stack([query_slope, key_slope, value_slope], axis=2).astype(jnp.bfloat16)
    triple_slope = triple_slope.reshape(row_count, 3 * model_width)
    triple_sums = jnp.sum(triple_slope, 0, dtype=jnp.float32).reshape(3, model_width)
    pair_sums = jnp.stack([triple_sums[0], triple_sums[2]])
    normed_one_slope = times_transposed(triple_slope, attend_back).reshape(
        slot_count, patch_count, model_width
    )
    hidden_extra, shift_one_slope, scale_one_slope = back_one(normed_one_slope)
    gradient_hidden = middle_slope + hidden_extra
    modulation_slope = (
        jnp.concatenate(
            [
                shift_one_slope,
                scale_one_slope,
                gate_one_slope[:, None],
                shift_two_slope,
                scale_two_slope,
                gate_two_slope[:, None],
            ],
            axis=1,
        )
        .reshape(slot_count, 6 * model_width)
        .astype(jnp.bfloat16)
    )
    cond_slope = times_transposed(modulation_slope, modulation_back)
    gradient_condition = silu_back(cond_slope)[0]
    modulation_sums = jnp.sum(modulation_slope, 0, dtype=jnp.float32)
    output_sums = jnp.sum(branch_low, 0, dtype=jnp.float32)
    attention_parts = (
        lax.psum_scatter(
            inner_rows(cond_low, modulation_slope), "dp", scatter_dimension=0, tiled=True
        ),
        lax.psum_scatter(modulation_sums, "dp", scatter_dimension=0, tiled=True),
        lax.psum_scatter(
            inner_rows(normed_one, triple_slope), "dp", scatter_dimension=0, tiled=True
        ),
        lax.psum_scatter(pair_sums, "dp", scatter_dimension=1, tiled=True),
        lax.psum_scatter(
            inner_rows(attended_low, branch_low), "dp", scatter_dimension=0, tiled=True
        ),
        lax.psum_scatter(output_sums, "dp", scatter_dimension=0, tiled=True),
    )
    copy_summed = (
        lax.psum_scatter(
            attention_parts[0].astype(jnp.bfloat16), "rep", scatter_dimension=1, tiled=True
        ).astype(jnp.float32),
        lax.psum_scatter(
            attention_parts[2].astype(jnp.bfloat16), "rep", scatter_dimension=1, tiled=True
        ).astype(jnp.float32),
        lax.psum_scatter(
            attention_parts[4].astype(jnp.bfloat16), "rep", scatter_dimension=1, tiled=True
        ).astype(jnp.float32),
        lax.psum_scatter(
            feed_parts[0].astype(jnp.bfloat16), "rep", scatter_dimension=1, tiled=True
        ).astype(jnp.float32),
        lax.psum_scatter(
            feed_parts[2].astype(jnp.bfloat16), "rep", scatter_dimension=1, tiled=True
        ).astype(jnp.float32),
    )
    collected = (
        lax.all_gather(copy_summed[0].astype(jnp.bfloat16), "rep", axis=1, tiled=True).astype(
            jnp.float32
        ),
        lax.all_gather(copy_summed[1].astype(jnp.bfloat16), "rep", axis=1, tiled=True).astype(
            jnp.float32
        ),
        lax.all_gather(copy_summed[2].astype(jnp.bfloat16), "rep", axis=1, tiled=True).astype(
            jnp.float32
        ),
        lax.all_gather(copy_summed[3].astype(jnp.bfloat16), "rep", axis=1, tiled=True).astype(
            jnp.float32
        ),
        lax.all_gather(copy_summed[4].astype(jnp.bfloat16), "rep", axis=1, tiled=True).astype(
            jnp.float32
        ),
        lax.all_gather(
            attention_parts[1][None].astype(jnp.bfloat16), "rep", axis=0, tiled=True
        ).astype(jnp.float32),
        lax.all_gather(
            attention_parts[3][None].astype(jnp.bfloat16), "rep", axis=0, tiled=True
        ).astype(jnp.float32),
        lax.all_gather(
            attention_parts[5][None].astype(jnp.bfloat16), "rep", axis=0, tiled=True
        ).astype(jnp.float32),
        lax.all_gather(feed_parts[1][None].astype(jnp.bfloat16), "rep", axis=0, tiled=True).astype(
            jnp.float32
        ),
        lax.all_gather(feed_parts[3][None].astype(jnp.bfloat16), "rep", axis=0, tiled=True).astype(
            jnp.float32
        ),
    )
    slope_mod_weight = collected[0]
    slope_att_weight = collected[1]
    slope_out_weight = collected[2]
    slope_exp_weight = collected[3]
    slope_shr_weight = collected[4]
    slope_mod_bias = jnp.sum(collected[5], 0)
    slope_att_bias = jnp.sum(collected[6], 0)
    slope_out_bias = jnp.sum(collected[7], 0)
    slope_exp_bias = jnp.sum(collected[8], 0)
    slope_shr_bias = jnp.sum(collected[9], 0)
    return (
        layer_out,
        gradient_hidden,
        gradient_condition,
        slope_mod_weight,
        slope_mod_bias,
        slope_att_weight,
        slope_att_bias,
        slope_out_weight,
        slope_out_bias,
        slope_exp_weight,
        slope_exp_bias,
        slope_shr_weight,
        slope_shr_bias,
    )


def solution(mesh):
    return jax.shard_map(
        per_device,
        mesh=mesh,
        in_specs=(
            P(("dp", "rep"), None, None),
            P(("dp", "rep"), None),
            P(("dp", "rep"), None),
            P(("dp", "rep")),
            P("dp", None),
            P("dp"),
            P("dp", None),
            P(None, "dp"),
            P("dp", None),
            P("dp"),
            P("dp", None),
            P("dp"),
            P("dp", None),
            P("dp"),
            P(("dp", "rep"), None, None),
        ),
        out_specs=(
            P(("dp", "rep"), None, None),
            P(("dp", "rep"), None, None),
            P(("dp", "rep"), None),
            P("dp", None),
            P("dp"),
            P("dp", None),
            P(None, "dp"),
            P("dp", None),
            P("dp"),
            P("dp", None),
            P("dp"),
            P("dp", None),
            P("dp"),
        ),
        check_vma=False,
    )
```

profile of v0, /device:TPU:0, one launch (start us, length us, event | category | flops | bytes accessed | tf_op | source)
XLA Modules:
  0.0 2622.3 jit_solution(1794235225630277773)
XLA Ops:
  13.9 22.4 all-gather.5
  37.5 34.3 %all-reduce.13 = (bf16[6912]{0:T(1024)(128)(2,1)S(1)}, bf16[1152]{0:T(1024)(128)(2,1)S(1)}, bf16[4608]{0:T(1024)(128)(2,1)S(1)}, bf16[1152]{0:T(1024)(128)(2,1)}) all-reduce(bf16[6912]{0:T(1024)(128)(2,1)S(1)} %dynamic-update-slice, bf16[1152]{0:T(1024)(128)(2,1)S(1)} %dynamic-update-slice.1, ...), channel_id=1, replica_groups=mesh['dp'=8,'rep'=4] {'dp'}, use_global_device_ids=true, to_apply=%add | all-reduce | flops 13824 | bytes 55296
  73.8 156.9 %all-gather.19.cloned.1.call-done = bf16[1152,6912]{1,0:T(8,128)(2,1)} async-done(((bf16[144,6912]{1,0:T(8,128)(2,1)}), bf16[1152,6912]{1,0:T(8,128)(2,1)}) %all-gather.19.cloned.1.call-update) | async-done | bytes 15925264 | tf_op jit(solution)/shard_map/all_gather | solution.py:69
  240.9 109.8 %all-gather.21.cloned.1.call-done = bf16[1152,3456]{1,0:T(8,128)(2,1)} async-done(((bf16[144,3456]{1,0:T(8,128)(2,1)}), bf16[1152,3456]{1,0:T(8,128)(2,1)}) %all-gather.21.cloned.1.call-update) | async-done | bytes 7962640 | tf_op jit(solution)/shard_map/all_gather | solution.py:71
  350.7 9.5 add_convert_fusion
  360.3 13.6 reshape.294
  416.0 143.3 %all-gather.25.cloned.1.call-done = bf16[1152,4608]{1,0:T(8,128)(2,1)} async-done(((bf16[144,4608]{1,0:T(8,128)(2,1)}), bf16[1152,4608]{1,0:T(8,128)(2,1)}) %all-gather.25.cloned.1.call-update) | async-done | bytes 10616848 | tf_op jit(solution)/shard_map/all_gather | solution.py:131
  559.3 9.4 fusion.69
  572.4 12.2 fusion.62
  584.6 127.4 %all-gather.27.cloned.1.call-done = bf16[4608,1152]{1,0:T(8,128)(2,1)} async-done(((bf16[576,1152]{1,0:T(8,128)(2,1)}), bf16[4608,1152]{1,0:T(8,128)(2,1)}) %all-gather.27.cloned.1.call-update) | async-done | bytes 10616848 | tf_op jit(solution)/shard_map/all_gather | solution.py:133
  712.0 16.3 convert_reduce_fusion
  730.5 10.2 fusion.73
  741.4 10.1 fusion.70
  754.0 13.3 convolution_add_fusion.1
  801.1 8.9 fusion.26
  814.9 12.7 fusion.57
  848.2 212.9 %reduce-scatter.32.cloned.1.call-done = f32[576,1152]{1,0:T(8,128)} async-done(((f32[4608,1152]{1,0:T(8,128)}), f32[576,1152]{1,0:T(8,128)}) %reduce-scatter.32.cloned.1.call-update) | async-done | bytes 2654224 | tf_op jit(solution)/shard_map/reduce_scatter | solution.py:160
  1064.8 347.2 %reduce-scatter.30.cloned.1.call-done = f32[144,4608]{1,0:T(8,128)} async-done(((f32[1152,4608]{1,0:T(8,128)}), f32[144,4608]{1,0:T(8,128)}) %reduce-scatter.30.cloned.1.call-update) | async-done | bytes 2654224 | tf_op jit(solution)/shard_map/reduce_scatter | solution.py:156
  1416.3 511.0 %reduce-scatter.24.cloned.1.call-done = f32[144,6912]{1,0:T(8,128)} async-done(((f32[1152,6912]{1,0:T(8,128)}), f32[144,6912]{1,0:T(8,128)}) %reduce-scatter.24.cloned.1.call-update) | async-done | bytes 3981328 | tf_op jit(solution)/shard_map/reduce_scatter | solution.py:229
  1934.7 99.6 %reduce-scatter.28.cloned.1.call-done = f32[144,1152]{1,0:T(8,128)} async-done(((f32[1152,1152]{1,0:T(8,128)}), f32[144,1152]{1,0:T(8,128)}) %reduce-scatter.28.cloned.1.call-update) | async-done | bytes 663568 | tf_op jit(solution)/shard_map/reduce_scatter | solution.py:237
  2036.5 271.0 %reduce-scatter.26.cloned.1.call-done = f32[144,3456]{1,0:T(8,128)} async-done(((f32[1152,3456]{1,0:T(8,128)}), f32[144,3456]{1,0:T(8,128)}) %reduce-scatter.26.cloned.1.call-update) | async-done | bytes 1990672 | tf_op jit(solution)/shard_map/reduce_scatter | solution.py:233
  2311.0 26.5 %reduce-scatter.44.cloned.1.call-done = bf16[288,576]{1,0:T(8,128)(2,1)} async-done(((bf16[1152,576]{1,0:T(8,128)(2,1)}), bf16[288,576]{1,0:T(8,128)(2,1)}) %reduce-scatter.44.cloned.1.call-update) | async-done | bytes 331792
  2337.6 36.0 %reduce-scatter.42.cloned.1.call-done = bf16[1152,144]{1,0:T(8,128)(2,1)} async-done(((bf16[4608,144]{1,0:T(8,128)(2,1)}), bf16[1152,144]{1,0:T(8,128)(2,1)}) %reduce-scatter.42.cloned.1.call-update) | async-done | bytes 331792
  2375.6 41.7 %reduce-scatter.34.cloned.1.call-done = bf16[1728,144]{1,0:T(8,128)(2,1)} async-done(((bf16[6912,144]{1,0:T(8,128)(2,1)}), bf16[1728,144]{1,0:T(8,128)(2,1)}) %reduce-scatter.34.cloned.1.call-update) | async-done | bytes 497680
  2424.2 38.0 %all-reduce.12 = (bf16[6912]{0:T(1024)(128)(2,1)S(1)}, bf16[1152]{0:T(1024)(128)(2,1)S(1)}, bf16[4608]{0:T(1024)(128)(2,1)S(1)}, bf16[1152]{0:T(1024)(128)(2,1)S(1)}) all-reduce(f32[6912]{0:T(1024)S(1)} %reduce_sum.269, f32[1152]{0:T(1024)S(1)} %copy-done.50, f32[4608]{0:T(1024)S(1)} %copy-done.53, ...), channel_id=9, replica_groups=mesh['dp'=8,'rep'=4] {'dp'}, use_global_device_ids=true, to_apply=%region_20.21.clone | all-reduce | flops 13824 | bytes 82944
  2463.3 10.4 all-reduce.14
  2476.4 10.4 fusion.48
  2493.4 13.4 reduce-scatter.40.cloned.1.call-done
  2515.6 23.8 reduce-scatter.36.cloned.1.call-done
  2540.6 9.5 all-gather.7
  2562.9 17.4 all-gather.29.cloned.1.call-done
  2583.4 21.5 all-gather.33.cloned.1.call-done
  (326 shorter events, 199.8 us)
Async XLA Ops:
  7.2 223.6 %all-gather.19.cloned.1.call-start = ((), (), s32[]{:S(2)}) async-start(), calls=%async_computation.11 | async-start | bytes 17915904 | tf_op jit(solution)/shard_map/all_gather | solution.py:69
  8.0 65.1 %copy-start.1 = (bf16[2,256,1152]{2,1,0:T(8,128)(2,1)S(1)}, bf16[2,256,1152]{2,1,0:T(8,128)(2,1)}, u32[]{:S(2)}) copy-start(bf16[2,256,1152]{2,1,0:T(8,128)(2,1)} %param.15) | copy-start | bytes 3538948
  8.0 342.7 %all-gather.21.cloned.1.call-start = ((), (), s32[]{:S(2)}) async-start(), calls=%async_computation.12 | async-start | bytes 8957952 | tf_op jit(solution)/shard_map/all_gather | solution.py:71
  8.7 397.4 %all-gather.23.cloned.1.call-start = ((), (), s32[]{:S(2)}) async-start(), calls=%async_computation.13 | async-start | bytes 2985984 | tf_op jit(solution)/shard_map/all_gather | solution.py:73
  9.5 221.3 %copy-start.38 = (bf16[2,1152]{1,0:T(2,128)(2,1)S(1)}, bf16[2,1152]{1,0:T(2,128)(2,1)}, u32[]{:S(2)}) copy-start(bf16[2,1152]{1,0:T(2,128)(2,1)} %param.16) | copy-start | bytes 13828
  9.5 549.8 %all-gather.25.cloned.1.call-start = ((), (), s32[]{:S(2)}) async-start(), calls=%async_computation.14 | async-start | bytes 11943936 | tf_op jit(solution)/shard_map/all_gather | solution.py:131
  10.1 701.9 %all-gather.27.cloned.1.call-start = ((), (), s32[]{:S(2)}) async-start(), calls=%async_computation.15 | async-start | bytes 11943936 | tf_op jit(solution)/shard_map/all_gather | solution.py:133
  10.7 1050.5 %reduce-scatter.32.cloned.1.call-start = ((), (), s32[]{:S(2)}) async-start(), calls=%async_computation.21 | async-start | bytes 23887872 | tf_op jit(solution)/shard_map/reduce_scatter | solution.py:160
  73.3 167.1 %copy-start.40 = (f32[2,256]{1,0:T(2,128)}, f32[2,256]{1,0:T(2,128)S(1)}, u32[]{:S(2)}) copy-start(f32[2,256]{1,0:T(2,128)S(1)} %broadcast_multiply_fusion.1) | copy-start | bytes 6148
  73.7 164.7 %copy-start.59 = (f32[2,256]{1,0:T(2,128)}, f32[2,256]{1,0:T(2,128)S(1)}, u32[]{:S(2)}) copy-start(f32[2,256]{1,0:T(2,128)S(1)} %fusion.25) | copy-start | bytes 6148
  73.8 319.8 %copy-start.42 = (pred[2,256]{1,0:T(4,128)(4,1)}, pred[2,256]{1,0:T(4,128)(4,1)S(1)}, u32[]{:S(2)}) copy-start(pred[2,256]{1,0:T(4,128)(4,1)S(1)} %broadcast_compare_fusion) | copy-start | bytes 1540
  73.8 166.6 %copy-start.51 = (f32[2,256]{1,0:T(2,128)}, f32[2,256]{1,0:T(2,128)S(1)}, u32[]{:S(2)}) copy-start(f32[2,256]{1,0:T(2,128)S(1)} %fusion.51) | copy-start | bytes 6148
  239.2 121.1 %copy-start.29 = (f32[2,1,1,1152]{3,0,1,2:T(2,128)}, f32[2,1,1,1152]{3,0,1,2:T(2,128)S(1)}, u32[]{:S(2)}) copy-start(f32[2,1,1,1152]{3,0,1,2:T(2,128)S(1)} %copy.136) | copy-start | bytes 27652
  240.9 119.4 %copy-start.23 = (bf16[2,256,1152]{2,1,0:T(8,128)(2,1)}, bf16[2,256,1152]{2,1,0:T(8,128)(2,1)S(1)}, u32[]{:S(2)}) copy-start(bf16[2,256,1152]{2,1,0:T(8,128)(2,1)S(1)} %fusion.23) | copy-start | bytes 3538948
  584.6 827.4 %reduce-scatter.30.cloned.1.call-start = ((), (), s32[]{:S(2)}) async-start(), calls=%async_computation.19 | async-start | bytes 23887872 | tf_op jit(solution)/shard_map/reduce_scatter | solution.py:156
  740.7 1186.6 %reduce-scatter.24.cloned.1.call-start = ((), (), s32[]{:S(2)}) async-start(), calls=%async_computation.16 | async-start | bytes 35831808 | tf_op jit(solution)/shard_map/reduce_scatter | solution.py:229
  827.6 1206.7 %reduce-scatter.28.cloned.1.call-start = ((), (), s32[]{:S(2)}) async-start(), calls=%async_computation.18 | async-start | bytes 5971968 | tf_op jit(solution)/shard_map/reduce_scatter | solution.py:237
  833.3 1474.3 %reduce-scatter.26.cloned.1.call-start = ((), (), s32[]{:S(2)}) async-start(), calls=%async_computation.17 | async-start | bytes 17915904 | tf_op jit(solution)/shard_map/reduce_scatter | solution.py:233
  848.2 1489.3 %reduce-scatter.44.cloned.1.call-start = ((), (), s32[]{:S(2)}) async-start(), calls=%async_computation.29 | async-start | bytes 1843200
  1064.7 1308.8 %reduce-scatter.42.cloned.1.call-start = ((), (), s32[]{:S(2)}) async-start(), calls=%async_computation.28 | async-start | bytes 2949120
  1416.2 1001.1 %reduce-scatter.34.cloned.1.call-start = ((), (), s32[]{:S(2)}) async-start(), calls=%async_computation.24 | async-start | bytes 4423680
  1932.6 554.2 %reduce-scatter.38.cloned.1.call-start = ((), (), s32[]{:S(2)}) async-start(), calls=%async_computation.26 | async-start | bytes 663552
  1934.6 572.2 %reduce-scatter.40.cloned.1.call-start = ((), (), s32[]{:S(2)}) async-start(), calls=%async_computation.27 | async-start | bytes 737280
  2036.5 502.9 %reduce-scatter.36.cloned.1.call-start = ((), (), s32[]{:S(2)}) async-start(), calls=%async_computation.25 | async-start | bytes 2211840
  2310.9 108.7 %copy-start.72 = (u32[32]{0:T(128)S(1)}, u32[32]{0:T(128)}, u32[]{:S(2)}) copy-start(u32[32]{0:T(128)} %constant.68) | copy-start | bytes 388
  2310.9 113.2 %copy-start.28 = (bf16[2,6,1152]{2,0,1:T(2,128)(2,1)S(1)}, bf16[2,6,1152]{2,0,1:T(2,128)(2,1)}, u32[]{:S(2)}) copy-start(bf16[2,6,1152]{2,0,1:T(2,128)(2,1)} %copy-done.27) | copy-start | bytes 82948
  2310.9 113.3 %copy-start.49 = (f32[1152]{0:T(1024)S(1)}, f32[1152]{0:T(1024)}, u32[]{:S(2)}) copy-start(f32[1152]{0:T(1024)} %get-tuple-element.61) | copy-start | bytes 13828
  2310.9 113.3 %copy-start.50 = (f32[1152]{0:T(1024)S(1)}, f32[1152]{0:T(1024)}, u32[]{:S(2)}) copy-start(f32[1152]{0:T(1024)} %get-tuple-element.65) | copy-start | bytes 13828
  2310.9 113.3 %copy-start.53 = (f32[4608]{0:T(1024)S(1)}, f32[4608]{0:T(1024)}, u32[]{:S(2)}) copy-start(f32[4608]{0:T(1024)} %get-tuple-element.63) | copy-start | bytes 55300
  2311.0 249.0 %all-gather.31.cloned.1.call-start = ((), (), s32[]{:S(2)}) async-start(), calls=%async_computation.22 | async-start | bytes 1843200 | tf_op jit(solution)/shard_map/all_gather | solution.py:272
  2337.6 242.7 %all-gather.29.cloned.1.call-start = ((), (), s32[]{:S(2)}) async-start(), calls=%async_computation.20 | async-start | bytes 1658880 | tf_op jit(solution)/shard_map/all_gather | solution.py:269
  2375.6 229.3 %all-gather.33.cloned.1.call-start = ((), (), s32[]{:S(2)}) async-start(), calls=%async_computation.23 | async-start | bytes 2580480 | tf_op jit(solution)/shard_map/all_gather | solution.py:260
  (63 other events, 435.0 us)
Sparse Core Ops, SparseCore 0:
  10.2 220.4 all-gather.18
  232.9 117.7 all-gather.20
  352.9 53.2 all-gather.22
  408.2 151.0 all-gather.24
  561.3 150.6 all-gather.26
  715.7 345.3 reduce-scatter.31
  1065.5 346.3 reduce-scatter.29
  1415.8 511.4 reduce-scatter.23
  1930.9 103.3 reduce-scatter.27
  2038.5 269.0 reduce-scatter.25
  2310.9 26.5 reduce-scatter.43
  2340.5 33.0 reduce-scatter.41
  2376.9 40.4 reduce-scatter.33
  2421.1 62.0 reduce-scatter.37
  2485.7 21.1 reduce-scatter.39
  2510.0 29.3 reduce-scatter.35
  2540.8 19.1 all-gather.30
  2562.0 18.2 all-gather.28
  2582.4 22.3 all-gather.32
where the time goes:
time: 2630 us; the launch traced here: 2620 us
  waiting for transfers between devices  2180 us (83%)
  matrix products  156 us (6%)
  blocking collectives  126 us (5%)
  local copies, waits for them, and re-layouts  101 us (4%)
  other arithmetic  39.4 us (1%)
    reduce_scatter x1, waiting for transfers between devices, per_device(): lax.psum_scatter(inner_rows(cond_low, modulation_slope), 'dp', scatter_di...  511 us
    reduce_scatter x1, waiting for transfers between devices, per_device(): lax.psum_scatter(inner_rows(normed_two, inner_low), 'dp', scatter_dimensi...  347 us
    reduce_scatter x1, waiting for transfers between devices, per_device(): lax.psum_scatter(inner_rows(normed_one, triple_slope), 'dp', scatter_dime...  271 us
    reduce_scatter x1, waiting for transfers between devices, per_device(): lax.psum_scatter(inner_rows(active_low, shrink_slope), 'dp', scatter_dime...  213 us
    all_gather x1, waiting for transfers between devices, per_device(): lax.all_gather(modulation_weight, 'dp', axis=0, tiled=True)  157 us
    unnamed x25, waiting for transfers between devices  145 us
    all_gather x1, waiting for transfers between devices, per_device(): lax.all_gather(expand_weight, 'dp', axis=0, tiled=True)  143 us
    all_gather x1, waiting for transfers between devices, per_device(): lax.all_gather(shrink_weight, 'dp', axis=0, tiled=True)  127 us
  transfers between devices with their start and end apart: 19, of which 18 were waited for; matrix products, arithmetic and copies ran while one was open for 10% of the time, Pallas kernels for 0%

commit v1 on v0

v1 whole, which is shorter than its diff:
```python
from functools import partial

import jax
import jax.numpy as jnp
from jax import lax
from jax.sharding import PartitionSpec as P

HEADS = 16


epsilon = 1e-06
masked_score = -1e30


def layer_norm(values):
    centered = values - jnp.mean(values, -1, keepdims=True)
    variance = jnp.mean(centered * centered, -1, keepdims=True)
    return centered * lax.rsqrt(variance + epsilon)


def modulate(values, shift_part, scale_part):
    return layer_norm(values) * (1.0 + scale_part) + shift_part


def inner_rows(left_side, right_side):
    return lax.dot_general(
        left_side, right_side, (((0,), (0,)), ((), ())), preferred_element_type=jnp.float32
    )


def times(left_side, right_side):
    return jnp.dot(left_side, right_side, preferred_element_type=jnp.float32)


def times_transposed(left_side, right_side):
    return lax.dot_general(
        left_side, right_side, (((1,), (1,)), ((), ())), preferred_element_type=jnp.float32
    )


class PermuteLinks:
    def __init__(self, dp):
        self.dp = dp
        self.depth = dp // 2
        here = lax.axis_index("dp")
        copy = lax.axis_index("rep")
        self.z = here // 2
        self.x = here % 2
        self.own = (copy % 2) * 2 + copy // 2
        self.order = [self.own ^ step for step in range(4)]

    def up(self, value):
        return lax.ppermute(value, "dp", [(i, (i + 2) % self.dp) for i in range(self.dp)])

    def swap_x(self, value):
        return lax.ppermute(value, "dp", [(i, i ^ 1) for i in range(self.dp)])

    def swap_y(self, value):
        return lax.ppermute(value, "rep", [(i, i ^ 2) for i in range(4)])

    def swap_core(self, value):
        return lax.ppermute(value, "rep", [(i, i ^ 1) for i in range(4)])

    def at_depth(self, step):
        return (self.z - step) % self.depth

    def pick(self, stacked, index):
        return lax.dynamic_index_in_dim(stacked, index, 0, keepdims=False)

    def collect(self, block):
        rows, columns = block.shape
        whole = jnp.zeros((self.dp, rows, columns), block.dtype)
        for step in range(self.depth):
            if step:
                block = self.up(block)
            place = 2 * self.at_depth(step)
            whole = lax.dynamic_update_slice(whole, block[None], (place + self.x, 0, 0))
            whole = lax.dynamic_update_slice(
                whole, self.swap_x(block)[None], (place + 1 - self.x, 0, 0)
            )
        return whole.reshape(self.dp * rows, columns)

    def gather(self, units, split_y):
        own = self.collect(self.pick(units, self.order[0]))
        if split_y:
            other = self.swap_y(own)
        else:
            other = self.collect(self.pick(units, self.order[1]))
        return [own, other, self.swap_core(own), self.swap_core(other)]

    def add(self, one, two):
        return (one.astype(jnp.float32) + two.astype(jnp.float32)).astype(jnp.bfloat16)

    def sum_shards(self, whole):
        rows = whole.shape[0] // self.dp
        cut = whole.reshape(self.depth, 2, rows, whole.shape[1])
        kept = lax.dynamic_index_in_dim(cut, self.x, 1, keepdims=False)
        sent = lax.dynamic_index_in_dim(cut, 1 - self.x, 1, keepdims=False)
        kept = self.add(kept, self.swap_x(sent))
        moving = self.pick(kept, self.at_depth(1))
        for step in range(2, self.depth + 1):
            moving = self.add(self.up(moving), self.pick(kept, self.at_depth(step)))
        return moving

    def reduce(self, wholes, split_y):
        own = self.add(wholes[0], self.swap_core(wholes[2]))
        other = self.add(wholes[1], self.swap_core(wholes[3]))
        if split_y:
            own = self.sum_shards(self.add(own, self.swap_y(other)))
            other = self.swap_y(own)
        else:
            own = self.sum_shards(own)
            other = self.sum_shards(other)
            own, other = self.add(own, self.swap_y(other)), self.add(other, self.swap_y(own))
        return [own, other, self.swap_core(own), self.swap_core(other)]


class PlainLinks:
    def __init__(self):
        self.order = [0, 1, 2, 3]

    def pick(self, stacked, index):
        return stacked[index]

    def gather(self, units, split_y):
        whole = lax.all_gather(units, "dp", axis=1, tiled=True)
        return [whole[0], whole[1], whole[2], whole[3]]

    def reduce(self, wholes, split_y):
        mine = lax.psum_scatter(jnp.stack(wholes), "dp", scatter_dimension=1, tiled=True)
        mine = lax.psum(mine, "rep")
        return [mine[0], mine[1], mine[2], mine[3]]


def in_order(links, units):
    whole = jnp.zeros((4,) + units[0].shape, units[0].dtype)
    for index, unit in zip(links.order, units):
        whole = lax.dynamic_update_slice(whole, unit[None], (index, 0, 0))
    return whole


def per_device(
    axis_sizes,
    hidden_in,
    condition,
    patch_mask,
    image_counts,
    modulation_weight,
    modulation_bias,
    attend_weight,
    attend_bias,
    output_weight,
    output_bias,
    expand_weight,
    expand_bias,
    shrink_weight,
    shrink_bias,
    cotangent,
):
    dp, rep = axis_sizes
    everyone = ("dp", "rep")
    here = lax.axis_index("dp")
    copy = lax.axis_index("rep")
    links = PermuteLinks(dp) if (dp == 8 and rep == 4) else PlainLinks()
    slot_count, patch_count, model_width = hidden_in.shape
    shard = modulation_weight.shape[0]
    inner_width = expand_weight.shape[1]
    head_count = HEADS
    head_dim = model_width // head_count
    row_count = slot_count * patch_count
    score_scale = head_dim ** (-0.5)
    key_valid = (patch_mask > 0)[:, None, None, :]
    live_images = (jnp.arange(slot_count) < image_counts[0]).astype(jnp.float32)

    attend_units = links.gather(
        jnp.concatenate(
            [attend_weight.reshape(shard, 3, model_width).transpose(1, 0, 2), output_weight[None]]
        ),
        False,
    )
    expand_units = links.gather(
        expand_weight.reshape(shard, dp, 4, shard).transpose(2, 0, 1, 3).reshape(4, shard, -1),
        True,
    )
    shrink_units = links.gather(
        shrink_weight.reshape(4, shard, model_width), True
    )
    query_full, key_full, value_full, output_full = in_order(links, attend_units)

    bias_sizes = (
        modulation_bias.shape[0],
        2 * shard,
        shard,
        expand_bias.shape[0],
        shard,
    )
    small = jnp.concatenate(
        [
            condition.reshape(-1),
            modulation_bias,
            attend_bias.reshape(-1),
            output_bias,
            expand_bias,
            shrink_bias,
        ]
    )
    small_all = lax.all_gather(small[None], everyone, axis=0, tiled=True).reshape(dp, rep, -1)
    cond_size = slot_count * model_width
    condition_all = small_all[:, :, :cond_size].reshape(dp, rep, slot_count, model_width)
    biases = small_all[:, 0, cond_size:].astype(jnp.float32)
    cuts = []
    start = 0
    for size in bias_sizes:
        cuts.append(biases[:, start : start + size])
        start += size
    modulation_bias_full = cuts[0].reshape(-1)
    attend_bias_full = cuts[1].reshape(dp, 2, shard).transpose(1, 0, 2).reshape(2, model_width)
    output_bias_full = cuts[2].reshape(-1)
    expand_bias_units = cuts[3].reshape(dp, 4, shard).transpose(1, 0, 2).reshape(4, -1)
    shrink_bias_full = cuts[4].reshape(-1)

    cond_rows = lax.dynamic_slice_in_dim(condition_all, here * shard, shard, 3)
    act_rows = jax.nn.silu(cond_rows.astype(jnp.float32)).astype(jnp.bfloat16)
    act_copy = lax.dynamic_index_in_dim(act_rows, copy, 1, keepdims=False)
    mod_terms = times(act_copy.reshape(dp * slot_count, shard), modulation_weight)
    modulation = (
        lax.psum_scatter(mod_terms, "dp", scatter_dimension=0, tiled=True) + modulation_bias_full
    )
    condition_f = condition.astype(jnp.float32)
    silu_back = jax.vjp(jax.nn.silu, condition_f)[1]

    hidden = hidden_in.astype(jnp.float32)
    pieces = modulation.reshape(slot_count, 6, 1, model_width)
    shift_one = pieces[:, 0]
    scale_one = pieces[:, 1]
    gate_one = pieces[:, 2]
    shift_two = pieces[:, 3]
    scale_two = pieces[:, 4]
    gate_two = pieces[:, 5]
    normed_value, back_one = jax.vjp(modulate, hidden, shift_one, scale_one)
    normed_one = normed_value.astype(jnp.bfloat16).reshape(row_count, model_width)

    def heads_of(flat):
        return flat.astype(jnp.bfloat16).reshape(slot_count, patch_count, head_count, head_dim)

    queries = heads_of(times(normed_one, query_full) + attend_bias_full[0])
    keys_all = heads_of(times(normed_one, key_full))
    values_all = heads_of(times(normed_one, value_full) + attend_bias_full[1])

    def attention_scores(query_low, key_low):
        raw = (
            jnp.einsum("sqhd,skhd->shqk", query_low, key_low, preferred_element_type=jnp.float32)
            * score_scale
        )
        return jnp.where(key_valid, raw, masked_score)

    scores = attention_scores(queries, keys_all)
    row_peak = jnp.max(scores, -1, keepdims=True)
    exponent = jnp.exp(scores - row_peak)
    row_total = jnp.sum(exponent, -1, keepdims=True)
    probs_low = (exponent / row_total).astype(jnp.bfloat16)
    log_total = row_peak + jnp.log(row_total)
    attended = jnp.einsum(
        "shqk,skhd->sqhd", probs_low, values_all, preferred_element_type=jnp.float32
    )
    attended_low = attended.reshape(row_count, model_width).astype(jnp.bfloat16)
    branch = times(attended_low, output_full) + output_bias_full
    branch = branch.reshape(slot_count, patch_count, model_width)
    middle = hidden + gate_one * branch
    normed_two_value, back_two = jax.vjp(modulate, middle, shift_two, scale_two)
    normed_two = normed_two_value.astype(jnp.bfloat16).reshape(row_count, model_width)

    slope = cotangent.astype(jnp.float32) * live_images[:, None, None]
    shrink_slope = (slope * gate_two).astype(jnp.bfloat16).reshape(row_count, model_width)
    mlp_out = shrink_bias_full
    normed_two_slope = 0.0
    expand_terms = []
    shrink_terms = []
    inner_sums = []
    for index, expand_unit, shrink_unit in zip(links.order, expand_units, shrink_units):
        inner = times(normed_two, expand_unit) + links.pick(expand_bias_units, index)
        active, gelu_back = jax.vjp(partial(jax.nn.gelu, approximate=True), inner)
        active_low = active.astype(jnp.bfloat16)
        mlp_out = mlp_out + times(active_low, shrink_unit)
        shrink_terms.append(inner_rows(active_low, shrink_slope).astype(jnp.bfloat16))
        active_slope = times_transposed(shrink_slope, shrink_unit)
        inner_low = gelu_back(active_slope)[0].astype(jnp.bfloat16)
        normed_two_slope = normed_two_slope + times_transposed(inner_low, expand_unit)
        expand_terms.append(inner_rows(normed_two, inner_low).astype(jnp.bfloat16))
        inner_sums.append(jnp.sum(inner_low, 0, dtype=jnp.float32))
    mlp_out = mlp_out.reshape(slot_count, patch_count, model_width)
    layer_out = (live_images[:, None, None] * (middle + gate_two * mlp_out)).astype(jnp.bfloat16)
    gate_two_slope = jnp.sum(slope * mlp_out, axis=1)
    shrink_sums = links.reduce(shrink_terms, True)
    expand_sums = links.reduce(expand_terms, False)
    normed_two_slope = normed_two_slope.reshape(slot_count, patch_count, model_width)
    middle_extra, shift_two_slope, scale_two_slope = back_two(normed_two_slope)
    middle_slope = slope + middle_extra
    gate_one_slope = jnp.sum(middle_slope * branch, axis=1)
    branch_low = (middle_slope * gate_one).astype(jnp.bfloat16).reshape(row_count, model_width)
    attended_slope = heads_of(times_transposed(branch_low, output_full))
    probs_again = jnp.exp(attention_scores(queries, keys_all) - log_total)
    again_low = probs_again.astype(jnp.bfloat16)
    prob_slope = jnp.einsum(
        "sqhd,skhd->shqk", attended_slope, values_all, preferred_element_type=jnp.float32
    )
    value_slope = jnp.einsum(
        "shqk,sqhd->skhd", again_low, attended_slope, preferred_element_type=jnp.float32
    )
    score_slope = (
        probs_again * (prob_slope - jnp.sum(probs_again * prob_slope, -1, keepdims=True))
    ).astype(jnp.bfloat16)
    query_slope = (
        jnp.einsum("shqk,skhd->sqhd", score_slope, keys_all, preferred_element_type=jnp.float32)
        * score_scale
    )
    key_slope = (
        jnp.einsum("shqk,sqhd->skhd", score_slope, queries, preferred_element_type=jnp.float32)
        * score_scale
    )

    def flat_of(by_head):
        return by_head.astype(jnp.bfloat16).reshape(row_count, model_width)

    query_low_slope = flat_of(query_slope)
    key_low_slope = flat_of(key_slope)
    value_low_slope = flat_of(value_slope)
    normed_one_slope = (
        times_transposed(query_low_slope, query_full)
        + times_transposed(key_low_slope, key_full)
        + times_transposed(value_low_slope, value_full)
    ).reshape(slot_count, patch_count, model_width)
    hidden_extra, shift_one_slope, scale_one_slope = back_one(normed_one_slope)
    gradient_hidden = middle_slope + hidden_extra

    rights = jnp.stack([query_low_slope, key_low_slope, value_low_slope, branch_low])
    lefts = jnp.stack([normed_one, normed_one, normed_one, attended_low])
    attend_terms = [
        inner_rows(links.pick(lefts, index), links.pick(rights, index)).astype(jnp.bfloat16)
        for index in links.order
    ]
    attend_sums = links.reduce(attend_terms, True)

    modulation_slope = (
        jnp.concatenate(
            [
                shift_one_slope,
                scale_one_slope,
                gate_one_slope[:, None],
                shift_two_slope,
                scale_two_slope,
                gate_two_slope[:, None],
            ],
            axis=1,
        )
        .reshape(slot_count, 6 * model_width)
        .astype(jnp.bfloat16)
    )
    mod_slope_all = lax.all_gather(modulation_slope, everyone, axis=0, tiled=True)
    slope_mod_weight = inner_rows(
        act_rows.reshape(dp * rep * slot_count, shard), mod_slope_all
    )
    mod_bias_size = modulation_bias.shape[0]
    slope_mod_bias = jnp.sum(
        lax.dynamic_slice_in_dim(mod_slope_all, here * mod_bias_size, mod_bias_size, 1),
        0,
        dtype=jnp.float32,
    )
    mod_slope_copy = lax.dynamic_index_in_dim(
        mod_slope_all.reshape(dp, rep, slot_count, -1), copy, 1, keepdims=False
    ).reshape(dp * slot_count, -1)
    cond_columns = times_transposed(mod_slope_copy, modulation_weight)
    cond_slope_all = lax.all_gather(cond_columns[None], "dp", axis=0, tiled=True)
    cond_slope = (
        lax.dynamic_slice_in_dim(cond_slope_all, here * slot_count, slot_count, 1)
        .transpose(1, 0, 2)
        .reshape(slot_count, model_width)
    )
    gradient_condition = silu_back(cond_slope)[0]

    sums = lax.psum(
        jnp.concatenate(
            [
                jnp.sum(query_low_slope, 0, dtype=jnp.float32),
                jnp.sum(value_low_slope, 0, dtype=jnp.float32),
                jnp.sum(branch_low, 0, dtype=jnp.float32),
                jnp.sum(shrink_slope, 0, dtype=jnp.float32),
                in_order(links, [part[None] for part in inner_sums])
                .reshape(4, dp, shard)
                .transpose(1, 0, 2)
                .reshape(-1),
            ]
        ),
        everyone,
    )
    rows = lax.dynamic_index_in_dim(
        sums[: 4 * model_width].reshape(4, dp, shard), here, 1, keepdims=False
    )
    slope_att_bias = rows[0:2]
    slope_out_bias = rows[2]
    slope_shr_bias = rows[3]
    slope_exp_bias = lax.dynamic_slice_in_dim(
        sums[4 * model_width :], here * expand_bias.shape[0], expand_bias.shape[0], 0
    )

    attend_all = in_order(links, attend_sums).astype(jnp.float32)
    slope_att_weight = attend_all[:3].transpose(1, 0, 2).reshape(shard, 3 * model_width)
    slope_out_weight = attend_all[3]
    slope_exp_weight = (
        in_order(links, expand_sums)
        .reshape(4, shard, dp, shard)
        .transpose(1, 2, 0, 3)
        .reshape(shard, inner_width)
        .astype(jnp.float32)
    )
    slope_shr_weight = (
        in_order(links, shrink_sums).reshape(4 * shard, model_width).astype(jnp.float32)
    )
    return (
        layer_out,
        gradient_hidden,
        gradient_condition,
        slope_mod_weight,
        slope_mod_bias,
        slope_att_weight,
        slope_att_bias,
        slope_out_weight,
        slope_out_bias,
        slope_exp_weight,
        slope_exp_bias,
        slope_shr_weight,
        slope_shr_bias,
    )


def solution(mesh):
    return jax.shard_map(
        partial(per_device, (mesh.shape["dp"], mesh.shape["rep"])),
        mesh=mesh,
        in_specs=(
            P(("dp", "rep"), None, None),
            P(("dp", "rep"), None),
            P(("dp", "rep"), None),
            P(("dp", "rep")),
            P("dp", None),
            P("dp"),
            P("dp", None),
            P(None, "dp"),
            P("dp", None),
            P("dp"),
            P("dp", None),
            P("dp"),
            P("dp", None),
            P("dp"),
            P(("dp", "rep"), None, None),
        ),
        out_specs=(
            P(("dp", "rep"), None, None),
            P(("dp", "rep"), None, None),
            P(("dp", "rep"), None),
            P("dp", None),
            P("dp"),
            P("dp", None),
            P(None, "dp"),
            P("dp", None),
            P("dp"),
            P("dp", None),
            P("dp"),
            P("dp", None),
            P("dp"),
        ),
        check_vma=False,
    )
```

time: 2630 us -> 1030 us (0.39)
  waiting for transfers between devices: 2180 us -> 385 us
  local copies, waits for them, and re-layouts: 101 us -> 216 us
  starting transfers between devices: 0.98 us -> 58.7 us
    reduce_scatter x5 -> x0, waiting for transfers between devices: 1440 us -> none  [the longest x1 511 us: per_device(): lax.psum_scatter(inner_rows(cond_low, modulation_slope), 'dp', scatter_di...]
    all_gather x8 -> x0, waiting for transfers between devices: 591 us -> none  [the longest x1 157 us: per_device(): lax.all_gather(modulation_weight, 'dp', axis=0, tiled=True)]
    ppermute x0 -> x70, waiting for transfers between devices: none -> 238 us  [the longest x24 96.5 us: up(): lax.ppermute(value, 'dp', [(i, (i + 2) % self.dp) for i in range(self.dp)])]
    unnamed x3 -> x0, blocking collectives: 82.6 us -> none
    ppermute x0 -> x70, starting transfers between devices: none -> 58.7 us  [the longest x20 24.5 us: swap_x(): return lax.ppermute(value, 'dp', [(i, i ^ 1) for i in range(self.dp)])]
    reshape x3 -> x27, local copies, waits for them, and re-layouts: 21.6 us -> 67 us  [the longest x8 39.8 us: heads_of(): flat.astype(jnp.bfloat16)]
    dynamic_update_slice x0 -> x44, local copies, waits for them, and re-layouts: none -> 42.5 us  [the longest x16 17.9 us: collect(): lax.dynamic_update_slice(whole, self.swap_x(block)[None], (place + 1 - se...]
    psum x0 -> x1, blocking collectives: none -> 37.2 us  [per_device(): lax.psum(jnp.concatenate([jnp.sum(query_low_slope, 0, dtype=jnp.float32),...]
  transfers between devices with their start and end apart: 19 -> 72, of which waited for: 18 -> 28; matrix products, arithmetic and copies ran while one was open for 10% -> 41% of each run, Pallas kernels for 0% -> 0%
where the time goes in v1:
time: 1030 us; the launch traced here: 1020 us
  waiting for transfers between devices  385 us (37%)
  local copies, waits for them, and re-layouts  216 us (21%)
  matrix products  179 us (17%)
  blocking collectives  112 us (11%)
  starting transfers between devices  58.7 us (6%)
  other arithmetic  53.6 us (5%)
  between operations  17.5 us (2%)
    unnamed x4, waiting for transfers between devices  147 us
    ppermute x24, waiting for transfers between devices, up(): lax.ppermute(value, 'dp', [(i, (i + 2) % self.dp) for i in range(self.dp)])  96.5 us
    ppermute x8, waiting for transfers between devices, swap_y(): return lax.ppermute(value, 'rep', [(i, i ^ 2) for i in range(4)])  80.6 us
    ppermute x20, waiting for transfers between devices, swap_x(): return lax.ppermute(value, 'dp', [(i, i ^ 1) for i in range(self.dp)])  60.1 us
    dot_general x13, matrix products, times_transposed(): lax.dot_general(left_side, right_side, (((1,), (1,)), ((), ())), preferre...  58.6 us
    dot_general x13, matrix products, times(): return jnp.dot(left_side, right_side, preferred_element_type=jnp.float32)  51.4 us
    dot_general x13, matrix products, inner_rows(): lax.dot_general(left_side, right_side, (((0,), (0,)), ((), ())), preferre...  48.6 us
    all_gather x1, blocking collectives, per_device(): lax.all_gather(modulation_slope, everyone, axis=0, tiled=True)  44.4 us
  transfers between devices with their start and end apart: 72, of which 28 were waited for; matrix products, arithmetic and copies ran while one was open for 41% of the time, Pallas kernels for 0%

profile of v1, /device:TPU:0, one launch (start us, length us, event | category | flops | bytes accessed | tf_op | source)
XLA Modules:
  0.0 1022.5 jit_solution(6015490541986724332)
XLA Ops:
  11.9 6.8 fusion.92
  32.0 5.9 reshape.360
  59.5 98.2 %all-reduce.5.cloned.1.call-done = bf16[138240]{0:T(1024)(128)(2,1)} async-done(((bf16[138240]{0:T(1024)(128)(2,1)}), bf16[138240]{0:T(1024)(128)(2,1)}) %all-reduce.5.cloned.1.call-update) | async-done | bytes 276496
  204.4 48.5 %all-reduce.7.cloned.1.call-done = f32[16,6912]{1,0:T(8,128)} async-done(((f32[16,6912]{1,0:T(8,128)}), f32[16,6912]{1,0:T(8,128)}) %all-reduce.7.cloned.1.call-update) | async-done | bytes 442384
  311.6 12.7 %collective-permute-done.22 = bf16[144,1152]{1,0:T(8,128)(2,1)S(1)} collective-permute-done((bf16[144,1152]{1,0:T(8,128)(2,1)S(1)}, bf16[144,1152]{1,0:T(8,128)(2,1)S(1)}, u32[]{:S(2)}, u32[]{:S(2)}) %collective-permute-start.22) | collective-permute-done | bytes 331808 | tf_op jit(solution)/shard_map/ppermute | solution.py:56
  348.1 5.8 reshape.423
  363.0 5.7 reshape.424
  372.8 5.7 reshape.425
  434.0 6.3 fusion.132
  450.6 5.8 fusion.131
  465.7 5.6 fusion.17
  506.1 6.1 reshape.426
  516.3 7.5 multiply_reduce_fusion
  578.9 44.4 %all-gather.2 = bf16[32,2,6912]{2,1,0:T(2,128)(2,1)} all-gather(bf16[1,2,6912]{2,1,0:T(2,128)(2,1)S(1)} %bitcast.484), channel_id=1, replica_groups=mesh['dp'=8,'rep'=4] {'dp','rep'}, dimensions={0}, use_global_device_ids=true | all-gather | bytes 912384 | tf_op jit(solution)/shard_map/all_gather | solution.py:359
  629.9 30.6 %all-gather.1 = f32[128,144]{1,0:T(8,128)S(1)} all-gather(f32[16,144]{1,0:T(8,128)S(1)} %fusion.147), channel_id=3, replica_groups=mesh['dp'=8,'rep'=4] {'dp'}, dimensions={0}, use_global_device_ids=true | all-gather | bytes 82944 | tf_op jit(solution)/shard_map/all_gather | solution.py:373
  680.8 37.2 %psum.7 = f32[9216]{0:T(1024)S(1)} all-reduce(f32[9216]{0:T(1024)S(1)} %constant_dynamic-update-slice_fusion.7), channel_id=1, replica_groups=mesh['dp'=8,'rep'=4] {'dp','rep'}, use_global_device_ids=true, to_apply=%region_27.28 | all-reduce | flops 9216 | bytes 73728 | tf_op jit(solution)/shard_map/psum | solution.py:381
  739.5 14.9 %collective-permute-done.47 = bf16[4,144,1152]{2,1,0:T(8,128)(2,1)S(1)} collective-permute-done((bf16[4,144,1152]{2,1,0:T(8,128)(2,1)S(1)}, bf16[4,144,1152]{2,1,0:T(8,128)(2,1)S(1)}, u32[]{:S(2)}, u32[]{:S(2)}) %collective-permute-start.47) | collective-permute-done | bytes 1327136 | tf_op jit(solution)/shard_map/ppermute | solution.py:56
  754.8 25.9 %collective-permute-done.52 = bf16[4,144,1152]{2,1,0:T(8,128)(2,1)S(1)} collective-permute-done((bf16[4,144,1152]{2,1,0:T(8,128)(2,1)S(1)}, bf16[4,144,1152]{2,1,0:T(8,128)(2,1)S(1)}, u32[]{:S(2)}, u32[]{:S(2)}) %collective-permute-start.52) | collective-permute-done | bytes 1327136 | tf_op jit(solution)/shard_map/ppermute | solution.py:56
  788.9 8.4 collective-permute-done.53
  799.3 7.9 collective-permute-done.54
  807.5 9.9 collective-permute-done.49
  817.5 11.1 %collective-permute-done.55 = bf16[144,1152]{1,0:T(8,128)(2,1)S(1)} collective-permute-done((bf16[144,1152]{1,0:T(8,128)(2,1)S(1)}, bf16[144,1152]{1,0:T(8,128)(2,1)S(1)}, u32[]{:S(2)}, u32[]{:S(2)}) %collective-permute-start.55) | collective-permute-done | bytes 331808 | tf_op jit(solution)/shard_map/ppermute | solution.py:53
  838.4 26.5 %collective-permute-done.56 = bf16[144,1152]{1,0:T(8,128)(2,1)S(1)} collective-permute-done((bf16[144,1152]{1,0:T(8,128)(2,1)S(1)}, bf16[144,1152]{1,0:T(8,128)(2,1)S(1)}, u32[]{:S(2)}, u32[]{:S(2)}) %collective-permute-start.56) | collective-permute-done | bytes 331808 | tf_op jit(solution)/shard_map/ppermute | solution.py:59
  874.3 47.1 %collective-permute-done.62 = bf16[1152,1152]{1,0:T(8,128)(2,1)S(1)} collective-permute-done((bf16[1152,1152]{1,0:T(8,128)(2,1)}, bf16[1152,1152]{1,0:T(8,128)(2,1)S(1)}, u32[]{:S(2)}, u32[]{:S(2)}) %collective-permute-start.62) | collective-permute-done | bytes 2654240 | tf_op jit(solution)/shard_map/ppermute | solution.py:59
  937.0 7.6 copy.404
  944.6 7.2 reshape.405
  957.7 8.9 collective-permute-done.40
  966.7 7.0 collective-permute-done.64
  973.8 7.0 collective-permute-done.41
  980.9 7.0 collective-permute-done.65
  988.1 6.9 collective-permute-done.42
  1004.0 6.8 collective-permute-done.67
  (561 shorter events, 462.2 us)
Async XLA Ops:
  7.2 150.5 %all-reduce.5.cloned.1.call-start = ((), (), s32[]{:S(2)}) async-start(), calls=%async_computation | async-start | bytes 552960
  21.4 158.9 %collective-permute-start = (bf16[144,1152]{1,0:T(8,128)(2,1)}, bf16[144,1152]{1,0:T(8,128)(2,1)}, u32[]{:S(2)}, u32[]{:S(2)}) collective-permute-start(bf16[144,1152]{1,0:T(8,128)(2,1)} %get-tuple-element.61), channel_id=1, source_target_pairs={{0,4},{4,0},{8,12},{12,8},{16,20},{20,16},{24,28},{28,24},{1,5},{5... | collective-permute-start | bytes 995336 | tf_op jit(solution)/shard_map/ppermute | solution.py:56
  24.3 164.5 %collective-permute-start.1 = (bf16[144,1152]{1,0:T(8,128)(2,1)}, bf16[144,1152]{1,0:T(8,128)(2,1)}, u32[]{:S(2)}, u32[]{:S(2)}) collective-permute-start(bf16[144,1152]{1,0:T(8,128)(2,1)} %get-tuple-element.61), channel_id=1, source_target_pairs={{0,8},{4,12},{8,16},{12,20},{16,24},{20,28},{24,0},{28,4},{1,9},{5... | collective-permute-start | bytes 995336 | tf_op jit(solution)/shard_map/ppermute | solution.py:53
  28.5 157.1 %collective-permute-start.7 = (bf16[144,1152]{1,0:T(8,128)(2,1)}, bf16[144,1152]{1,0:T(8,128)(2,1)}, u32[]{:S(2)}, u32[]{:S(2)}) collective-permute-start(bf16[144,1152]{1,0:T(8,128)(2,1)} %get-tuple-element.59), channel_id=1, source_target_pairs={{0,4},{4,0},{8,12},{12,8},{16,20},{20,16},{24,28},{28,24},{1,5},{5... | collective-permute-start | bytes 995336 | tf_op jit(solution)/shard_map/ppermute | solution.py:56
  29.0 161.9 %collective-permute-start.8 = (bf16[144,1152]{1,0:T(8,128)(2,1)}, bf16[144,1152]{1,0:T(8,128)(2,1)}, u32[]{:S(2)}, u32[]{:S(2)}) collective-permute-start(bf16[144,1152]{1,0:T(8,128)(2,1)} %get-tuple-element.59), channel_id=1, source_target_pairs={{0,8},{4,12},{8,16},{12,20},{16,24},{20,28},{24,0},{28,4},{1,9},{5... | collective-permute-start | bytes 995336 | tf_op jit(solution)/shard_map/ppermute | solution.py:53
  32.0 220.9 %all-reduce.7.cloned.1.call-start = ((), (), s32[]{:S(2)}) async-start(), calls=%async_computation.1 | async-start | bytes 884736
  49.5 143.8 %collective-permute-start.16 = (bf16[144,1152]{1,0:T(8,128)(2,1)}, bf16[144,1152]{1,0:T(8,128)(2,1)}, u32[]{:S(2)}, u32[]{:S(2)}) collective-permute-start(bf16[144,1152]{1,0:T(8,128)(2,1)} %get-tuple-element.54), channel_id=1, source_target_pairs={{0,4},{4,0},{8,12},{12,8},{16,20},{20,16},{24,28},{28,24},{1,5},{5... | collective-permute-start | bytes 995336 | tf_op jit(solution)/shard_map/ppermute | solution.py:56
  191.0 71.0 %collective-permute-start.2 = (bf16[144,1152]{1,0:T(8,128)(2,1)}, bf16[144,1152]{1,0:T(8,128)(2,1)}, u32[]{:S(2)}, u32[]{:S(2)}) collective-permute-start(bf16[144,1152]{1,0:T(8,128)(2,1)} %collective-permute-done.1), channel_id=1, source_target_pairs={{0,4},{4,0},{8,12},{12,8},{16,20},{20,16},{24,28},{28,24},{1,5},{5... | collective-permute-start | bytes 995336 | tf_op jit(solution)/shard_map/ppermute | solution.py:56
  193.2 74.4 %collective-permute-start.3 = (bf16[144,1152]{1,0:T(8,128)(2,1)}, bf16[144,1152]{1,0:T(8,128)(2,1)}, u32[]{:S(2)}, u32[]{:S(2)}) collective-permute-start(bf16[144,1152]{1,0:T(8,128)(2,1)} %collective-permute-done.1), channel_id=1, source_target_pairs={{0,8},{4,12},{8,16},{12,20},{16,24},{20,28},{24,0},{28,4},{1,9},{5... | collective-permute-start | bytes 995336 | tf_op jit(solution)/shard_map/ppermute | solution.py:53
  196.6 67.9 %collective-permute-start.9 = (bf16[144,1152]{1,0:T(8,128)(2,1)}, bf16[144,1152]{1,0:T(8,128)(2,1)}, u32[]{:S(2)}, u32[]{:S(2)}) collective-permute-start(bf16[144,1152]{1,0:T(8,128)(2,1)} %collective-permute-done.8), channel_id=1, source_target_pairs={{0,4},{4,0},{8,12},{12,8},{16,20},{20,16},{24,28},{28,24},{1,5},{5... | collective-permute-start | bytes 995336 | tf_op jit(solution)/shard_map/ppermute | solution.py:56
  199.8 70.9 %collective-permute-start.10 = (bf16[144,1152]{1,0:T(8,128)(2,1)}, bf16[144,1152]{1,0:T(8,128)(2,1)}, u32[]{:S(2)}, u32[]{:S(2)}) collective-permute-start(bf16[144,1152]{1,0:T(8,128)(2,1)} %collective-permute-done.8), channel_id=1, source_target_pairs={{0,8},{4,12},{8,16},{12,20},{16,24},{20,28},{24,0},{28,4},{1,9},{5... | collective-permute-start | bytes 995336 | tf_op jit(solution)/shard_map/ppermute | solution.py:53
  202.5 70.3 %collective-permute-start.18 = (bf16[144,1152]{1,0:T(8,128)(2,1)}, bf16[144,1152]{1,0:T(8,128)(2,1)}, u32[]{:S(2)}, u32[]{:S(2)}) collective-permute-start(bf16[144,1152]{1,0:T(8,128)(2,1)} %collective-permute-done.17), channel_id=1, source_target_pairs={{0,4},{4,0},{8,12},{12,8},{16,20},{20,16},{24,28},{28,24},{1,5},{5... | collective-permute-start | bytes 995336 | tf_op jit(solution)/shard_map/ppermute | solution.py:56
  325.1 76.0 %collective-permute-start.32 = (bf16[1152,1152]{1,0:T(8,128)(2,1)}, bf16[1152,1152]{1,0:T(8,128)(2,1)}, u32[]{:S(2)}, u32[]{:S(2)}) collective-permute-start(bf16[1152,1152]{1,0:T(8,128)(2,1)} %bitcast.41), channel_id=1, source_target_pairs={{0,1},{1,0},{2,3},{3,2},{4,5},{5,4},{6,7},{7,6},{8,9},{9,8},{10,11... | collective-permute-start | bytes 7962632 | tf_op jit(solution)/shard_map/ppermute | solution.py:62
  325.1 97.2 %collective-permute-start.30 = (bf16[1152,1152]{1,0:T(8,128)(2,1)}, bf16[1152,1152]{1,0:T(8,128)(2,1)}, u32[]{:S(2)}, u32[]{:S(2)}) collective-permute-start(bf16[1152,1152]{1,0:T(8,128)(2,1)} %bitcast.41), channel_id=1, source_target_pairs={{0,2},{1,3},{2,0},{3,1},{4,6},{5,7},{6,4},{7,5},{8,10},{9,11},{10,... | collective-permute-start | bytes 7962632 | tf_op jit(solution)/shard_map/ppermute | solution.py:59
  329.7 75.4 %collective-permute-start.33 = (bf16[1152,1152]{1,0:T(8,128)(2,1)}, bf16[1152,1152]{1,0:T(8,128)(2,1)}, u32[]{:S(2)}, u32[]{:S(2)}) collective-permute-start(bf16[1152,1152]{1,0:T(8,128)(2,1)} %bitcast.52), channel_id=1, source_target_pairs={{0,1},{1,0},{2,3},{3,2},{4,5},{5,4},{6,7},{7,6},{8,9},{9,8},{10,11... | collective-permute-start | bytes 7962632 | tf_op jit(solution)/shard_map/ppermute | solution.py:62
  334.9 110.9 %collective-permute-start.31 = (bf16[1152,1152]{1,0:T(8,128)(2,1)}, bf16[1152,1152]{1,0:T(8,128)(2,1)}, u32[]{:S(2)}, u32[]{:S(2)}) collective-permute-start(bf16[1152,1152]{1,0:T(8,128)(2,1)} %bitcast.52), channel_id=1, source_target_pairs={{0,2},{1,3},{2,0},{3,1},{4,6},{5,7},{6,4},{7,5},{8,10},{9,11},{10,... | collective-permute-start | bytes 7962632 | tf_op jit(solution)/shard_map/ppermute | solution.py:59
  412.9 305.3 %collective-permute-start.46 = (bf16[1152,1152]{1,0:T(8,128)(2,1)}, bf16[1152,1152]{1,0:T(8,128)(2,1)}, u32[]{:S(2)}, u32[]{:S(2)}) collective-permute-start(bf16[1152,1152]{1,0:T(8,128)(2,1)} %convolution_convert_fusion.6), channel_id=1, source_target_pairs={{0,1},{1,0},{2,3},{3,2},{4,5},{5,4},{6,7},{7,6},{8,9},{9,8},{10,11... | collective-permute-start | bytes 7962632 | tf_op jit(solution)/shard_map/ppermute | solution.py:62
  416.5 457.8 %collective-permute-start.60 = (bf16[1152,1152]{1,0:T(8,128)(2,1)}, bf16[1152,1152]{1,0:T(8,128)(2,1)}, u32[]{:S(2)}, u32[]{:S(2)}) collective-permute-start(bf16[1152,1152]{1,0:T(8,128)(2,1)} %convolution_convert_fusion.2), channel_id=1, source_target_pairs={{0,1},{1,0},{2,3},{3,2},{4,5},{5,4},{6,7},{7,6},{8,9},{9,8},{10,11... | collective-permute-start | bytes 7962632 | tf_op jit(solution)/shard_map/ppermute | solution.py:62
  422.2 56.2 %collective-permute-start.34 = (bf16[1152,1152]{1,0:T(8,128)(2,1)}, bf16[1152,1152]{1,0:T(8,128)(2,1)}, u32[]{:S(2)}, u32[]{:S(2)}) collective-permute-start(bf16[1152,1152]{1,0:T(8,128)(2,1)} %collective-permute-done.30), channel_id=1, source_target_pairs={{0,1},{1,0},{2,3},{3,2},{4,5},{5,4},{6,7},{7,6},{8,9},{9,8},{10,11... | collective-permute-start | bytes 7962632 | tf_op jit(solution)/shard_map/ppermute | solution.py:62
  445.7 36.4 %collective-permute-start.35 = (bf16[1152,1152]{1,0:T(8,128)(2,1)}, bf16[1152,1152]{1,0:T(8,128)(2,1)}, u32[]{:S(2)}, u32[]{:S(2)}) collective-permute-start(bf16[1152,1152]{1,0:T(8,128)(2,1)} %collective-permute-done.31), channel_id=1, source_target_pairs={{0,1},{1,0},{2,3},{3,2},{4,5},{5,4},{6,7},{7,6},{8,9},{9,8},{10,11... | collective-permute-start | bytes 7962632 | tf_op jit(solution)/shard_map/ppermute | solution.py:62
  670.6 113.4 %collective-permute-start.37 = (bf16[1152,1152]{1,0:T(8,128)(2,1)}, bf16[1152,1152]{1,0:T(8,128)(2,1)}, u32[]{:S(2)}, u32[]{:S(2)}) collective-permute-start(bf16[1152,1152]{1,0:T(8,128)(2,1)} %convolution_convert_fusion.8), channel_id=1, source_target_pairs={{0,1},{1,0},{2,3},{3,2},{4,5},{5,4},{6,7},{7,6},{8,9},{9,8},{10,11... | collective-permute-start | bytes 7962632 | tf_op jit(solution)/shard_map/ppermute | solution.py:62
  675.2 192.4 %collective-permute-start.36 = (bf16[1152,1152]{1,0:T(8,128)(2,1)}, bf16[1152,1152]{1,0:T(8,128)(2,1)}, u32[]{:S(2)}, u32[]{:S(2)}) collective-permute-start(bf16[1152,1152]{1,0:T(8,128)(2,1)} %convolution_convert_fusion.10), channel_id=1, source_target_pairs={{0,1},{1,0},{2,3},{3,2},{4,5},{5,4},{6,7},{7,6},{8,9},{9,8},{10,11... | collective-permute-start | bytes 7962632 | tf_op jit(solution)/shard_map/ppermute | solution.py:62
  680.2 50.9 %collective-permute-start.51 = (bf16[1152,1152]{1,0:T(8,128)(2,1)}, bf16[1152,1152]{1,0:T(8,128)(2,1)}, u32[]{:S(2)}, u32[]{:S(2)}) collective-permute-start(bf16[1152,1152]{1,0:T(8,128)(2,1)} %convolution_convert_fusion.4), channel_id=1, source_target_pairs={{0,1},{1,0},{2,3},{3,2},{4,5},{5,4},{6,7},{7,6},{8,9},{9,8},{10,11... | collective-permute-start | bytes 7962632 | tf_op jit(solution)/shard_map/ppermute | solution.py:62
  722.1 32.3 %collective-permute-start.47 = (bf16[4,144,1152]{2,1,0:T(8,128)(2,1)S(1)}, bf16[4,144,1152]{2,1,0:T(8,128)(2,1)S(1)}, u32[]{:S(2)}, u32[]{:S(2)}) collective-permute-start(bf16[4,144,1152]{2,1,0:T(8,128)(2,1)S(1)} %dynamic-slice_bitcast_fusion.2), channel_id=1, source_target_pairs={{0,4},{4,0},{8,12},{12,8},{16,20},{20,16},{24,28},{28,24},{1,5},{5... | collective-permute-start | bytes 3981320 | tf_op jit(solution)/shard_map/ppermute | solution.py:56
  735.0 45.7 %collective-permute-start.52 = (bf16[4,144,1152]{2,1,0:T(8,128)(2,1)S(1)}, bf16[4,144,1152]{2,1,0:T(8,128)(2,1)S(1)}, u32[]{:S(2)}, u32[]{:S(2)}) collective-permute-start(bf16[4,144,1152]{2,1,0:T(8,128)(2,1)S(1)} %dynamic-slice_bitcast_fusion.1), channel_id=1, source_target_pairs={{0,4},{4,0},{8,12},{12,8},{16,20},{20,16},{24,28},{28,24},{1,5},{5... | collective-permute-start | bytes 3981320 | tf_op jit(solution)/shard_map/ppermute | solution.py:56
  754.4 74.4 %collective-permute-start.61 = (bf16[1152,1152]{1,0:T(8,128)(2,1)S(1)}, bf16[1152,1152]{1,0:T(8,128)(2,1)S(1)}, u32[]{:S(2)}, u32[]{:S(2)}) collective-permute-start(bf16[1152,1152]{1,0:T(8,128)(2,1)S(1)} %convolution_convert_fusion), channel_id=1, source_target_pairs={{0,1},{1,0},{2,3},{3,2},{4,5},{5,4},{6,7},{7,6},{8,9},{9,8},{10,11... | collective-permute-start | bytes 7962632 | tf_op jit(solution)/shard_map/ppermute | solution.py:62
  797.3 70.3 %collective-permute-start.38 = (bf16[1152,1152]{1,0:T(8,128)(2,1)S(1)}, bf16[1152,1152]{1,0:T(8,128)(2,1)S(1)}, u32[]{:S(2)}, u32[]{:S(2)}) collective-permute-start(bf16[1152,1152]{1,0:T(8,128)(2,1)S(1)} %add_convert_fusion.6), channel_id=1, source_target_pairs={{0,2},{1,3},{2,0},{3,1},{4,6},{5,7},{6,4},{7,5},{8,10},{9,11},{10,... | collective-permute-start | bytes 7962632 | tf_op jit(solution)/shard_map/ppermute | solution.py:59
  828.9 36.0 %collective-permute-start.56 = (bf16[144,1152]{1,0:T(8,128)(2,1)S(1)}, bf16[144,1152]{1,0:T(8,128)(2,1)S(1)}, u32[]{:S(2)}, u32[]{:S(2)}) collective-permute-start(bf16[144,1152]{1,0:T(8,128)(2,1)S(1)} %fusion.97), channel_id=1, source_target_pairs={{0,2},{1,3},{2,0},{3,1},{4,6},{5,7},{6,4},{7,5},{8,10},{9,11},{10,... | collective-permute-start | bytes 995336 | tf_op jit(solution)/shard_map/ppermute | solution.py:59
  837.7 83.7 %collective-permute-start.62 = (bf16[1152,1152]{1,0:T(8,128)(2,1)}, bf16[1152,1152]{1,0:T(8,128)(2,1)S(1)}, u32[]{:S(2)}, u32[]{:S(2)}) collective-permute-start(bf16[1152,1152]{1,0:T(8,128)(2,1)} %add_convert_fusion.1), channel_id=1, source_target_pairs={{0,2},{1,3},{2,0},{3,1},{4,6},{5,7},{6,4},{7,5},{8,10},{9,11},{10,... | collective-permute-start | bytes 7962632 | tf_op jit(solution)/shard_map/ppermute | solution.py:59
  867.0 61.3 %collective-permute-start.57 = (bf16[144,1152]{1,0:T(8,128)(2,1)S(1)}, bf16[144,1152]{1,0:T(8,128)(2,1)S(1)}, u32[]{:S(2)}, u32[]{:S(2)}) collective-permute-start(bf16[144,1152]{1,0:T(8,128)(2,1)S(1)} %get-tuple-element.31), channel_id=1, source_target_pairs={{0,2},{1,3},{2,0},{3,1},{4,6},{5,7},{6,4},{7,5},{8,10},{9,11},{10,... | collective-permute-start | bytes 995336 | tf_op jit(solution)/shard_map/ppermute | solution.py:59
  867.6 61.6 %collective-permute-start.58 = (bf16[144,1152]{1,0:T(8,128)(2,1)S(1)}, bf16[144,1152]{1,0:T(8,128)(2,1)S(1)}, u32[]{:S(2)}, u32[]{:S(2)}) collective-permute-start(bf16[144,1152]{1,0:T(8,128)(2,1)S(1)} %get-tuple-element.30), channel_id=1, source_target_pairs={{0,1},{1,0},{2,3},{3,2},{4,5},{5,4},{6,7},{7,6},{8,9},{9,8},{10,11... | collective-permute-start | bytes 995336 | tf_op jit(solution)/shard_map/ppermute | solution.py:62
  871.8 80.1 %collective-permute-start.39 = (bf16[4,144,1152]{2,1,0:T(8,128)(2,1)}, bf16[4,144,1152]{2,1,0:T(8,128)(2,1)}, u32[]{:S(2)}, u32[]{:S(2)}) collective-permute-start(bf16[4,144,1152]{2,1,0:T(8,128)(2,1)} %dynamic-slice_bitcast_fusion.3), channel_id=1, source_target_pairs={{0,4},{4,0},{8,12},{12,8},{16,20},{20,16},{24,28},{28,24},{1,5},{5... | collective-permute-start | bytes 3981320 | tf_op jit(solution)/shard_map/ppermute | solution.py:56
  (127 other events, 1715.6 us)
Sparse Core Ops, SparseCore 0:
  32.1 125.5 all-reduce.4
  165.6 87.1 all-reduce.6

commit v2 on v0

v2 whole, which is shorter than its diff:
```python
import math
from functools import partial

import jax
import jax.numpy as jnp
from jax import lax
from jax.experimental import pallas as pl
from jax.experimental.pallas import tpu as pltpu
from jax.sharding import PartitionSpec as P

HEADS = 16


epsilon = 1e-06
masked_score = -1e30


def layer_norm(values):
    centered = values - jnp.mean(values, -1, keepdims=True)
    variance = jnp.mean(centered * centered, -1, keepdims=True)
    return centered * lax.rsqrt(variance + epsilon)


def modulate(values, shift_part, scale_part):
    return layer_norm(values) * (1.0 + scale_part) + shift_part


def gelu(values):
    return jax.nn.gelu(values, approximate=True)


def low(values):
    return values.astype(jnp.bfloat16)


def inner_rows(left_side, right_side):
    return lax.dot_general(
        left_side, right_side, (((0,), (0,)), ((), ())), preferred_element_type=jnp.float32
    )


def times(left_side, right_side):
    return jnp.dot(left_side, right_side, preferred_element_type=jnp.float32)


def times_transposed(left_side, right_side):
    return lax.dot_general(
        left_side, right_side, (((1,), (1,)), ((), ())), preferred_element_type=jnp.float32
    )


def column_sums(values):
    return jnp.sum(values, 0, dtype=jnp.float32)


def head_window(head, head_dim, model_width):
    first = head * head_dim
    last = first + head_dim
    start = first // 128 * 128
    stop = min(-(-last // 128) * 128, model_width)
    lane = lax.broadcasted_iota(jnp.int32, (1, stop - start), 1) + start
    return slice(start, stop), (lane >= first) & (lane < last)


def only(inside, values):
    return jnp.where(inside, values, jnp.zeros_like(values))


def head_order(heads):
    half = heads // 2
    return [head + shift for head in range(half) for shift in (0, half)]


def head_scores(query, key_window, valid, score_scale):
    scores = times_transposed(query, key_window) * score_scale
    return jnp.where(valid, scores, masked_score)


def attend_kernel(heads, query_ref, key_ref, value_ref, mask_ref, out_ref, log_ref, total_ref):
    patch_count, model_width = query_ref.shape
    head_dim = model_width // heads
    valid = mask_ref[0] > 0
    total_ref[...] = jnp.zeros_like(total_ref)
    for head in head_order(heads):
        cut, inside = head_window(head, head_dim, model_width)
        query = only(inside, query_ref[:, cut])
        scores = head_scores(query, key_ref[:, cut], valid, head_dim ** (-0.5))
        peak = jnp.max(scores, -1, keepdims=True)
        exponent = jnp.exp(scores - peak)
        row_total = jnp.sum(exponent, -1, keepdims=True)
        log_ref[:, head : head + 1] = peak + jnp.log(row_total)
        probs = low(exponent * (1.0 / row_total))
        total_ref[:, cut] += times(probs, only(inside, value_ref[:, cut]))
    out_ref[...] = low(total_ref[...])


def attend(queries, keys_all, values_all, patch_mask):
    slot_count, patch_count = patch_mask.shape
    model_width = queries.shape[1]
    block = pl.BlockSpec((patch_count, model_width), lambda slot: (slot, 0))
    return pl.pallas_call(
        partial(attend_kernel, HEADS),
        grid=(slot_count,),
        out_shape=[
            jax.ShapeDtypeStruct(queries.shape, jnp.bfloat16),
            jax.ShapeDtypeStruct((queries.shape[0], HEADS), jnp.float32),
        ],
        in_specs=[block] * 3 + [pl.BlockSpec((1, 1, patch_count), lambda slot: (slot, 0, 0))],
        out_specs=[block, pl.BlockSpec((patch_count, HEADS), lambda slot: (slot, 0))],
        scratch_shapes=[pltpu.VMEM((patch_count, model_width), jnp.float32)],
        compiler_params=pltpu.CompilerParams(vmem_limit_bytes=32 << 20),
    )(queries, keys_all, values_all, patch_mask[:, None, :])


def attend_back_kernel(
    heads,
    query_ref,
    key_ref,
    value_ref,
    slope_ref,
    mask_ref,
    log_ref,
    query_out,
    key_out,
    value_out,
    query_total,
    key_total,
    value_total,
):
    patch_count, model_width = query_ref.shape
    head_dim = model_width // heads
    score_scale = head_dim ** (-0.5)
    valid = mask_ref[0] > 0
    for total in (query_total, key_total, value_total):
        total[...] = jnp.zeros_like(total)
    for head in head_order(heads):
        cut, inside = head_window(head, head_dim, model_width)
        query = only(inside, query_ref[:, cut])
        key = only(inside, key_ref[:, cut])
        slope = only(inside, slope_ref[:, cut])
        probs = jnp.exp(head_scores(query, key, valid, score_scale) - log_ref[:, head : head + 1])
        prob_slope = times_transposed(slope, value_ref[:, cut])
        row = jnp.sum(probs * prob_slope, -1, keepdims=True)
        score_slope = low(probs * (prob_slope - row))
        query_total[:, cut] += times(score_slope, key)
        key_total[:, cut] += inner_rows(score_slope, query)
        value_total[:, cut] += inner_rows(low(probs), slope)
    query_out[...] = low(query_total[...] * score_scale)
    key_out[...] = low(key_total[...] * score_scale)
    value_out[...] = low(value_total[...])


def attend_back(queries, keys_all, values_all, slopes, patch_mask, logs):
    slot_count, patch_count = patch_mask.shape
    model_width = queries.shape[1]
    block = pl.BlockSpec((patch_count, model_width), lambda slot: (slot, 0))
    return pl.pallas_call(
        partial(attend_back_kernel, HEADS),
        grid=(slot_count,),
        out_shape=[jax.ShapeDtypeStruct(queries.shape, jnp.bfloat16)] * 3,
        in_specs=[block] * 4
        + [
            pl.BlockSpec((1, 1, patch_count), lambda slot: (slot, 0, 0)),
            pl.BlockSpec((patch_count, HEADS), lambda slot: (slot, 0)),
        ],
        out_specs=[block] * 3,
        scratch_shapes=[pltpu.VMEM((patch_count, model_width), jnp.float32)] * 3,
        compiler_params=pltpu.CompilerParams(vmem_limit_bytes=32 << 20),
    )(queries, keys_all, values_all, slopes, patch_mask[:, None, :], logs)


def norm_parts(values):
    centered = values - jnp.mean(values, -1, keepdims=True)
    inverse = lax.rsqrt(jnp.mean(centered * centered, -1, keepdims=True) + epsilon)
    return centered * inverse, inverse


def norm_back(normed, inverse, slope):
    mean = jnp.mean(slope, -1, keepdims=True)
    return (slope - mean - normed * jnp.mean(slope * normed, -1, keepdims=True)) * inverse


def patch_sums(values):
    return jnp.sum(values, 0, keepdims=True)


def middle_kernel(attended_ref, weight_ref, bias_ref, hidden_ref, mod_ref, branch_ref, middle_ref, normed_ref):
    gate_one, shift_two, scale_two = [mod_ref[0, i : i + 1] for i in (2, 3, 4)]
    branch = times(attended_ref[...], weight_ref[0]) + bias_ref[...]
    branch_ref[...] = branch
    middle = hidden_ref[...].astype(jnp.float32) + gate_one * branch
    middle_ref[...] = middle
    normed_ref[...] = low(norm_parts(middle)[0] * (1.0 + scale_two) + shift_two)


def finish_kernel(
    live_ref,
    middle_ref,
    branch_ref,
    out_ref,
    back_ref,
    cotangent_ref,
    bias_ref,
    mod_ref,
    layer_ref,
    middle_slope_ref,
    branch_low_ref,
    slopes_ref,
):
    gate_one, shift_two, scale_two, gate_two = [mod_ref[0, i : i + 1] for i in (2, 3, 4, 5)]
    live = live_ref[pl.program_id(0)]
    middle = middle_ref[...]
    mlp_out = out_ref[...] + bias_ref[...]
    layer_ref[...] = low(live * (middle + gate_two * mlp_out))
    slope = cotangent_ref[...].astype(jnp.float32) * live
    slopes_ref[0, 3:4] = patch_sums(slope * mlp_out)
    normed, inverse = norm_parts(middle)
    back = back_ref[...]
    slopes_ref[0, 1:2] = patch_sums(back)
    slopes_ref[0, 2:3] = patch_sums(back * normed)
    middle_slope = slope + norm_back(normed, inverse, back * (1.0 + scale_two))
    middle_slope_ref[...] = middle_slope
    slopes_ref[0, 0:1] = patch_sums(middle_slope * branch_ref[...])
    branch_low_ref[...] = low(middle_slope * gate_one)


def start_back_kernel(
    query_ref, key_ref, value_ref, weight_ref, middle_slope_ref, hidden_ref, mod_ref, out_ref, slopes_ref
):
    scale_one = mod_ref[0, 1:2]
    back = times_transposed(query_ref[...], weight_ref[0])
    back += times_transposed(key_ref[...], weight_ref[1])
    back += times_transposed(value_ref[...], weight_ref[2])
    normed, inverse = norm_parts(hidden_ref[...].astype(jnp.float32))
    slopes_ref[0, 0:1] = patch_sums(back)
    slopes_ref[0, 1:2] = patch_sums(back * normed)
    out_ref[...] = middle_slope_ref[...] + norm_back(normed, inverse, back * (1.0 + scale_one))


def assemble_kernel(place_ref, *refs):
    blocks, whole_ref = refs[:-1], refs[-1]
    for index, block in enumerate(blocks):
        whole_ref[place_ref[index]] = block[0]


def assemble(blocks, places, count):
    shape = (count,) + blocks[0][0].shape[1:]

    def row_spec(row):
        return pl.BlockSpec((1,) + shape[1:], lambda step: (row, 0, 0))

    return pl.pallas_call(
        assemble_kernel,
        grid=(1,),
        in_specs=[pl.BlockSpec(memory_space=pltpu.SMEM)] + [row_spec(row) for _, row in blocks],
        out_specs=pl.BlockSpec(shape, lambda step: (0, 0, 0)),
        out_shape=jax.ShapeDtypeStruct(shape, blocks[0][0].dtype),
        compiler_params=pltpu.CompilerParams(vmem_limit_bytes=32 << 20),
        cost_estimate=pl.CostEstimate(
            flops=0, bytes_accessed=4 * count * shape[1] * shape[2], transcendentals=0
        ),
    )(jnp.stack(places).astype(jnp.int32), *[array for array, _ in blocks])


def rows_of(parts):
    if len(parts) == 1:
        return parts[0]
    row = lax.broadcasted_iota(jnp.int32, (2, 1, 1), 0)
    return jnp.where(row == 0, parts[0], parts[1])


def take(places, wholes, parts=()):
    count = len(places)
    total = 0.0
    for whole in wholes:
        cut = [lax.dynamic_slice_in_dim(whole, place, 1, 0) for place in places]
        total = total + rows_of(cut).astype(jnp.float32)
    for part, row in parts:
        total = total + part[row : row + count].astype(jnp.float32)
    return low(total)


def pair_rows(one, one_row, two, two_row):
    return rows_of([one[one_row : one_row + 1], two[two_row : two_row + 1]])


def reorder_kernel(place_ref, *refs):
    units, whole_ref = refs[:-1], refs[-1]
    for index, unit in enumerate(units):
        whole_ref[place_ref[index]] = unit[...]


def reorder(units, order, parts):
    rows, width = units[0].shape
    block = rows // parts
    return pl.pallas_call(
        reorder_kernel,
        grid=(parts,),
        in_specs=[pl.BlockSpec(memory_space=pltpu.SMEM)]
        + [pl.BlockSpec((block, width), lambda step: (step, 0))] * 4,
        out_specs=pl.BlockSpec((4, block, width), lambda step: (0, step, 0)),
        out_shape=jax.ShapeDtypeStruct((4, rows, width), units[0].dtype),
        compiler_params=pltpu.CompilerParams(vmem_limit_bytes=32 << 20),
        cost_estimate=pl.CostEstimate(
            flops=0, bytes_accessed=16 * rows * width, transcendentals=0
        ),
    )(jnp.stack(order).astype(jnp.int32), *units)


def regroup_kernel(parts, in_ref, out_ref):
    width = in_ref.shape[1] // (4 * parts)
    for unit in range(4):
        out_ref[unit] = jnp.concatenate(
            [
                in_ref[:, (4 * part + unit) * width : (4 * part + unit + 1) * width]
                for part in range(parts)
            ],
            axis=1,
        )


def regroup(columns, parts):
    rows, width = columns.shape
    return pl.pallas_call(
        partial(regroup_kernel, parts),
        out_shape=jax.ShapeDtypeStruct((4, rows, width // 4), columns.dtype),
        compiler_params=pltpu.CompilerParams(vmem_limit_bytes=32 << 20),
    )(columns)


def spread_kernel(parts, order_ref, *refs):
    units, out_ref, held = refs[:4], refs[4], refs[5]
    for index in range(4):
        held[order_ref[index]] = units[index][...]
    width = units[0].shape[1] // parts
    out_ref[...] = jnp.concatenate(
        [
            held[unit, :, part * width : (part + 1) * width].astype(jnp.float32)
            for part in range(parts)
            for unit in range(4)
        ],
        axis=1,
    )


def spread(units, order, parts):
    rows, width = units[0].shape
    vmem = pl.BlockSpec(memory_space=pltpu.VMEM)
    return pl.pallas_call(
        partial(spread_kernel, parts),
        in_specs=[pl.BlockSpec(memory_space=pltpu.SMEM)] + [vmem] * 4,
        out_specs=vmem,
        out_shape=jax.ShapeDtypeStruct((rows, 4 * width), jnp.float32),
        scratch_shapes=[pltpu.VMEM((4, rows, width), units[0].dtype)],
        compiler_params=pltpu.CompilerParams(vmem_limit_bytes=32 << 20),
    )(jnp.stack(order).astype(jnp.int32), *units)


class Layer:
    def __init__(self, hidden_in, condition, patch_mask, image_counts, cotangent):
        self.slots, self.patches, self.width = hidden_in.shape
        self.rows = self.slots * self.patches
        self.patch_mask = patch_mask
        self.condition = condition
        self.live = (jnp.arange(self.slots) < image_counts[0]).astype(jnp.float32)
        self.hidden_in = hidden_in
        self.hidden = hidden_in.reshape(self.rows, self.width)
        self.cotangent = cotangent
        self.whole = (self.rows, self.width)

    def flat(self, values):
        return values.reshape(self.rows, self.width)

    def pieces(self, modulation):
        cut = modulation.reshape(self.slots, 6, 1, self.width)
        return [cut[:, i] for i in range(6)]

    def start(self, modulation):
        shift_one, scale_one = self.pieces(modulation)[:2]
        normed = modulate(self.hidden_in.astype(jnp.float32), shift_one, scale_one)
        return self.flat(low(normed))

    def shrink_slope(self, modulation):
        slope = self.cotangent.astype(jnp.float32) * self.live[:, None, None]
        return self.flat(low(slope * self.pieces(modulation)[5]))

    def attention(self, normed_one, weights, attend_bias):
        queries = low(times(normed_one, weights[0]) + attend_bias[0])
        keys_all = low(times(normed_one, weights[1]))
        values_all = low(times(normed_one, weights[2]) + attend_bias[1])
        attended, logs = attend(queries, keys_all, values_all, self.patch_mask)
        return queries, keys_all, values_all, attended, logs

    def per_image(self, kernel, outs, ins):
        rows = pl.BlockSpec((self.patches, self.width), lambda slot: (slot, 0))

        def spec(kind, shape):
            if kind == "rows":
                return rows
            if kind == "scalar":
                return pl.BlockSpec(memory_space=pltpu.SMEM)
            if kind == "all":
                return pl.BlockSpec(shape, lambda slot: (0,) * len(shape))
            if isinstance(kind, tuple):
                return pl.BlockSpec((kind[0],) + shape[1:], lambda slot: (kind[1], 0, 0))
            return pl.BlockSpec((1,) + shape[1:], lambda slot: (slot, 0, 0))

        shapes = [
            self.whole if kind == "rows" else (self.slots, kind, self.width) for kind, _ in outs
        ]
        return pl.pallas_call(
            kernel,
            grid=(self.slots,),
            in_specs=[spec(kind, array.shape) for kind, array in ins],
            out_specs=[spec(kind, shape) for (kind, _), shape in zip(outs, shapes)],
            out_shape=[jax.ShapeDtypeStruct(shape, kind[1]) for kind, shape in zip(outs, shapes)],
            compiler_params=pltpu.CompilerParams(vmem_limit_bytes=56 << 20),
        )(*[array for _, array in ins])

    def six(self, modulation):
        return "mod", modulation.reshape(self.slots, 6, self.width)

    def middle(self, attended, weights, output_bias, modulation):
        return self.per_image(
            middle_kernel,
            [("rows", jnp.float32), ("rows", jnp.float32), ("rows", jnp.bfloat16)],
            [
                ("rows", attended),
                ((1, 3), weights),
                ("all", output_bias),
                ("rows", self.hidden),
                self.six(modulation),
            ],
        )

    def expand(self, normed_two, unit, biases, index):
        bias = lax.dynamic_index_in_dim(biases, index, 0, keepdims=False)
        inner = times(normed_two, unit) + bias
        return inner, low(gelu(inner))

    def shrink(self, inner, active, shrink_slope, expand_unit, unit, *totals):
        active_slope = times_transposed(shrink_slope, unit)
        inner_slope = low(jax.vjp(gelu, inner)[1](active_slope)[0])
        out = times(active, unit)
        back = times_transposed(inner_slope, expand_unit)
        if totals:
            out, back = out + totals[0], back + totals[1]
        return inner_slope, column_sums(inner_slope)[None], out, back

    def finish(self, middle, branch, out, back, shrink_bias, modulation):
        layer_out, *others = self.per_image(
            finish_kernel,
            [
                ("rows", jnp.bfloat16),
                ("rows", jnp.float32),
                ("rows", jnp.bfloat16),
                (4, jnp.float32),
            ],
            [
                ("scalar", self.live),
                ("rows", middle),
                ("rows", branch),
                ("rows", out),
                ("rows", back),
                ("rows", self.flat(self.cotangent)),
                ("all", shrink_bias),
                self.six(modulation),
            ],
        )
        return layer_out.reshape(self.hidden_in.shape), *others

    def attention_back(self, slopes, queries, keys_all, values_all, logs):
        return attend_back(queries, keys_all, values_all, slopes, self.patch_mask, logs)

    def start_back(self, slopes, weights, middle_slope, modulation, later_slopes):
        gradient, first_slopes = self.per_image(
            start_back_kernel,
            [("rows", jnp.float32), (2, jnp.float32)],
            [("rows", slope) for slope in slopes]
            + [
                ((3, 0), weights),
                ("rows", middle_slope),
                ("rows", self.hidden),
                self.six(modulation),
            ],
        )
        modulation_slope = low(jnp.concatenate([first_slopes, later_slopes], 1))
        return gradient.reshape(self.hidden_in.shape), modulation_slope.reshape(self.slots, -1)

    def condition_back(self, slope):
        return jax.vjp(jax.nn.silu, self.condition.astype(jnp.float32))[1](slope)[0]


def act_rows(conditions, here, shard):
    rows = lax.dynamic_slice_in_dim(conditions, here * shard, shard, 1)
    return low(jax.nn.silu(rows.astype(jnp.float32)))


def unpack_kernel(parts, packed_ref, mod_ref, attend_ref, output_ref, expand_ref, shrink_ref):
    shard = output_ref.shape[1] // parts
    start = packed_ref.shape[1] - 14 * shard

    def joined(first, size):
        cut = [
            packed_ref[part : part + 1, start + first : start + first + size].astype(jnp.float32)
            for part in range(parts)
        ]
        return jnp.concatenate(cut, axis=1)

    mod_ref[...] = joined(0, 6 * shard)
    for row in range(2):
        attend_ref[row : row + 1] = joined((6 + row) * shard, shard)
    output_ref[...] = joined(8 * shard, shard)
    for unit in range(4):
        expand_ref[unit : unit + 1] = joined((9 + unit) * shard, shard)
    shrink_ref[...] = joined(13 * shard, shard)


def unpack(packed, shard):
    parts = packed.shape[0]
    width = parts * shard
    return pl.pallas_call(
        partial(unpack_kernel, parts),
        out_shape=[
            jax.ShapeDtypeStruct((rows, columns), jnp.float32)
            for rows, columns in ((1, 6 * width), (2, width), (1, width), (4, width), (1, width))
        ],
    )(packed)


def pack(condition, *biases):
    row = jnp.concatenate([condition.reshape(-1)] + [bias.reshape(-1) for bias in biases])
    return row[None]


def modulation_tail(modulation_slopes, conditions, here, shard, bias_size):
    weight = inner_rows(act_rows(conditions, here, shard), modulation_slopes)
    bias = lax.dynamic_slice_in_dim(modulation_slopes, here * bias_size, bias_size, 1)
    return weight, column_sums(bias)


def bias_tail(sums, here, shard):
    mine = lax.dynamic_slice_in_dim(sums, here * shard, shard, 1)
    return mine[0:2], mine[2], mine[4:8].reshape(-1), mine[3]


def condition_columns(gathered, image, slots):
    mine = lax.dynamic_slice_in_dim(gathered, image, slots, 1)
    return mine.transpose(1, 0, 2).reshape(slots, -1)


def plain_device(
    dp,
    rep,
    hidden_in,
    condition,
    patch_mask,
    image_counts,
    modulation_weight,
    modulation_bias,
    attend_weight,
    attend_bias,
    output_weight,
    output_bias,
    expand_weight,
    expand_bias,
    shrink_weight,
    shrink_bias,
    cotangent,
):
    here = lax.axis_index("dp")
    layer = Layer(hidden_in, condition, patch_mask, image_counts, cotangent)
    shard, width, slots = modulation_weight.shape[0], layer.width, layer.slots

    def whole(block):
        return lax.all_gather(block, "dp", axis=0, tiled=True)

    def summed(term):
        return lax.psum(
            lax.psum_scatter(term, "dp", scatter_dimension=0, tiled=True), "rep"
        ).astype(jnp.float32)

    packed = pack(
        condition, modulation_bias, attend_bias, output_bias, expand_bias, shrink_bias
    )
    packed = lax.all_gather(packed, "dp", axis=0, tiled=True)
    conditions = packed[:, : condition.size].reshape(-1, width)
    biases = unpack(packed, shard)
    expand_biases = biases[3].reshape(4, dp, shard).transpose(1, 0, 2).reshape(4, width)
    terms = times(act_rows(conditions, here, shard), modulation_weight)
    modulation = lax.psum_scatter(terms, "dp", scatter_dimension=0, tiled=True) + biases[0]
    weights = whole(jnp.concatenate([attend_weight, output_weight], 1))
    weights = weights.reshape(width, 4, width).transpose(1, 0, 2)
    expand_full, shrink_full = whole(expand_weight), whole(shrink_weight)
    normed_one = layer.start(modulation)
    shrink_slope = layer.shrink_slope(modulation)
    queries, keys_all, values_all, attended, logs = layer.attention(normed_one, weights, biases[1])
    branch, middle, normed_two = layer.middle(attended, weights, biases[2], modulation)
    totals = ()
    expand_terms, shrink_terms, inner_sums = [], [], []
    for unit in range(4):
        cut = slice(unit * width, (unit + 1) * width)
        inner, active = layer.expand(normed_two, expand_full[:, cut], expand_biases, unit)
        inner_slope, inner_sum, *totals = layer.shrink(
            inner, active, shrink_slope, expand_full[:, cut], shrink_full[cut], *totals
        )
        expand_terms.append(low(inner_rows(normed_two, inner_slope)))
        shrink_terms.append(low(inner_rows(active, shrink_slope)))
        inner_sums.append(inner_sum)
    layer_out, middle_slope, branch_low, later = layer.finish(
        middle, branch, *totals, biases[4], modulation
    )
    attended_slope = low(times_transposed(branch_low, weights[3]))
    slopes = layer.attention_back(attended_slope, queries, keys_all, values_all, logs)
    gradient_hidden, mod_slope = layer.start_back(
        slopes, weights, middle_slope, modulation, later
    )
    all_slopes = lax.all_gather(mod_slope, ("dp", "rep"), axis=0, tiled=True)
    all_conditions = lax.all_gather(condition, ("dp", "rep"), axis=0, tiled=True)
    mod_weight, mod_bias = modulation_tail(
        all_slopes, all_conditions, here, shard, modulation_bias.shape[0]
    )
    columns = lax.all_gather(times_transposed(all_slopes, modulation_weight), "dp")
    inner_sums = jnp.concatenate(inner_sums, 1).reshape(dp, 4, shard)
    inner_sums = inner_sums.transpose(1, 0, 2).reshape(4, width)
    others = [column_sums(value) for value in (slopes[0], slopes[2], branch_low, shrink_slope)]
    sums = lax.psum(jnp.concatenate([jnp.stack(others), inner_sums]), ("dp", "rep"))
    att_bias, out_bias, exp_bias, shr_bias = bias_tail(sums, here, shard)
    return (
        layer_out,
        gradient_hidden,
        layer.condition_back(condition_columns(columns, (here * rep + lax.axis_index("rep")) * slots, slots)),
        mod_weight,
        mod_bias,
        summed(low(inner_rows(normed_one, jnp.concatenate(slopes, 1)))),
        att_bias,
        summed(low(inner_rows(attended, branch_low))),
        out_bias,
        summed(jnp.concatenate(expand_terms, 1)),
        exp_bias,
        summed(jnp.concatenate(shrink_terms)),
        shr_bias,
    )


class Ticks:
    def __init__(self):
        self.ops = []

    def at(self, tick, outs, ins, call):
        outs, ins = [(names,) if isinstance(names, str) else names for names in (outs, ins)]
        self.ops.append((tick, len(self.ops), outs, ins, call))

    def run(self, results):
        ops = sorted(self.ops, key=lambda op: op[:2])
        last = {}
        for tick, _, _, ins, _ in ops:
            for name in ins:
                last[name] = tick
        state = {}
        for position, (tick, _, outs, ins, call) in enumerate(ops):
            values = call(*[state[name] for name in ins])
            if len(outs) == 1:
                values = (values,)
            state.update(zip(outs, values))
            ends = position + 1 == len(ops) or ops[position + 1][0] > tick
            if ends:
                names = sorted(name for name in state if last.get(name, -1) > tick)
                kept = [name for name in results if name in state and name not in names]
                final = {name: state[name] for name in kept}
                state = dict(zip(names, lax.optimization_barrier(tuple(state[n] for n in names))))
                state.update(final)
        return [state[name] for name in results]


def ticked_device(
    dp,
    rep,
    hidden_in,
    condition,
    patch_mask,
    image_counts,
    modulation_weight,
    modulation_bias,
    attend_weight,
    attend_bias,
    output_weight,
    output_bias,
    expand_weight,
    expand_bias,
    shrink_weight,
    shrink_bias,
    cotangent,
):
    here = lax.axis_index("dp")
    copy = lax.axis_index("rep")
    depth = dp // 2
    z, x, y, core = here // 2, here % 2, copy // 2, copy % 2
    order = [(2 * core + y) ^ step for step in range(4)]
    layer = Layer(hidden_in, condition, patch_mask, image_counts, cotangent)
    shard, width, slots = modulation_weight.shape[0], layer.width, layer.slots
    ticks = Ticks()
    at = ticks.at

    def up(value):
        return lax.ppermute(value, "dp", [(i, (i + 2) % dp) for i in range(dp)])

    def jump(step, value):
        return lax.ppermute(value, "dp", [(i, (i + 2 * step) % dp) for i in range(dp)])

    def swap_x(value):
        return lax.ppermute(value, "dp", [(i, i ^ 1) for i in range(dp)])

    def swap_y(value):
        return lax.ppermute(value, "rep", [(i, i ^ 2) for i in range(4)])

    def swap_core(value):
        return lax.ppermute(value, "rep", [(i, i ^ 1) for i in range(4)])

    def pair(one, two):
        return jnp.concatenate([one, two])

    def below(step):
        return (z - step) % depth

    def add(one, two):
        return low(one.astype(jnp.float32) + two.astype(jnp.float32))

    def attend_block(index):
        column = jnp.minimum(index, 2) * width
        block = lax.dynamic_slice_in_dim(attend_weight, column, width, 1)
        return jnp.where(index == 3, output_weight, block)[None]

    def shrink_block(index):
        return lax.dynamic_slice_in_dim(shrink_weight, index * shard, shard, 0)[None]

    def pick(stacked, index):
        return lax.dynamic_slice_in_dim(stacked, index, 1, 0)

    at(0, "A0", (), lambda: attend_block(order[0]))
    at(0, "a0", (), lambda: attend_block(order[1]))
    at(0, "Bs", (), lambda: regroup(expand_weight, dp))
    at(0, "P0", "Bs", lambda s: pick(s, order[1]))
    at(0, "C0", (), lambda: shrink_block(order[0]))
    at(0, "c0", (), lambda: shrink_block(order[1]))

    at(0, "AB0", ("A0", "Bs"), lambda p, q: pair(p, pick(q, order[0])))
    for name, ring_ticks, x_ticks in (
        ("AB", (0, 1, 2), (0, 1, 2, 3)),
        ("P", (3, 4, 5), (4, 5, 6, 6)),
        ("C", (3, 6, 7), (6, 7, 7, 8)),
    ):
        for step, tick in enumerate(ring_ticks):
            at(tick, f"{name}{step + 1}", f"{name}{step}", up)
        for step, tick in enumerate(x_ticks):
            at(tick, f"{name}x{step}", f"{name}{step}", swap_x)
    for step, tick in enumerate((1, 2, 3)):
        at(tick, f"ABy{step}", (f"ABx{step}", f"AB{step + 1}"),
           lambda p, q: swap_y(pair_rows(p, 0, q, 0)))
    at(4, "ABy3", "ABx3", lambda p: swap_y(p[:1]))
    for name, tick in (("C1", 5), ("Cx0", 7), ("Cx1", 8), ("C2", 8), ("Cx2", 8), ("C3", 9), ("Cx3", 9)):
        at(tick, f"{name}y", name, swap_y)

    def spot(step, cross):
        return 2 * below(step) + (1 - x if cross else x)

    def unit(blocks):
        parts = [(array, row) for array, row, _, _ in blocks]
        places = [spot(step, cross) for _, _, step, cross in blocks]
        return assemble(parts, places, dp).reshape(dp * shard, width)

    def streamed(zs, xs):
        return unit(
            [(array, row, step, False) for step, (array, row) in enumerate(zs)]
            + [(array, row, step, True) for step, (array, row) in enumerate(xs)]
        )

    def own_unit(row, *parts):
        return streamed([(part, row) for part in parts[:4]], [(part, row) for part in parts[4:]])

    def other_unit(local, *parts):
        return streamed(
            [(local, 0)] + [(part, 1) for part in parts[:3]], [(part, 0) for part in parts]
        )

    def steps(name, ending=""):
        zs = tuple(f"{name}{step}{ending}" for step in range(4))
        return zs, tuple(f"{name}x{step}{ending}" for step in range(4))

    for name, stream, row, tick in (
        ("Aown", "AB", 0, 4), ("Bown", "AB", 1, 5), ("By", "P", 0, 7), ("Cown", "C", 0, 9)
    ):
        zs, xs = steps(stream)
        at(tick, name, zs + xs, partial(own_unit, row))
    at(5, "Ay", ("a0",) + tuple(f"ABy{step}" for step in range(4)), other_unit)
    zs, xs = steps("C", "y")
    at(10, "Cy", ("c0",) + zs[1:] + xs, partial(own_unit, 0))
    at(4, "Ac", "Aown", swap_core)
    at(5, "Acy", "Ay", swap_core)
    at(6, "Bc", "Bown", swap_core)
    at(7, "Bcy", "By", swap_core)
    at(9, "Cc", "Cown", swap_core)
    at(10, "Ccy", "Cy", swap_core)

    def swap_z(distance, value):
        return lax.ppermute(value, "dp", [(i, i ^ (2 * distance)) for i in range(dp)])

    bits = {
        "core": (core, swap_core),
        "y": (y, swap_y),
        "x": (x, swap_x),
        "near": (z % 2, partial(swap_z, 1)),
        "far": (z // 2, partial(swap_z, 2)),
    }

    def grow(tick, name, axes):
        for axis in axes:
            bit, swap = bits[axis]

            def join(mine, other, bit=bit):
                return jnp.where(bit == 0, pair(mine, other), pair(other, mine))

            at(tick, name + "_in", name, swap)
            at(tick, name + "+", (name, name + "_in"), join)
            name += "+"
        return name

    def shrink_terms(tick, name, axes):
        for axis in axes:
            bit, swap = bits[axis]

            def send(terms, bit=bit, swap=swap):
                half = terms.shape[0] // 2
                return swap(lax.dynamic_slice_in_dim(terms, (1 - bit) * half, half, 0))

            def keep(terms, other, bit=bit):
                half = terms.shape[0] // 2
                return lax.dynamic_slice_in_dim(terms, bit * half, half, 0) + other

            at(tick, name + "_in", name, send)
            at(tick, name + "-", (name, name + "_in"), keep)
            name += "-"
        return name

    at(0, "small", (), lambda: pack(
        condition, modulation_bias, attend_bias, output_bias, expand_bias, shrink_bias))
    small = grow(0, "small", ("x",))
    small = grow(1, small, ("near",))
    small = grow(2, small, ("far",))
    at(3, ("mod_bias", "att_bias", "out_bias", "exp_bias", "shr_bias"), small,
       lambda packed: unpack(packed, shard))

    def first_terms(packed):
        conditions = packed[:, : condition.size].reshape(2, 2, 2, slots, width)
        conditions = conditions.transpose(2, 1, 0, 3, 4).reshape(-1, width)
        return times(act_rows(conditions, here, shard), modulation_weight)

    at(2, "terms", small, first_terms)
    terms = shrink_terms(3, "terms", ("x",))
    terms = shrink_terms(4, terms, ("near",))
    terms = shrink_terms(5, terms, ("far",))
    at(6, "mod", (f"{terms}", "mod_bias"), lambda terms, bias: terms + bias)
    at(6, "n1", "mod", layer.start)
    at(6, "gm", "mod", layer.shrink_slope)

    def natural(*units):
        return reorder(units, order, 8)

    at(6, "W", ("Aown", "Ay", "Ac", "Acy"), natural)
    at(6, ("q", "k", "v", "att", "logs"), ("n1", "W", "att_bias"), lambda n1, w, bias: layer.attention(n1, w, bias))
    at(7, ("branch", "middle", "n2"), ("att", "W", "out_bias", "mod"), layer.middle)

    def expand(index, n2, weight, biases):
        return layer.expand(n2, weight, biases, order[index])

    def term(left, right, *received):
        total = inner_rows(left, right)
        for value in received:
            total = total + value.astype(jnp.float32)
        return low(total)

    for index, (name, tick) in enumerate((("own", 7), ("y", 8), ("c", 7), ("cy", 8))):
        at(tick, (f"in_{name}", f"act_{name}"), ("n2", f"B{name}", "exp_bias"), partial(expand, index))
    at(7, "dC_c", ("act_c", "gm"), term)
    at(8, "dC_cy", ("act_cy", "gm"), term)
    at(9, "dC_own", ("act_own", "gm", "dC_rc"), term)
    at(10, "dC_y", ("act_y", "gm", "dC_rcy"), term)

    total = ()
    for index, (name, tick) in enumerate((("own", 9), ("c", 10), ("cy", 11), ("y", 12))):
        ins = (f"in_{name}", f"act_{name}", "gm", f"B{name}", f"C{name}") + total
        total = (f"out{index}", f"back{index}")
        at(tick, (f"gi_{name}", f"sum_{name}") + total, ins, layer.shrink)
    at(10, "dB_c", ("n2", "gi_c"), term)
    at(11, "dB_cy", ("n2", "gi_cy"), term)
    at(12, "dB_own", ("n2", "gi_own", "dB_rc"), term)
    at(13, "dB_y", ("n2", "gi_y", "dB_rcy"), term)

    at(13, ("layer_out", "middle_slope", "branch_low", "later"),
       ("middle", "branch", "out3", "back3", "shr_bias", "mod"), layer.finish)
    at(13, "g_att", ("branch_low", "W"), lambda b, w: low(times_transposed(b, w[3])))
    at(14, ("gq", "gk", "gv"), ("g_att", "q", "k", "v", "logs"), layer.attention_back)
    at(15, ("gradient_hidden", "mod_slope"), ("gq", "gk", "gv", "W", "middle_slope", "mod", "later"),
       lambda a, b, c, w, ms, mod, later: layer.start_back((a, b, c), w, ms, mod, later))

    def attend_term(index, n1, att, gq, gk, gv, branch_low, *received):
        which = order[index]
        right = lax.select_n(which, gq, gk, gv, branch_low)
        return term(jnp.where(which == 3, att, n1), right, *received)

    for index, (name, tick, received) in enumerate(
        (("own", 16, ("dA_rc",)), ("y", 16, ("dA_rcy",)), ("c", 14, ()), ("cy", 14, ()))
    ):
        ins = ("n1", "att", "gq", "gk", "gv", "branch_low") + received
        at(tick, f"dA_{name}", ins, partial(attend_term, index))

    def slab(step, moved, whole, *parts):
        cut = lax.dynamic_slice_in_dim(whole, below(step) * (2 * shard), 2 * shard, 0)
        if parts:
            cut = low(sum(value.astype(jnp.float32) for value in (cut,) + parts))
        return moved(cut)

    def stay(value):
        return value

    def along_ring(name, start, source, added):
        for step in range(1, 5):
            ins = (source,) + tuple(f"{part}{step}" for part in added)
            if step > 1:
                ins += (f"{name}{step - 1}",)
            at(start + step - 1, f"{name}{step}", ins, partial(slab, step, up if step < 4 else stay))
        at(start + 3, f"{name}_in", f"{name}4", lambda total: swap_x(
            lax.dynamic_slice_in_dim(total, (1 - x) * shard, shard, 0)))
        at(start + 4, f"{name}_sum", (f"{name}4", f"{name}_in"), lambda total, other: low(
            lax.dynamic_slice_in_dim(total, x * shard, shard, 0).astype(jnp.float32)
            + other.astype(jnp.float32)))
        return f"{name}_sum"

    def wide(name, start_own, start_other, late):
        one = along_ring(f"{name}_o", start_own, f"{name}_own", ())
        two = along_ring(f"{name}_p", start_other, f"{name}_y", ())
        at(late, f"{name}_yo", two, swap_y)
        at(late, f"{name}_yp", one, swap_y)
        at(late + 1, f"{name}_0", (one, f"{name}_yo"), add)
        at(late + 1, f"{name}_1", (two, f"{name}_yp"), add)
        at(late + 1, f"{name}_2", f"{name}_0", swap_core)
        at(late + 1, f"{name}_3", f"{name}_1", swap_core)
        return late + 2

    def halved(name, y_ticks, start_ring, late):
        for step, tick in enumerate(y_ticks, 1):
            at(tick, f"{name}_s{step}", f"{name}_y", partial(slab, step, swap_y))
        one = along_ring(f"{name}_o", start_ring, f"{name}_own", (f"{name}_s",))
        at(late, f"{name}_0", one, stay)
        at(late, f"{name}_1", one, swap_y)
        at(late + 1, f"{name}_2", one, swap_core)
        at(late + 1, f"{name}_3", f"{name}_1", swap_core)
        return late + 2

    for name, tick_one, tick_two in (("dC", 8, 9), ("dB", 11, 12), ("dA", 15, 15)):
        at(tick_one, f"{name}_rc", f"{name}_c", swap_core)
        at(tick_two, f"{name}_rcy", f"{name}_cy", swap_core)
    end_c = wide("dC", 9, 12, 21)
    end_b = halved("dB", (13, 14, 14, 15), 14, 20)
    end_a = halved("dA", (16, 17, 18, 19), 17, 21)

    def attend_out(*units):
        whole = jnp.zeros((4,) + units[0].shape, units[0].dtype)
        for index, value in zip(order, units):
            whole = lax.dynamic_update_slice(whole, value[None], (index, 0, 0))
        whole = whole.astype(jnp.float32)
        return jnp.concatenate([whole[0], whole[1], whole[2]], 1), whole[3]

    def shrink_out(*units):
        whole = assemble([(unit[None], 0) for unit in units], order, 4)
        return whole.reshape(-1, width).astype(jnp.float32)

    def four(name):
        return tuple(f"{name}_{i}" for i in range(4))

    at(end_c, "shr_weight", four("dC"), shrink_out)
    at(end_b, "exp_weight", four("dB"), lambda *units: spread(units, order, dp))
    at(end_a, ("att_weight", "out_weight"), four("dA"), attend_out)

    def join(tick, name, axis):
        at(tick, name + "_in", name, bits[axis][1])
        at(tick, name + "+", (name, name + "_in"), pair)
        return name + "+"

    mod_size = 6 * width
    def bias_terms(gq, gv, branch_low, gm, *sums):
        unit_sums = jnp.zeros((4, width), jnp.float32)
        for index, value in zip(order, sums):
            unit_sums = lax.dynamic_update_slice(unit_sums, value, (index, 0))
        others = jnp.stack([column_sums(value) for value in (gq, gv, branch_low, gm)])
        return low(pair(others, unit_sums)).reshape(slots, -1)

    at(15, "sums", ("gq", "gv", "branch_low", "gm", "sum_own", "sum_y", "sum_c", "sum_cy"), bias_terms)
    at(16, "sent", ("mod_slope", "sums"), lambda m, sums: jnp.concatenate([m, condition, sums], 1))
    sent = "sent"
    for tick, axis in ((16, "y"), (17, "far"), (18, "near"), (19, "x"), (19, "core")):
        sent = join(tick, sent, axis)

    def modulation_terms(sent):
        slopes = sent[:, :mod_size]
        weight, bias = modulation_tail(
            slopes, sent[:, mod_size : mod_size + width], here, shard, modulation_bias.shape[0]
        )
        row = lax.broadcasted_iota(jnp.int32, (slots, sent.shape[0]), 1)
        picked = low(row % slots == lax.broadcasted_iota(jnp.int32, row.shape, 0))
        sums = times(picked, sent[:, mod_size + width :]).reshape(-1, width)
        return (weight, bias) + bias_tail(sums, here, shard)

    at(20, "columns", sent, lambda sent: times_transposed(sent[:, :mod_size], modulation_weight))
    at(20, ("mod_weight", "mod_bias_out", "att_bias_out", "out_bias_out", "exp_bias_out", "shr_bias_out"),
       sent, modulation_terms)

    def trade(tick, name, axis, swap):
        at(tick, name + "_in", name, lambda held: swap(jnp.split(held, 2, axis)[1]))
        at(tick, name + "+", (name, name + "_in"), lambda held, got: jnp.stack(
            [jnp.split(held, 2, axis)[0], got]))
        return name + "+"

    at(20, "traded", "columns", lambda columns: columns.reshape(
        2, 2, 2, 2, 2, slots, shard)[0, :, :, :, 0])
    traded = trade(20, "traded", 0, swap_x)
    traded = trade(21, traded, 2, partial(swap_z, 1))
    traded = trade(22, traded, 4, partial(swap_z, 2))

    def condition_slope(held):
        for axis, bit in enumerate((z // 2, z % 2, x)):
            held = jnp.where(bit == 1, jnp.flip(held, axis), held)
        held = held.reshape(dp, slots, shard).transpose(1, 0, 2)
        return layer.condition_back(held.reshape(slots, width))

    at(23, "gradient_condition", traded, condition_slope)
    return tuple(
        ticks.run(
            [
                "layer_out",
                "gradient_hidden",
                "gradient_condition",
                "mod_weight",
                "mod_bias_out",
                "att_weight",
                "att_bias_out",
                "out_weight",
                "out_bias_out",
                "exp_weight",
                "exp_bias_out",
                "shr_weight",
                "shr_bias_out",
            ]
        )
    )


def solution(mesh):
    dp, rep = mesh.shape["dp"], mesh.shape["rep"]
    device = ticked_device if (dp, rep) == (8, 4) else plain_device
    return jax.shard_map(
        partial(device, dp, rep),
        mesh=mesh,
        in_specs=(
            P(("dp", "rep"), None, None),
            P(("dp", "rep"), None),
            P(("dp", "rep"), None),
            P(("dp", "rep")),
            P("dp", None),
            P("dp"),
            P("dp", None),
            P(None, "dp"),
            P("dp", None),
            P("dp"),
            P("dp", None),
            P("dp"),
            P("dp", None),
            P("dp"),
            P(("dp", "rep"), None, None),
        ),
        out_specs=(
            P(("dp", "rep"), None, None),
            P(("dp", "rep"), None, None),
            P(("dp", "rep"), None),
            P("dp", None),
            P("dp"),
            P("dp", None),
            P(None, "dp"),
            P("dp", None),
            P("dp"),
            P("dp", None),
            P("dp"),
            P("dp", None),
            P("dp"),
        ),
        check_vma=False,
    )
```

time: 2630 us -> 536 us (0.20)
  waiting for transfers between devices: 2180 us -> 185 us
  blocking collectives: 126 us -> 0 us
  starting transfers between devices: 0.98 us -> 76.5 us
  Pallas kernels: 0 us -> 69.2 us
  local copies, waits for them, and re-layouts: 101 us -> 41 us
  matrix products: 156 us -> 103 us
    reduce_scatter x5 -> x0, waiting for transfers between devices: 1440 us -> none  [the longest x1 511 us: per_device(): lax.psum_scatter(inner_rows(cond_low, modulation_slope), 'dp', scatter_di...]
    all_gather x8 -> x0, waiting for transfers between devices: 591 us -> none  [the longest x1 157 us: per_device(): lax.all_gather(modulation_weight, 'dp', axis=0, tiled=True)]
    ppermute x0 -> x92, waiting for transfers between devices: none -> 185 us  [the longest x24 69.9 us: swap_y(): return lax.ppermute(value, 'rep', [(i, i ^ 2) for i in range(4)])]
    unnamed x25 -> x0, waiting for transfers between devices: 145 us -> none
    unnamed x3 -> x0, blocking collectives: 82.6 us -> none
    ppermute x0 -> x92, starting transfers between devices: none -> 76.5 us  [the longest x21 24.1 us: up(): return lax.ppermute(value, 'dp', [(i, (i + 2) % dp) for i in range(dp)])]
    pallas_call x0 -> x16, Pallas kernels: none -> 69.2 us  [the longest x3 26.6 us: per_image(): pl.pallas_call(kernel, grid=(self.slots,), in_specs=[spec(kind, array.sha...]
    all_gather x4 -> x0, blocking collectives: 43.4 us -> none  [the longest x1 22.4 us: per_device(): lax.all_gather(attend_bias, 'dp', axis=1, tiled=True)]
  transfers between devices with their start and end apart: 19 -> 92, of which waited for: 18 -> 35; matrix products, arithmetic and copies ran while one was open for 10% -> 30% of each run, Pallas kernels for 0% -> 11%
where the time goes in v2:
time: 536 us; the launch traced here: 529 us
  waiting for transfers between devices  185 us (35%)
  matrix products  103 us (19%)
  starting transfers between devices  76.5 us (14%)
  Pallas kernels  69.2 us (13%)
  other arithmetic  50.8 us (9%)
  local copies, waits for them, and re-layouts  41 us (8%)
    ppermute x24, waiting for transfers between devices, swap_y(): return lax.ppermute(value, 'rep', [(i, i ^ 2) for i in range(4)])  69.9 us
    ppermute x21, waiting for transfers between devices, up(): return lax.ppermute(value, 'dp', [(i, (i + 2) % dp) for i in range(dp)])  45.1 us
    ppermute x8, waiting for transfers between devices, swap_z(): return lax.ppermute(value, 'dp', [(i, i ^ 2 * distance) for i in range(dp)])  40.3 us
    dot_general x13, matrix products, inner_rows(): lax.dot_general(left_side, right_side, (((0,), (0,)), ((), ())), preferre...  39.2 us
    dot_general x13, matrix products, times(): return jnp.dot(left_side, right_side, preferred_element_type=jnp.float32)  35.8 us
    ppermute x20, waiting for transfers between devices, swap_x(): return lax.ppermute(value, 'dp', [(i, i ^ 1) for i in range(dp)])  29.3 us
    dot_general x10, matrix products, times_transposed(): lax.dot_general(left_side, right_side, (((1,), (1,)), ((), ())), preferre...  28.2 us
    pallas_call x3, Pallas kernels, per_image(): pl.pallas_call(kernel, grid=(self.slots,), in_specs=[spec(kind, array.sha...  26.6 us
  transfers between devices with their start and end apart: 92, of which 35 were waited for; matrix products, arithmetic and copies ran while one was open for 30% of the time, Pallas kernels for 11%

profile of v2, /device:TPU:0, one launch (start us, length us, event | category | flops | bytes accessed | tf_op | source)
XLA Modules:
  0.0 529.0 jit_solution(5193992539818466901)
XLA Ops:
  14.6 10.9 %collective-permute-done.2 = bf16[1,4320]{1,0:T(2,128)(2,1)S(1)} collective-permute-done((bf16[1,4320]{1,0:T(2,128)(2,1)S(1)}, bf16[1,4320]{1,0:T(2,128)(2,1)S(1)}, u32[]{:S(2)}, u32[]{:S(2)}) %collective-permute-start.2) | collective-permute-done | bytes 8672 | tf_op jit(solution)/shard_map/ppermute | solution.py:712
  34.7 9.3 %collective-permute-done.6 = bf16[2,4320]{1,0:T(2,128)(2,1)S(1)} collective-permute-done((bf16[2,4320]{1,0:T(2,128)(2,1)S(1)}, bf16[2,4320]{1,0:T(2,128)(2,1)S(1)}, u32[]{:S(2)}, u32[]{:S(2)}) %collective-permute-start.6) | collective-permute-done | bytes 17312 | tf_op jit(solution)/shard_map/ppermute | solution.py:806
  54.5 10.9 %collective-permute-done.10 = bf16[4,4320]{1,0:T(4,128)(2,1)S(1)} collective-permute-done((bf16[4,4320]{1,0:T(4,128)(2,1)S(1)}, bf16[4,4320]{1,0:T(4,128)(2,1)S(1)}, u32[]{:S(2)}, u32[]{:S(2)}) %collective-permute-start.10) | collective-permute-done | bytes 34592 | tf_op jit(solution)/shard_map/ppermute | solution.py:806
  77.7 10.7 %collective-permute-done.15 = f32[8,6912]{1,0:T(8,128)} collective-permute-done((f32[8,6912]{1,0:T(8,128)}, f32[8,6912]{1,0:T(8,128)}, u32[]{:S(2)}, u32[]{:S(2)}) %collective-permute-start.15) | collective-permute-done | bytes 221216 | tf_op jit(solution)/shard_map/ppermute | solution.py:712
  100.4 5.8 %collective-permute-done.16.refs_7_ = bf16[1,144,1152]{2,1,0:T(8,128)(2,1)S(1)} collective-permute-done((bf16[1,144,1152]{2,1,0:T(8,128)(2,1)S(1)}, bf16[1,144,1152]{2,1,0:T(8,128)(2,1)S(1)}, u32[]{:S(2)}, u32[]{:S(2)}) %collective-permute-start.16) | collective-permute-done | bytes 331808 | tf_op jit(solution)/shard_map/ppermute | solution.py:715
  138.1 5.7 %shard_map.251.weight_ref = bf16[4,1152,1152]{2,1,0:T(8,128)(2,1)S(1)} custom-call(s32[4]{0:T(128)S(1)} %pad_add_fusion.place_ref.order_ref, bf16[1152,1152]{1,0:T(8,128)(2,1)S(1)} %bitcast.170, bf16[1152,1152]{1,0:T(8,128)(2,1)} %bitcast.21.refs_1_, bf16[1152,1152]{1,0:T(8,128)(2,1)S(1)} %copy-done.14, bf16[1152,1152]{1,0:T(8,128)(2,1)} %collective-permute-done.21.refs_3_), custom_call_target="tpu_custom_call" | custom-call | bytes 21233664 | tf_op jit(solution)/shard_map/pallas_call | solution.py:296
  150.2 5.2 shard_map.252
  165.9 6.9 %shard_map.254 = (f32[512,1152]{1,0:T(8,128)}, f32[512,1152]{1,0:T(8,128)}, bf16[512,1152]{1,0:T(8,128)(2,1)}) custom-call(bf16[512,1152]{1,0:T(8,128)(2,1)} %copy-done.21, bf16[4,1152,1152]{2,1,0:T(8,128)(2,1)} %copy-done.1, f32[1,1152]{1,0:T(1,128)} %get-tuple-element.619.bias_ref, bf16[512,1152]{1,0:T(8,128)(2,1)} %bitcast.184, ...), custom_call_target="tpu_custom_call" | custom-call | tf_op jit(solution)/shard_map/pallas_call | solution.py:411
  172.9 4.8 fusion.51
  189.4 4.1 fusion.67
  193.6 5.2 fusion.75
  203.9 6.7 %collective-permute-done.38.refs_6_ = bf16[1,144,1152]{2,1,0:T(8,128)(2,1)S(1)} collective-permute-done((bf16[1,144,1152]{2,1,0:T(8,128)(2,1)}, bf16[1,144,1152]{2,1,0:T(8,128)(2,1)S(1)}, u32[]{:S(2)}, u32[]{:S(2)}) %collective-permute-start.38) | collective-permute-done | bytes 331808 | tf_op jit(solution)/shard_map/ppermute | solution.py:715
  229.5 8.1 %collective-permute-done.44 = bf16[288,1152]{1,0:T(8,128)(2,1)S(1)} collective-permute-done((bf16[288,1152]{1,0:T(8,128)(2,1)S(1)}, bf16[288,1152]{1,0:T(8,128)(2,1)S(1)}, u32[]{:S(2)}, u32[]{:S(2)}) %collective-permute-start.44) | collective-permute-done | bytes 663584 | tf_op jit(solution)/shard_map/ppermute | solution.py:706
  268.4 7.5 %collective-permute-done.49 = bf16[288,1152]{1,0:T(8,128)(2,1)S(1)} collective-permute-done((bf16[288,1152]{1,0:T(8,128)(2,1)S(1)}, bf16[288,1152]{1,0:T(8,128)(2,1)S(1)}, u32[]{:S(2)}, u32[]{:S(2)}) %collective-permute-start.49) | collective-permute-done | bytes 663584 | tf_op jit(solution)/shard_map/ppermute | solution.py:706
  283.7 5.5 %convolution_add_fusion.7.back_ref = f32[512,1152]{1,0:T(8,128)} fusion(f32[512,1152]{1,0:T(8,128)S(1)} %convolution_add_fusion.9, bf16[512,1152]{1,0:T(8,128)(2,1)S(1)} %get-tuple-element.815, bf16[1152,1152]{1,0:T(8,128)(2,1)} %bitcast.32), kind=kOutput, calls=%fused_computation.31 | convolution fusion | flops 1359544320 | bytes 8552448 | tf_op jit(solution)/shard_map/dot_general | solution.py:47
  299.7 4.2 fusion.3
  304.4 7.2 %shard_map.257 = (bf16[512,1152]{1,0:T(8,128)(2,1)}, f32[512,1152]{1,0:T(8,128)}, bf16[512,1152]{1,0:T(8,128)(2,1)}, f32[2,4,1152]{2,1,0:T(4,128)}) custom-call(f32[2]{0:T(128)} %copy-done.89, f32[512,1152]{1,0:T(8,128)} %get-tuple-element.803.middle_ref, f32[512,1152]{1,0:T(8,128)} %get-tuple-element.804.branch_ref, ...), custom_call_target="tpu_custom_call" | custom-call | tf_op jit(solution)/shard_map/pallas_call | solution.py:411
  311.7 4.1 convolution_convert_fusion.6.slope_ref
  328.5 13.5 %shard_map.258 = (bf16[512,1152]{1,0:T(8,128)(2,1)S(1)}, bf16[512,1152]{1,0:T(8,128)(2,1)S(1)}, bf16[512,1152]{1,0:T(8,128)(2,1)S(1)}) custom-call(bf16[512,1152]{1,0:T(8,128)(2,1)S(1)} %copy-done.7, bf16[512,1152]{1,0:T(8,128)(2,1)S(1)} %convolution_convert_fusion.7.key_ref, bf16[512,1152]{1,0:T(8,128)(2,1)S(1)} %copy-done.5, ...), custom_call_target="tpu_custom_call" | custom-call | tf_op jit(solution)/shard_map/pallas_call | solution.py:157
  366.0 12.5 %shard_map.259 = (f32[512,1152]{1,0:T(8,128)}, f32[2,2,1152]{2,1,0:T(2,128)}) custom-call(bf16[512,1152]{1,0:T(8,128)(2,1)} %copy-done.8, bf16[512,1152]{1,0:T(8,128)(2,1)} %copy-done.24, bf16[512,1152]{1,0:T(8,128)(2,1)} %copy-done.11, bf16[4,1152,1152]{2,1,0:T(8,128)(2,1)} %copy-done.1, f32[512,1152]{1,0:T(8,128)} %get-tuple-element.863.middle_slope_ref, ...), custom_call_target="tpu_custom_call" | custom-call | tf_op jit(solution)/shard_map/pallas_call | solution.py:411
  384.6 4.1 fusion.5
  389.3 4.3 fusion.4
  395.7 4.8 collective-permute-done.65
  409.8 15.1 %collective-permute-done.70 = bf16[4,12672]{1,0:T(4,128)(2,1)S(1)} collective-permute-done((bf16[4,12672]{1,0:T(4,128)(2,1)S(1)}, bf16[4,12672]{1,0:T(4,128)(2,1)S(1)}, u32[]{:S(2)}, u32[]{:S(2)}) %collective-permute-start.70) | collective-permute-done | bytes 101408 | tf_op jit(solution)/shard_map/ppermute | solution.py:806
  428.5 4.8 collective-permute-done.73
  433.3 5.5 %collective-permute-done.72 = bf16[288,1152]{1,0:T(8,128)(2,1)S(1)} collective-permute-done((bf16[288,1152]{1,0:T(8,128)(2,1)S(1)}, bf16[288,1152]{1,0:T(8,128)(2,1)S(1)}, u32[]{:S(2)}, u32[]{:S(2)}) %collective-permute-start.72) | collective-permute-done | bytes 663584 | tf_op jit(solution)/shard_map/ppermute | solution.py:715
  438.8 5.9 %collective-permute-done.71 = bf16[288,1152]{1,0:T(8,128)(2,1)S(1)} collective-permute-done((bf16[288,1152]{1,0:T(8,128)(2,1)S(1)}, bf16[288,1152]{1,0:T(8,128)(2,1)S(1)}, u32[]{:S(2)}, u32[]{:S(2)}) %collective-permute-start.71) | collective-permute-done | bytes 663584 | tf_op jit(solution)/shard_map/ppermute | solution.py:706
  445.5 7.7 %collective-permute-done.76 = bf16[16,12672]{1,0:T(8,128)(2,1)S(1)} collective-permute-done((bf16[16,12672]{1,0:T(8,128)(2,1)S(1)}, bf16[16,12672]{1,0:T(8,128)(2,1)S(1)}, u32[]{:S(2)}, u32[]{:S(2)}) %collective-permute-start.76) | collective-permute-done | bytes 405536 | tf_op jit(solution)/shard_map/ppermute | solution.py:712
  458.7 14.0 %collective-permute-done.75 = bf16[288,1152]{1,0:T(8,128)(2,1)S(1)} collective-permute-done((bf16[288,1152]{1,0:T(8,128)(2,1)S(1)}, bf16[288,1152]{1,0:T(8,128)(2,1)S(1)}, u32[]{:S(2)}, u32[]{:S(2)}) %collective-permute-start.75) | collective-permute-done | bytes 663584 | tf_op jit(solution)/shard_map/ppermute | solution.py:715
  496.6 7.9 %collective-permute-done.81 = bf16[144,1152]{1,0:T(8,128)(2,1)S(1)} collective-permute-done((bf16[144,1152]{1,0:T(8,128)(2,1)S(1)}, bf16[144,1152]{1,0:T(8,128)(2,1)S(1)}, u32[]{:S(2)}, u32[]{:S(2)}) %collective-permute-start.81) | collective-permute-done | bytes 331808 | tf_op jit(solution)/shard_map/ppermute | solution.py:715
  504.5 7.1 %collective-permute-done.84 = bf16[144,1152]{1,0:T(8,128)(2,1)S(1)} collective-permute-done((bf16[144,1152]{1,0:T(8,128)(2,1)}, bf16[144,1152]{1,0:T(8,128)(2,1)S(1)}, u32[]{:S(2)}, u32[]{:S(2)}) %collective-permute-start.84) | collective-permute-done | bytes 331808 | tf_op jit(solution)/shard_map/ppermute | solution.py:715
  511.6 4.6 collective-permute-done.85
  (585 shorter events, 290.7 us)
Async XLA Ops:
  5.8 20.0 %collective-permute-start = (bf16[2,144,1152]{2,1,0:T(8,128)(2,1)S(1)}, bf16[2,144,1152]{2,1,0:T(8,128)(2,1)S(1)}, u32[]{:S(2)}, u32[]{:S(2)}) collective-permute-start(bf16[2,144,1152]{2,1,0:T(8,128)(2,1)S(1)} %pad_maximum_fusion.3.refs_0_), channel_id=1, source_target_pairs={{0,8},{4,12},{8,16},{12,20},{16,24},{20,28},{24,0},{28,4},{1,9},{5... | collective-permute-start | bytes 1990664 | tf_op jit(solution)/shard_map/ppermute | solution.py:706
  25.8 21.7 %collective-permute-start.3 = (bf16[2,144,1152]{2,1,0:T(8,128)(2,1)S(1)}, bf16[2,144,1152]{2,1,0:T(8,128)(2,1)}, u32[]{:S(2)}, u32[]{:S(2)}) collective-permute-start(bf16[2,144,1152]{2,1,0:T(8,128)(2,1)S(1)} %collective-permute-done.refs_1_), channel_id=1, source_target_pairs={{0,8},{4,12},{8,16},{12,20},{16,24},{20,28},{24,0},{28,4},{1,9},{5... | collective-permute-start | bytes 1990664 | tf_op jit(solution)/shard_map/ppermute | solution.py:706
  27.3 20.1 %collective-permute-start.4 = (bf16[2,144,1152]{2,1,0:T(8,128)(2,1)S(1)}, bf16[2,144,1152]{2,1,0:T(8,128)(2,1)}, u32[]{:S(2)}, u32[]{:S(2)}) collective-permute-start(bf16[2,144,1152]{2,1,0:T(8,128)(2,1)S(1)} %collective-permute-done.refs_1_), channel_id=1, source_target_pairs={{0,4},{4,0},{8,12},{12,8},{16,20},{20,16},{24,28},{28,24},{1,5},{5... | collective-permute-start | bytes 1990664 | tf_op jit(solution)/shard_map/ppermute | solution.py:712
  68.0 22.9 %collective-permute-start.11 = (bf16[2,144,1152]{2,1,0:T(8,128)(2,1)}, bf16[2,144,1152]{2,1,0:T(8,128)(2,1)}, u32[]{:S(2)}, u32[]{:S(2)}) collective-permute-start(bf16[2,144,1152]{2,1,0:T(8,128)(2,1)} %collective-permute-done.7.refs_3_), channel_id=1, source_target_pairs={{0,4},{4,0},{8,12},{12,8},{16,20},{20,16},{24,28},{28,24},{1,5},{5... | collective-permute-start | bytes 1990664 | tf_op jit(solution)/shard_map/ppermute | solution.py:712
  129.3 27.7 %collective-permute-start.26 = (bf16[1152,1152]{1,0:T(8,128)(2,1)}, bf16[1152,1152]{1,0:T(8,128)(2,1)S(1)}, u32[]{:S(2)}, u32[]{:S(2)}) collective-permute-start(bf16[1152,1152]{1,0:T(8,128)(2,1)} %bitcast.177), channel_id=1, source_target_pairs={{0,1},{1,0},{2,3},{3,2},{4,5},{5,4},{6,7},{7,6},{8,9},{9,8},{10,11... | collective-permute-start | bytes 7962632 | tf_op jit(solution)/shard_map/ppermute | solution.py:718
  129.5 27.5 %collective-permute-start.27 = (bf16[1,144,1152]{2,1,0:T(8,128)(2,1)}, bf16[1,144,1152]{2,1,0:T(8,128)(2,1)S(1)}, u32[]{:S(2)}, u32[]{:S(2)}) collective-permute-start(bf16[1,144,1152]{2,1,0:T(8,128)(2,1)} %collective-permute-done.13.refs_1_), channel_id=1, source_target_pairs={{0,8},{4,12},{8,16},{12,20},{16,24},{20,28},{24,0},{28,4},{1,9},{5... | collective-permute-start | bytes 995336 | tf_op jit(solution)/shard_map/ppermute | solution.py:706
  130.8 26.1 %collective-permute-start.28 = (bf16[1,144,1152]{2,1,0:T(8,128)(2,1)}, bf16[1,144,1152]{2,1,0:T(8,128)(2,1)S(1)}, u32[]{:S(2)}, u32[]{:S(2)}) collective-permute-start(bf16[1,144,1152]{2,1,0:T(8,128)(2,1)} %get-tuple-element.672.refs_0_), channel_id=1, source_target_pairs={{0,4},{4,0},{8,12},{12,8},{16,20},{20,16},{24,28},{28,24},{1,5},{5... | collective-permute-start | bytes 995336 | tf_op jit(solution)/shard_map/ppermute | solution.py:712
  132.5 24.4 %collective-permute-start.29 = (bf16[1,144,1152]{2,1,0:T(8,128)(2,1)}, bf16[1,144,1152]{2,1,0:T(8,128)(2,1)S(1)}, u32[]{:S(2)}, u32[]{:S(2)}) collective-permute-start(bf16[1,144,1152]{2,1,0:T(8,128)(2,1)} %copy-done.34), channel_id=1, source_target_pairs={{0,4},{4,0},{8,12},{12,8},{16,20},{20,16},{24,28},{28,24},{1,5},{5... | collective-permute-start | bytes 995336 | tf_op jit(solution)/shard_map/ppermute | solution.py:712
  132.9 24.1 %collective-permute-start.30 = (bf16[1,144,1152]{2,1,0:T(8,128)(2,1)}, bf16[1,144,1152]{2,1,0:T(8,128)(2,1)S(1)}, u32[]{:S(2)}, u32[]{:S(2)}) collective-permute-start(bf16[1,144,1152]{2,1,0:T(8,128)(2,1)} %collective-permute-done.23.refs_3_), channel_id=1, source_target_pairs={{0,4},{4,0},{8,12},{12,8},{16,20},{20,16},{24,28},{28,24},{1,5},{5... | collective-permute-start | bytes 995336 | tf_op jit(solution)/shard_map/ppermute | solution.py:712
  160.7 25.5 %collective-permute-start.31 = (bf16[1152,1152]{1,0:T(8,128)(2,1)}, bf16[1152,1152]{1,0:T(8,128)(2,1)}, u32[]{:S(2)}, u32[]{:S(2)}) collective-permute-start(bf16[1152,1152]{1,0:T(8,128)(2,1)} %bitcast.32), channel_id=1, source_target_pairs={{0,1},{1,0},{2,3},{3,2},{4,5},{5,4},{6,7},{7,6},{8,9},{9,8},{10,11... | collective-permute-start | bytes 7962632 | tf_op jit(solution)/shard_map/ppermute | solution.py:718
  160.7 24.0 %collective-permute-start.32 = (bf16[1,144,1152]{2,1,0:T(8,128)(2,1)S(1)}, bf16[1,144,1152]{2,1,0:T(8,128)(2,1)}, u32[]{:S(2)}, u32[]{:S(2)}) collective-permute-start(bf16[1,144,1152]{2,1,0:T(8,128)(2,1)S(1)} %collective-permute-done.27.refs_2_), channel_id=1, source_target_pairs={{0,8},{4,12},{8,16},{12,20},{16,24},{20,28},{24,0},{28,4},{1,9},{5... | collective-permute-start | bytes 995336 | tf_op jit(solution)/shard_map/ppermute | solution.py:706
  161.2 24.3 %collective-permute-start.35 = (bf16[1,144,1152]{2,1,0:T(8,128)(2,1)S(1)}, bf16[1,144,1152]{2,1,0:T(8,128)(2,1)}, u32[]{:S(2)}, u32[]{:S(2)}) collective-permute-start(bf16[1,144,1152]{2,1,0:T(8,128)(2,1)S(1)} %collective-permute-done.27.refs_2_), channel_id=1, source_target_pairs={{0,4},{4,0},{8,12},{12,8},{16,20},{20,16},{24,28},{28,24},{1,5},{5... | collective-permute-start | bytes 995336 | tf_op jit(solution)/shard_map/ppermute | solution.py:712
  163.0 21.7 %collective-permute-start.33 = (bf16[1,144,1152]{2,1,0:T(8,128)(2,1)}, bf16[1,144,1152]{2,1,0:T(8,128)(2,1)S(1)}, u32[]{:S(2)}, u32[]{:S(2)}) collective-permute-start(bf16[1,144,1152]{2,1,0:T(8,128)(2,1)} %copy-done.28), channel_id=1, source_target_pairs={{0,2},{1,3},{2,0},{3,1},{4,6},{5,7},{6,4},{7,5},{8,10},{9,11},{10,... | collective-permute-start | bytes 995336 | tf_op jit(solution)/shard_map/ppermute | solution.py:715
  164.1 21.3 %collective-permute-start.34 = (bf16[1,144,1152]{2,1,0:T(8,128)(2,1)}, bf16[1,144,1152]{2,1,0:T(8,128)(2,1)S(1)}, u32[]{:S(2)}, u32[]{:S(2)}) collective-permute-start(bf16[1,144,1152]{2,1,0:T(8,128)(2,1)} %collective-permute-done.13.refs_1_), channel_id=1, source_target_pairs={{0,4},{4,0},{8,12},{12,8},{16,20},{20,16},{24,28},{28,24},{1,5},{5... | collective-permute-start | bytes 995336 | tf_op jit(solution)/shard_map/ppermute | solution.py:712
  186.2 24.4 %collective-permute-start.40 = (bf16[1152,1152]{1,0:T(8,128)(2,1)}, bf16[1152,1152]{1,0:T(8,128)(2,1)}, u32[]{:S(2)}, u32[]{:S(2)}) collective-permute-start(bf16[1152,1152]{1,0:T(8,128)(2,1)} %convolution_convert_fusion.5), channel_id=1, source_target_pairs={{0,1},{1,0},{2,3},{3,2},{4,5},{5,4},{6,7},{7,6},{8,9},{9,8},{10,11... | collective-permute-start | bytes 7962632 | tf_op jit(solution)/shard_map/ppermute | solution.py:718
  188.2 22.4 %collective-permute-start.38 = (bf16[1,144,1152]{2,1,0:T(8,128)(2,1)}, bf16[1,144,1152]{2,1,0:T(8,128)(2,1)S(1)}, u32[]{:S(2)}, u32[]{:S(2)}) collective-permute-start(bf16[1,144,1152]{2,1,0:T(8,128)(2,1)} %collective-permute-done.35.refs_6_), channel_id=1, source_target_pairs={{0,2},{1,3},{2,0},{3,1},{4,6},{5,7},{6,4},{7,5},{8,10},{9,11},{10,... | collective-permute-start | bytes 995336 | tf_op jit(solution)/shard_map/ppermute | solution.py:715
  189.1 21.5 %collective-permute-start.39 = (bf16[1,144,1152]{2,1,0:T(8,128)(2,1)}, bf16[1,144,1152]{2,1,0:T(8,128)(2,1)S(1)}, u32[]{:S(2)}, u32[]{:S(2)}) collective-permute-start(bf16[1,144,1152]{2,1,0:T(8,128)(2,1)} %collective-permute-done.32.refs_3_), channel_id=1, source_target_pairs={{0,4},{4,0},{8,12},{12,8},{16,20},{20,16},{24,28},{28,24},{1,5},{5... | collective-permute-start | bytes 995336 | tf_op jit(solution)/shard_map/ppermute | solution.py:712
  214.2 23.3 %collective-permute-start.42 = (bf16[1152,1152]{1,0:T(8,128)(2,1)S(1)}, bf16[1152,1152]{1,0:T(8,128)(2,1)S(1)}, u32[]{:S(2)}, u32[]{:S(2)}) collective-permute-start(bf16[1152,1152]{1,0:T(8,128)(2,1)S(1)} %bitcast.174), channel_id=1, source_target_pairs={{0,1},{1,0},{2,3},{3,2},{4,5},{5,4},{6,7},{7,6},{8,9},{9,8},{10,11... | collective-permute-start | bytes 7962632 | tf_op jit(solution)/shard_map/ppermute | solution.py:718
  214.3 23.2 %collective-permute-start.45 = (bf16[1152,1152]{1,0:T(8,128)(2,1)S(1)}, bf16[1152,1152]{1,0:T(8,128)(2,1)S(1)}, u32[]{:S(2)}, u32[]{:S(2)}) collective-permute-start(bf16[1152,1152]{1,0:T(8,128)(2,1)S(1)} %convolution_convert_fusion.4), channel_id=1, source_target_pairs={{0,1},{1,0},{2,3},{3,2},{4,5},{5,4},{6,7},{7,6},{8,9},{9,8},{10,11... | collective-permute-start | bytes 7962632 | tf_op jit(solution)/shard_map/ppermute | solution.py:718
  256.1 19.8 %collective-permute-start.48 = (bf16[1152,1152]{1,0:T(8,128)(2,1)S(1)}, bf16[1152,1152]{1,0:T(8,128)(2,1)S(1)}, u32[]{:S(2)}, u32[]{:S(2)}) collective-permute-start(bf16[1152,1152]{1,0:T(8,128)(2,1)S(1)} %convolution_convert_fusion.3), channel_id=1, source_target_pairs={{0,1},{1,0},{2,3},{3,2},{4,5},{5,4},{6,7},{7,6},{8,9},{9,8},{10,11... | collective-permute-start | bytes 7962632 | tf_op jit(solution)/shard_map/ppermute | solution.py:718
  276.5 20.3 %collective-permute-start.50 = (bf16[1152,1152]{1,0:T(8,128)(2,1)S(1)}, bf16[1152,1152]{1,0:T(8,128)(2,1)}, u32[]{:S(2)}, u32[]{:S(2)}) collective-permute-start(bf16[1152,1152]{1,0:T(8,128)(2,1)S(1)} %convolution_convert_fusion.2), channel_id=1, source_target_pairs={{0,1},{1,0},{2,3},{3,2},{4,5},{5,4},{6,7},{7,6},{8,9},{9,8},{10,11... | collective-permute-start | bytes 7962632 | tf_op jit(solution)/shard_map/ppermute | solution.py:718
  322.1 26.7 %collective-permute-start.58 = (bf16[288,1152]{1,0:T(8,128)(2,1)S(1)}, bf16[288,1152]{1,0:T(8,128)(2,1)S(1)}, u32[]{:S(2)}, u32[]{:S(2)}) collective-permute-start(bf16[288,1152]{1,0:T(8,128)(2,1)S(1)} %add_convert_fusion.8), channel_id=1, source_target_pairs={{0,8},{4,12},{8,16},{12,20},{16,24},{20,28},{24,0},{28,4},{1,9},{5... | collective-permute-start | bytes 1990664 | tf_op jit(solution)/shard_map/ppermute | solution.py:706
  322.3 26.5 %collective-permute-start.56 = (bf16[288,1152]{1,0:T(8,128)(2,1)S(1)}, bf16[288,1152]{1,0:T(8,128)(2,1)S(1)}, u32[]{:S(2)}, u32[]{:S(2)}) collective-permute-start(bf16[288,1152]{1,0:T(8,128)(2,1)S(1)} %get-tuple-element.984), channel_id=1, source_target_pairs={{0,2},{1,3},{2,0},{3,1},{4,6},{5,7},{6,4},{7,5},{8,10},{9,11},{10,... | collective-permute-start | bytes 1990664 | tf_op jit(solution)/shard_map/ppermute | solution.py:715
  322.8 29.5 %collective-permute-start.57 = (bf16[288,1152]{1,0:T(8,128)(2,1)S(1)}, bf16[288,1152]{1,0:T(8,128)(2,1)S(1)}, u32[]{:S(2)}, u32[]{:S(2)}) collective-permute-start(bf16[288,1152]{1,0:T(8,128)(2,1)S(1)} %get-tuple-element.983), channel_id=1, source_target_pairs={{0,2},{1,3},{2,0},{3,1},{4,6},{5,7},{6,4},{7,5},{8,10},{9,11},{10,... | collective-permute-start | bytes 1990664 | tf_op jit(solution)/shard_map/ppermute | solution.py:715
  325.7 28.2 %collective-permute-start.55 = (bf16[288,1152]{1,0:T(8,128)(2,1)S(1)}, bf16[288,1152]{1,0:T(8,128)(2,1)S(1)}, u32[]{:S(2)}, u32[]{:S(2)}) collective-permute-start(bf16[288,1152]{1,0:T(8,128)(2,1)S(1)} %add_convert_fusion.9), channel_id=1, source_target_pairs={{0,8},{4,12},{8,16},{12,20},{16,24},{20,28},{24,0},{28,4},{1,9},{5... | collective-permute-start | bytes 1990664 | tf_op jit(solution)/shard_map/ppermute | solution.py:706
  353.8 25.7 %collective-permute-start.59 = (bf16[1152,1152]{1,0:T(8,128)(2,1)}, bf16[1152,1152]{1,0:T(8,128)(2,1)}, u32[]{:S(2)}, u32[]{:S(2)}) collective-permute-start(bf16[1152,1152]{1,0:T(8,128)(2,1)} %convolution_convert_fusion.1), channel_id=1, source_target_pairs={{0,1},{1,0},{2,3},{3,2},{4,5},{5,4},{6,7},{7,6},{8,9},{9,8},{10,11... | collective-permute-start | bytes 7962632 | tf_op jit(solution)/shard_map/ppermute | solution.py:718
  353.8 25.7 %collective-permute-start.60 = (bf16[1152,1152]{1,0:T(8,128)(2,1)}, bf16[1152,1152]{1,0:T(8,128)(2,1)}, u32[]{:S(2)}, u32[]{:S(2)}) collective-permute-start(bf16[1152,1152]{1,0:T(8,128)(2,1)} %convolution_convert_fusion), channel_id=1, source_target_pairs={{0,1},{1,0},{2,3},{3,2},{4,5},{5,4},{6,7},{7,6},{8,9},{9,8},{10,11... | collective-permute-start | bytes 7962632 | tf_op jit(solution)/shard_map/ppermute | solution.py:718
  355.4 24.1 %collective-permute-start.61 = (bf16[288,1152]{1,0:T(8,128)(2,1)}, bf16[288,1152]{1,0:T(8,128)(2,1)}, u32[]{:S(2)}, u32[]{:S(2)}) collective-permute-start(bf16[288,1152]{1,0:T(8,128)(2,1)} %add_convert_fusion.7), channel_id=1, source_target_pairs={{0,8},{4,12},{8,16},{12,20},{16,24},{20,28},{24,0},{28,4},{1,9},{5... | collective-permute-start | bytes 1990664 | tf_op jit(solution)/shard_map/ppermute | solution.py:706
  357.1 22.4 %collective-permute-start.62 = (bf16[288,1152]{1,0:T(8,128)(2,1)}, bf16[288,1152]{1,0:T(8,128)(2,1)}, u32[]{:S(2)}, u32[]{:S(2)}) collective-permute-start(bf16[288,1152]{1,0:T(8,128)(2,1)} %constant_dynamic-slice_fusion.8), channel_id=1, source_target_pairs={{0,2},{1,3},{2,0},{3,1},{4,6},{5,7},{6,4},{7,5},{8,10},{9,11},{10,... | collective-permute-start | bytes 1990664 | tf_op jit(solution)/shard_map/ppermute | solution.py:715
  359.4 20.1 %collective-permute-start.63 = (bf16[144,1152]{1,0:T(8,128)(2,1)}, bf16[144,1152]{1,0:T(8,128)(2,1)}, u32[]{:S(2)}, u32[]{:S(2)}) collective-permute-start(bf16[144,1152]{1,0:T(8,128)(2,1)} %constant_dynamic-slice_fusion.7), channel_id=1, source_target_pairs={{0,4},{4,0},{8,12},{12,8},{16,20},{20,16},{24,28},{28,24},{1,5},{5... | collective-permute-start | bytes 995336 | tf_op jit(solution)/shard_map/ppermute | solution.py:712
  404.0 21.0 %collective-permute-start.70 = (bf16[4,12672]{1,0:T(4,128)(2,1)S(1)}, bf16[4,12672]{1,0:T(4,128)(2,1)S(1)}, u32[]{:S(2)}, u32[]{:S(2)}) collective-permute-start(bf16[4,12672]{1,0:T(4,128)(2,1)S(1)} %pad_maximum_fusion.6), channel_id=1, source_target_pairs={{0,16},{4,20},{8,24},{12,28},{16,0},{20,4},{24,8},{28,12},{1,17},{... | collective-permute-start | bytes 304136 | tf_op jit(solution)/shard_map/ppermute | solution.py:806
  496.3 19.9 %collective-permute-start.85 = (bf16[144,1152]{1,0:T(8,128)(2,1)}, bf16[144,1152]{1,0:T(8,128)(2,1)S(1)}, u32[]{:S(2)}, u32[]{:S(2)}) collective-permute-start(bf16[144,1152]{1,0:T(8,128)(2,1)} %add_convert_fusion.19), channel_id=1, source_target_pairs={{0,2},{1,3},{2,0},{3,1},{4,6},{5,7},{6,4},{7,5},{8,10},{9,11},{10,... | collective-permute-start | bytes 995336 | tf_op jit(solution)/shard_map/ppermute | solution.py:715
  (173 other events, 1745.1 us)

commit v3 on v2

--- a/solution.py
+++ b/solution.py
@@ -123,6 +123,7 @@
     query_out,
     key_out,
     value_out,
+    sums_out,
     query_total,
     key_total,
     value_total,
@@ -145,9 +146,13 @@
         query_total[:, cut] += times(score_slope, key)
         key_total[:, cut] += inner_rows(score_slope, query)
         value_total[:, cut] += inner_rows(low(probs), slope)
-    query_out[...] = low(query_total[...] * score_scale)
+    query_slope = low(query_total[...] * score_scale)
+    query_out[...] = query_slope
+    sums_out[0, 0:1] = jnp.sum(query_slope.astype(jnp.float32), 0, keepdims=True)
     key_out[...] = low(key_total[...] * score_scale)
-    value_out[...] = low(value_total[...])
+    value_slope = low(value_total[...])
+    value_out[...] = value_slope
+    sums_out[0, 1:2] = jnp.sum(value_slope.astype(jnp.float32), 0, keepdims=True)
 
 
 def attend_back(queries, keys_all, values_all, slopes, patch_mask, logs):
@@ -157,13 +162,14 @@
     return pl.pallas_call(
         partial(attend_back_kernel, HEADS),
         grid=(slot_count,),
-        out_shape=[jax.ShapeDtypeStruct(queries.shape, jnp.bfloat16)] * 3,
+        out_shape=[jax.ShapeDtypeStruct(queries.shape, jnp.bfloat16)] * 3
+        + [jax.ShapeDtypeStruct((slot_count, 2, model_width), jnp.float32)],
         in_specs=[block] * 4
         + [
             pl.BlockSpec((1, 1, patch_count), lambda slot: (slot, 0, 0)),
             pl.BlockSpec((patch_count, HEADS), lambda slot: (slot, 0)),
         ],
-        out_specs=[block] * 3,
+        out_specs=[block] * 3 + [pl.BlockSpec((1, 2, model_width), lambda slot: (slot, 0, 0))],
         scratch_shapes=[pltpu.VMEM((patch_count, model_width), jnp.float32)] * 3,
         compiler_params=pltpu.CompilerParams(vmem_limit_bytes=32 << 20),
     )(queries, keys_all, values_all, slopes, patch_mask[:, None, :], logs)
@@ -184,9 +190,53 @@
     return jnp.sum(values, 0, keepdims=True)
 
 
+def fetch(sources, held_ref, sems, places=None):
+    copies = []
+    for index, source in enumerate(sources):
+        place = index if places is None else places[index]
+        copies.append(pltpu.make_async_copy(source, held_ref.at[place], sems.at[index]))
+    for copy in copies:
+        copy.start()
+    return copies
+
+
+def project_kernel(
+    order_ref, normed_ref, bias_ref, *refs
+):
+    units, outs, last_ref, held, sems = refs[:4], refs[4:7], refs[7], refs[8], refs[9]
+    for copy in fetch(units, held, sems, order_ref):
+        copy.wait()
+    copy = pltpu.make_async_copy(held.at[3], last_ref, sems.at[4])
+    copy.start()
+    for index, row in ((0, 0), (1, None), (2, 1)):
+        value = times(normed_ref[...], held[index])
+        if row is not None:
+            value = value + bias_ref[row : row + 1, :]
+        outs[index][...] = low(value)
+    copy.wait()
+
+
+def project(normed, units, order, bias):
+    rows, width = normed.shape
+    vmem = pl.BlockSpec(memory_space=pltpu.VMEM)
+    anywhere = pl.BlockSpec(memory_space=pl.ANY)
+    return pl.pallas_call(
+        project_kernel,
+        in_specs=[pl.BlockSpec(memory_space=pltpu.SMEM), vmem, vmem] + [anywhere] * 4,
+        out_specs=[vmem] * 3 + [anywhere],
+        out_shape=[jax.ShapeDtypeStruct((rows, width), jnp.bfloat16)] * 3
+        + [jax.ShapeDtypeStruct((width, width), jnp.bfloat16)],
+        scratch_shapes=[
+            pltpu.VMEM((4, width, width), jnp.bfloat16),
+            pltpu.SemaphoreType.DMA((5,)),
+        ],
+        compiler_params=pltpu.CompilerParams(vmem_limit_bytes=40 << 20),
+    )(jnp.stack(order).astype(jnp.int32), normed, bias, *units)
+
+
 def middle_kernel(attended_ref, weight_ref, bias_ref, hidden_ref, mod_ref, branch_ref, middle_ref, normed_ref):
     gate_one, shift_two, scale_two = [mod_ref[0, i : i + 1] for i in (2, 3, 4)]
-    branch = times(attended_ref[...], weight_ref[0]) + bias_ref[...]
+    branch = times(attended_ref[...], weight_ref[...]) + bias_ref[...]
     branch_ref[...] = branch
     middle = hidden_ref[...].astype(jnp.float32) + gate_one * branch
     middle_ref[...] = middle
@@ -221,16 +271,33 @@
     middle_slope = slope + norm_back(normed, inverse, back * (1.0 + scale_two))
     middle_slope_ref[...] = middle_slope
     slopes_ref[0, 0:1] = patch_sums(middle_slope * branch_ref[...])
-    branch_low_ref[...] = low(middle_slope * gate_one)
+    branch_low = low(middle_slope * gate_one)
+    branch_low_ref[...] = branch_low
+    slopes_ref[0, 4:5] = patch_sums(branch_low.astype(jnp.float32))
+    slopes_ref[0, 5:6] = patch_sums(low(slope * gate_two).astype(jnp.float32))
 
 
 def start_back_kernel(
-    query_ref, key_ref, value_ref, weight_ref, middle_slope_ref, hidden_ref, mod_ref, out_ref, slopes_ref
+    order_ref,
+    query_ref,
+    key_ref,
+    value_ref,
+    middle_slope_ref,
+    hidden_ref,
+    mod_ref,
+    *refs,
 ):
+    units, out_ref, slopes_ref, held, sems = refs[:4], refs[4], refs[5], refs[6], refs[7]
+
+    @pl.when(pl.program_id(0) == 0)
+    def _():
+        for copy in fetch(units, held, sems, order_ref):
+            copy.wait()
+
     scale_one = mod_ref[0, 1:2]
-    back = times_transposed(query_ref[...], weight_ref[0])
-    back += times_transposed(key_ref[...], weight_ref[1])
-    back += times_transposed(value_ref[...], weight_ref[2])
+    back = times_transposed(query_ref[...], held[0])
+    back += times_transposed(key_ref[...], held[1])
+    back += times_transposed(value_ref[...], held[2])
     normed, inverse = norm_parts(hidden_ref[...].astype(jnp.float32))
     slopes_ref[0, 0:1] = patch_sums(back)
     slopes_ref[0, 1:2] = patch_sums(back * normed)
@@ -328,6 +395,32 @@
     )(columns)
 
 
+def attend_out_kernel(order_ref, *refs):
+    units, attend_ref, output_ref, held = refs[:4], refs[4], refs[5], refs[6]
+    for index in range(4):
+        held[order_ref[index]] = units[index][...]
+    width = output_ref.shape[1]
+    for unit in range(3):
+        attend_ref[:, unit * width : (unit + 1) * width] = held[unit].astype(jnp.float32)
+    output_ref[...] = held[3].astype(jnp.float32)
+
+
+def attend_out(units, order):
+    rows, width = units[0].shape
+    vmem = pl.BlockSpec(memory_space=pltpu.VMEM)
+    return pl.pallas_call(
+        attend_out_kernel,
+        in_specs=[pl.BlockSpec(memory_space=pltpu.SMEM)] + [vmem] * 4,
+        out_specs=[vmem] * 2,
+        out_shape=[
+            jax.ShapeDtypeStruct((rows, 3 * width), jnp.float32),
+            jax.ShapeDtypeStruct((rows, width), jnp.float32),
+        ],
+        scratch_shapes=[pltpu.VMEM((4, rows, width), units[0].dtype)],
+        compiler_params=pltpu.CompilerParams(vmem_limit_bytes=32 << 20),
+    )(jnp.stack(order).astype(jnp.int32), *units)
+
+
 def spread_kernel(parts, order_ref, *refs):
     units, out_ref, held = refs[:4], refs[4], refs[5]
     for index in range(4):
@@ -384,14 +477,14 @@
         slope = self.cotangent.astype(jnp.float32) * self.live[:, None, None]
         return self.flat(low(slope * self.pieces(modulation)[5]))
 
-    def attention(self, normed_one, weights, attend_bias):
-        queries = low(times(normed_one, weights[0]) + attend_bias[0])
-        keys_all = low(times(normed_one, weights[1]))
-        values_all = low(times(normed_one, weights[2]) + attend_bias[1])
+    def attention(self, normed_one, units, order, attend_bias):
+        queries, keys_all, values_all, output_full = project(
+            normed_one, units, order, attend_bias
+        )
         attended, logs = attend(queries, keys_all, values_all, self.patch_mask)
-        return queries, keys_all, values_all, attended, logs
-
-    def per_image(self, kernel, outs, ins):
+        return queries, keys_all, values_all, output_full, attended, logs
+
+    def per_image(self, kernel, outs, ins, scratch=()):
         rows = pl.BlockSpec((self.patches, self.width), lambda slot: (slot, 0))
 
         def spec(kind, shape):
@@ -399,10 +492,10 @@
                 return rows
             if kind == "scalar":
                 return pl.BlockSpec(memory_space=pltpu.SMEM)
+            if kind == "any":
+                return pl.BlockSpec(memory_space=pl.ANY)
             if kind == "all":
                 return pl.BlockSpec(shape, lambda slot: (0,) * len(shape))
-            if isinstance(kind, tuple):
-                return pl.BlockSpec((kind[0],) + shape[1:], lambda slot: (kind[1], 0, 0))
             return pl.BlockSpec((1,) + shape[1:], lambda slot: (slot, 0, 0))
 
         shapes = [
@@ -414,19 +507,20 @@
             in_specs=[spec(kind, array.shape) for kind, array in ins],
             out_specs=[spec(kind, shape) for (kind, _), shape in zip(outs, shapes)],
             out_shape=[jax.ShapeDtypeStruct(shape, kind[1]) for kind, shape in zip(outs, shapes)],
+            scratch_shapes=list(scratch),
             compiler_params=pltpu.CompilerParams(vmem_limit_bytes=56 << 20),
         )(*[array for _, array in ins])
 
     def six(self, modulation):
         return "mod", modulation.reshape(self.slots, 6, self.width)
 
-    def middle(self, attended, weights, output_bias, modulation):
+    def middle(self, attended, output_full, output_bias, modulation):
         return self.per_image(
             middle_kernel,
             [("rows", jnp.float32), ("rows", jnp.float32), ("rows", jnp.bfloat16)],
             [
                 ("rows", attended),
-                ((1, 3), weights),
+                ("all", output_full),
                 ("all", output_bias),
                 ("rows", self.hidden),
                 self.six(modulation),
@@ -454,7 +548,7 @@
                 ("rows", jnp.bfloat16),
                 ("rows", jnp.float32),
                 ("rows", jnp.bfloat16),
-                (4, jnp.float32),
+                (6, jnp.float32),
             ],
             [
                 ("scalar", self.live),
@@ -472,20 +566,20 @@
     def attention_back(self, slopes, queries, keys_all, values_all, logs):
         return attend_back(queries, keys_all, values_all, slopes, self.patch_mask, logs)
 
-    def start_back(self, slopes, weights, middle_slope, modulation, later_slopes):
+    def start_back(self, slopes, units, order, middle_slope, modulation):
         gradient, first_slopes = self.per_image(
             start_back_kernel,
             [("rows", jnp.float32), (2, jnp.float32)],
-            [("rows", slope) for slope in slopes]
-            + [
-                ((3, 0), weights),
-                ("rows", middle_slope),
-                ("rows", self.hidden),
-                self.six(modulation),
+            [("scalar", jnp.stack(order).astype(jnp.int32))]
+            + [("rows", slope) for slope in slopes]
+            + [("rows", middle_slope), ("rows", self.hidden), self.six(modulation)]
+            + [("any", unit) for unit in units],
+            [
+                pltpu.VMEM((4, self.width, self.width), jnp.bfloat16),
+                pltpu.SemaphoreType.DMA((4,)),
             ],
         )
-        modulation_slope = low(jnp.concatenate([first_slopes, later_slopes], 1))
-        return gradient.reshape(self.hidden_in.shape), modulation_slope.reshape(self.slots, -1)
+        return gradient.reshape(self.hidden_in.shape), first_slopes
 
     def condition_back(self, slope):
         return jax.vjp(jax.nn.silu, self.condition.astype(jnp.float32))[1](slope)[0]
@@ -526,6 +620,33 @@
             for rows, columns in ((1, 6 * width), (2, width), (1, width), (4, width), (1, width))
         ],
     )(packed)
+
+
+def pack_slopes_kernel(order_ref, first_ref, later_ref, head_ref, condition_ref, *refs):
+    units, out_ref, held_ref = refs[:4], refs[4], refs[5]
+    for index, unit in enumerate(units):
+        held_ref[pl.ds(order_ref[index], 1), :] = unit[...]
+    slots, width = condition_ref.shape
+    sums = [head_ref[0, i : i + 1] + head_ref[1, i : i + 1] for i in range(2)]
+    sums += [later_ref[0, i : i + 1] + later_ref[1, i : i + 1] for i in (4, 5)]
+    for slot in range(slots):
+        parts = [first_ref[slot, i : i + 1] for i in range(2)]
+        parts += [later_ref[slot, i : i + 1] for i in range(4)]
+        parts += [condition_ref[slot : slot + 1, :].astype(jnp.float32)]
+        parts += sums if slot == 0 else [held_ref[i : i + 1, :] for i in range(4)]
+        out_ref[slot : slot + 1, :] = low(jnp.concatenate(parts, axis=1))
+
+
+def pack_slopes(order, first, later, heads, condition, units):
+    slots, width = condition.shape
+    vmem = pl.BlockSpec(memory_space=pltpu.VMEM)
+    return pl.pallas_call(
+        pack_slopes_kernel,
+        in_specs=[pl.BlockSpec(memory_space=pltpu.SMEM)] + [vmem] * 8,
+        out_specs=vmem,
+        out_shape=jax.ShapeDtypeStruct((slots, 11 * width), jnp.bfloat16),
+        scratch_shapes=[pltpu.VMEM((4, width), jnp.float32)],
+    )(jnp.stack(order).astype(jnp.int32), first, later, heads, condition, *units)
 
 
 def pack(condition, *biases):
@@ -590,12 +711,15 @@
     terms = times(act_rows(conditions, here, shard), modulation_weight)
     modulation = lax.psum_scatter(terms, "dp", scatter_dimension=0, tiled=True) + biases[0]
     weights = whole(jnp.concatenate([attend_weight, output_weight], 1))
-    weights = weights.reshape(width, 4, width).transpose(1, 0, 2)
+    weights = [weights[:, unit * width : (unit + 1) * width] for unit in range(4)]
+    natural = [jnp.int32(unit) for unit in range(4)]
     expand_full, shrink_full = whole(expand_weight), whole(shrink_weight)
     normed_one = layer.start(modulation)
     shrink_slope = layer.shrink_slope(modulation)
-    queries, keys_all, values_all, attended, logs = layer.attention(normed_one, weights, biases[1])
-    branch, middle, normed_two = layer.middle(attended, weights, biases[2], modulation)
+    queries, keys_all, values_all, output_full, attended, logs = layer.attention(
+        normed_one, weights, natural, biases[1]
+    )
+    branch, middle, normed_two = layer.middle(attended, output_full, biases[2], modulation)
     totals = ()
     expand_terms, shrink_terms, inner_sums = [], [], []
     for unit in range(4):
@@ -610,11 +734,14 @@
     layer_out, middle_slope, branch_low, later = layer.finish(
         middle, branch, *totals, biases[4], modulation
     )
-    attended_slope = low(times_transposed(branch_low, weights[3]))
-    slopes = layer.attention_back(attended_slope, queries, keys_all, values_all, logs)
-    gradient_hidden, mod_slope = layer.start_back(
-        slopes, weights, middle_slope, modulation, later
+    attended_slope = low(times_transposed(branch_low, output_full))
+    *slopes, head_sums = layer.attention_back(
+        attended_slope, queries, keys_all, values_all, logs
     )
+    gradient_hidden, first = layer.start_back(
+        slopes, weights, natural, middle_slope, modulation
+    )
+    mod_slope = low(jnp.concatenate([first, later[:, :4]], 1)).reshape(slots, -1)
     all_slopes = lax.all_gather(mod_slope, ("dp", "rep"), axis=0, tiled=True)
     all_conditions = lax.all_gather(condition, ("dp", "rep"), axis=0, tiled=True)
     mod_weight, mod_bias = modulation_tail(
@@ -623,8 +750,8 @@
     columns = lax.all_gather(times_transposed(all_slopes, modulation_weight), "dp")
     inner_sums = jnp.concatenate(inner_sums, 1).reshape(dp, 4, shard)
     inner_sums = inner_sums.transpose(1, 0, 2).reshape(4, width)
-    others = [column_sums(value) for value in (slopes[0], slopes[2], branch_low, shrink_slope)]
-    sums = lax.psum(jnp.concatenate([jnp.stack(others), inner_sums]), ("dp", "rep"))
+    sums = jnp.concatenate([jnp.sum(head_sums, 0), jnp.sum(later[:, 4:], 0), inner_sums])
+    sums = lax.psum(sums, ("dp", "rep"))
     att_bias, out_bias, exp_bias, shr_bias = bias_tail(sums, here, shard)
     return (
         layer_out,
@@ -665,12 +792,16 @@
             state.update(zip(outs, values))
             ends = position + 1 == len(ops) or ops[position + 1][0] > tick
             if ends:
-                names = sorted(name for name in state if last.get(name, -1) > tick)
-                kept = [name for name in results if name in state and name not in names]
-                final = {name: state[name] for name in kept}
+                names = sorted(
+                    name for name in state if last.get(name, -1) > tick or name in results
+                )
                 state = dict(zip(names, lax.optimization_barrier(tuple(state[n] for n in names))))
-                state.update(final)
         return [state[name] for name in results]
+
+
+class Names:
+    def __getattr__(self, name):
+        return name
 
 
 def ticked_device(
@@ -692,8 +823,9 @@
     shrink_bias,
     cotangent,
 ):
-    here = lax.axis_index("dp")
-    copy = lax.axis_index("rep")
+    n = Names()
+    here = lax.axis_index(n.dp)
+    copy = lax.axis_index(n.rep)
     depth = dp // 2
     z, x, y, core = here // 2, here % 2, copy // 2, copy % 2
     order = [(2 * core + y) ^ step for step in range(4)]
@@ -703,19 +835,19 @@
     at = ticks.at
 
     def up(value):
-        return lax.ppermute(value, "dp", [(i, (i + 2) % dp) for i in range(dp)])
+        return lax.ppermute(value, n.dp, [(i, (i + 2) % dp) for i in range(dp)])
 
     def jump(step, value):
-        return lax.ppermute(value, "dp", [(i, (i + 2 * step) % dp) for i in range(dp)])
+        return lax.ppermute(value, n.dp, [(i, (i + 2 * step) % dp) for i in range(dp)])
 
     def swap_x(value):
-        return lax.ppermute(value, "dp", [(i, i ^ 1) for i in range(dp)])
+        return lax.ppermute(value, n.dp, [(i, i ^ 1) for i in range(dp)])
 
     def swap_y(value):
-        return lax.ppermute(value, "rep", [(i, i ^ 2) for i in range(4)])
+        return lax.ppermute(value, n.rep, [(i, i ^ 2) for i in range(4)])
 
     def swap_core(value):
-        return lax.ppermute(value, "rep", [(i, i ^ 1) for i in range(4)])
+        return lax.ppermute(value, n.rep, [(i, i ^ 1) for i in range(4)])
 
     def pair(one, two):
         return jnp.concatenate([one, two])
@@ -737,29 +869,31 @@
     def pick(stacked, index):
         return lax.dynamic_slice_in_dim(stacked, index, 1, 0)
 
-    at(0, "A0", (), lambda: attend_block(order[0]))
-    at(0, "a0", (), lambda: attend_block(order[1]))
-    at(0, "Bs", (), lambda: regroup(expand_weight, dp))
-    at(0, "P0", "Bs", lambda s: pick(s, order[1]))
-    at(0, "C0", (), lambda: shrink_block(order[0]))
-    at(0, "c0", (), lambda: shrink_block(order[1]))
-
-    at(0, "AB0", ("A0", "Bs"), lambda p, q: pair(p, pick(q, order[0])))
+    at(0, n.A0, (), lambda: attend_block(order[0]))
+    at(0, n.a0, (), lambda: attend_block(order[1]))
+    at(0, n.Bs, (), lambda: regroup(expand_weight, dp))
+    at(0, n.P0, n.Bs, lambda s: pick(s, order[1]))
+    at(0, n.C0, (), lambda: shrink_block(order[0]))
+    at(0, n.c0, (), lambda: shrink_block(order[1]))
+
+    at(0, n.AB0, (n.A0, n.Bs), lambda p, q: pair(p, pick(q, order[0])))
     for name, ring_ticks, x_ticks in (
-        ("AB", (0, 1, 2), (0, 1, 2, 3)),
-        ("P", (3, 4, 5), (4, 5, 6, 6)),
-        ("C", (3, 6, 7), (6, 7, 7, 8)),
+        (n.AB, (0, 1, 2), (0, 1, 2, 3)),
+        (n.P, (3, 4, 5), (4, 5)),
+        (n.C, (3, 6, 7), (6, 7, 7, 8)),
     ):
         for step, tick in enumerate(ring_ticks):
-            at(tick, f"{name}{step + 1}", f"{name}{step}", up)
+            at(tick, (str(name) + str(step + 1)), (str(name) + str(step)), up)
         for step, tick in enumerate(x_ticks):
-            at(tick, f"{name}x{step}", f"{name}{step}", swap_x)
-    for step, tick in enumerate((1, 2, 3)):
-        at(tick, f"ABy{step}", (f"ABx{step}", f"AB{step + 1}"),
+            at(tick, (str(name) + n.x + str(step)), (str(name) + str(step)), swap_x)
+    for step in range(3):
+        at(step + 1, (n.ABy + str(step)), ((n.ABx + str(step)), (n.AB + str(step + 1))),
            lambda p, q: swap_y(pair_rows(p, 0, q, 0)))
-    at(4, "ABy3", "ABx3", lambda p: swap_y(p[:1]))
-    for name, tick in (("C1", 5), ("Cx0", 7), ("Cx1", 8), ("C2", 8), ("Cx2", 8), ("C3", 9), ("Cx3", 9)):
-        at(tick, f"{name}y", name, swap_y)
+    at(4, n.ABy3, n.ABx3, lambda p: swap_y(p[:1]))
+    at(6, n.Px23, (n.P2, n.P3), lambda p, q: swap_x(pair(p, q)))
+    at(6, n.C1y, n.C1, swap_y)
+    for tick, one, two in ((7, n.Cx0, n.C2), (8, n.Cx1, n.C3), (9, n.Cx2, n.Cx3)):
+        at(tick, one + two, (one, two), lambda p, q: swap_y(pair(p, q)))
 
     def spot(step, cross):
         return 2 * below(step) + (1 - x if cross else x)
@@ -783,34 +917,41 @@
             [(local, 0)] + [(part, 1) for part in parts[:3]], [(part, 0) for part in parts]
         )
 
-    def steps(name, ending=""):
-        zs = tuple(f"{name}{step}{ending}" for step in range(4))
-        return zs, tuple(f"{name}x{step}{ending}" for step in range(4))
+    def other_late(local, one, two, three, four):
+        return streamed(
+            [(local, 0), (one, 0), (two, 1), (three, 1)], [(two, 0), (three, 0), (four, 0), (four, 1)]
+        )
+
+    def pair_unit(*parts):
+        return streamed(
+            [(part, 0) for part in parts[:4]], [(parts[4], 0), (parts[5], 0), (parts[6], 0), (parts[6], 1)]
+        )
 
     for name, stream, row, tick in (
-        ("Aown", "AB", 0, 4), ("Bown", "AB", 1, 5), ("By", "P", 0, 7), ("Cown", "C", 0, 9)
+        (n.Aown, n.AB, 0, 5), (n.Bown, n.AB, 1, 6), (n.Cown, n.C, 0, 9)
     ):
-        zs, xs = steps(stream)
-        at(tick, name, zs + xs, partial(own_unit, row))
-    at(5, "Ay", ("a0",) + tuple(f"ABy{step}" for step in range(4)), other_unit)
-    zs, xs = steps("C", "y")
-    at(10, "Cy", ("c0",) + zs[1:] + xs, partial(own_unit, 0))
-    at(4, "Ac", "Aown", swap_core)
-    at(5, "Acy", "Ay", swap_core)
-    at(6, "Bc", "Bown", swap_core)
-    at(7, "Bcy", "By", swap_core)
-    at(9, "Cc", "Cown", swap_core)
-    at(10, "Ccy", "Cy", swap_core)
+        parts = tuple((str(stream) + str(step)) for step in range(4))
+        parts += tuple((str(stream) + n.x + str(step)) for step in range(4))
+        at(tick, name, parts, partial(own_unit, row))
+    at(5, n.Ay, (n.a0,) + tuple((n.ABy + str(step)) for step in range(4)), other_unit)
+    at(7, n.By, (n.P0, n.P1, n.P2, n.P3, n.Px0, n.Px1, n.Px23), pair_unit)
+    at(10, n.Cy, (n.c0, n.C1y, n.Cx0C2, n.Cx1C3, n.Cx2Cx3), other_late)
+    at(5, n.Ac, n.Aown, swap_core)
+    at(5, n.Acy, n.Ay, swap_core)
+    at(6, n.Bc, n.Bown, swap_core)
+    at(7, n.Bcy, n.By, swap_core)
+    at(9, n.Cc, n.Cown, swap_core)
+    at(10, n.Ccy, n.Cy, swap_core)
 
     def swap_z(distance, value):
-        return lax.ppermute(value, "dp", [(i, i ^ (2 * distance)) for i in range(dp)])
+        return lax.ppermute(value, n.dp, [(i, i ^ (2 * distance)) for i in range(dp)])
 
     bits = {
-        "core": (core, swap_core),
-        "y": (y, swap_y),
-        "x": (x, swap_x),
-        "near": (z % 2, partial(swap_z, 1)),
-        "far": (z // 2, partial(swap_z, 2)),
+        n.core: (core, swap_core),
+        n.y: (y, swap_y),
+        n.x: (x, swap_x),
+        n.near: (z % 2, partial(swap_z, 1)),
+        n.far: (z // 2, partial(swap_z, 2)),
     }
 
     def grow(tick, name, axes):
@@ -820,8 +961,8 @@
             def join(mine, other, bit=bit):
                 return jnp.where(bit == 0, pair(mine, other), pair(other, mine))
 
-            at(tick, name + "_in", name, swap)
-            at(tick, name + "+", (name, name + "_in"), join)
+            at(tick, name + n._in, name, swap)
+            at(tick, name + "+", (name, name + n._in), join)
             name += "+"
         return name
 
@@ -837,17 +978,17 @@
                 half = terms.shape[0] // 2
                 return lax.dynamic_slice_in_dim(terms, bit * half, half, 0) + other
 
-            at(tick, name + "_in", name, send)
-            at(tick, name + "-", (name, name + "_in"), keep)
+            at(tick, name + n._in, name, send)
+            at(tick, name + "-", (name, name + n._in), keep)
             name += "-"
         return name
 
-    at(0, "small", (), lambda: pack(
+    at(0, n.small, (), lambda: pack(
         condition, modulation_bias, attend_bias, output_bias, expand_bias, shrink_bias))
-    small = grow(0, "small", ("x",))
-    small = grow(1, small, ("near",))
-    small = grow(2, small, ("far",))
-    at(3, ("mod_bias", "att_bias", "out_bias", "exp_bias", "shr_bias"), small,
+    small = grow(0, n.small, (n.x,))
+    small = grow(1, small, (n.near,))
+    small = grow(2, small, (n.far,))
+    at(3, (n.mod_bias, n.att_bias, n.out_bias, n.exp_bias, n.shr_bias), small,
        lambda packed: unpack(packed, shard))
 
     def first_terms(packed):
@@ -855,20 +996,18 @@
         conditions = conditions.transpose(2, 1, 0, 3, 4).reshape(-1, width)
         return times(act_rows(conditions, here, shard), modulation_weight)
 
-    at(2, "terms", small, first_terms)
-    terms = shrink_terms(3, "terms", ("x",))
-    terms = shrink_terms(4, terms, ("near",))
-    terms = shrink_terms(5, terms, ("far",))
-    at(6, "mod", (f"{terms}", "mod_bias"), lambda terms, bias: terms + bias)
-    at(6, "n1", "mod", layer.start)
-    at(6, "gm", "mod", layer.shrink_slope)
-
-    def natural(*units):
-        return reorder(units, order, 8)
-
-    at(6, "W", ("Aown", "Ay", "Ac", "Acy"), natural)
-    at(6, ("q", "k", "v", "att", "logs"), ("n1", "W", "att_bias"), lambda n1, w, bias: layer.attention(n1, w, bias))
-    at(7, ("branch", "middle", "n2"), ("att", "W", "out_bias", "mod"), layer.middle)
+    at(2, n.terms, small, first_terms)
+    terms = shrink_terms(3, n.terms, (n.x,))
+    terms = shrink_terms(4, terms, (n.near,))
+    terms = shrink_terms(5, terms, (n.far,))
+    at(6, n.mod, (str(terms), n.mod_bias), lambda terms, bias: terms + bias)
+    at(6, n.n1, n.mod, layer.start)
+    at(6, n.gm, n.mod, layer.shrink_slope)
+
+    units_a = (n.Aown, n.Ay, n.Ac, n.Acy)
+    at(6, (n.q, n.k, n.v, n.O, n.att, n.logs), (n.n1, n.att_bias) + units_a,
+       lambda n1, bias, *units: layer.attention(n1, units, order, bias))
+    at(7, (n.branch, n.middle, n.n2), (n.att, n.O, n.out_bias, n.mod), layer.middle)
 
     def expand(index, n2, weight, biases):
         return layer.expand(n2, weight, biases, order[index])
@@ -879,126 +1018,124 @@
             total = total + value.astype(jnp.float32)
         return low(total)
 
-    for index, (name, tick) in enumerate((("own", 7), ("y", 8), ("c", 7), ("cy", 8))):
-        at(tick, (f"in_{name}", f"act_{name}"), ("n2", f"B{name}", "exp_bias"), partial(expand, index))
-    at(7, "dC_c", ("act_c", "gm"), term)
-    at(8, "dC_cy", ("act_cy", "gm"), term)
-    at(9, "dC_own", ("act_own", "gm", "dC_rc"), term)
-    at(10, "dC_y", ("act_y", "gm", "dC_rcy"), term)
+    for index, (name, tick) in enumerate(((n.own, 7), (n.y, 8), (n.c, 7), (n.cy, 8))):
+        at(tick, ((n.in_ + str(name)), (n.act_ + str(name))), (n.n2, (n.B + str(name)), n.exp_bias), partial(expand, index))
+    at(7, n.dC_c, (n.act_c, n.gm), term)
+    at(8, n.dC_cy, (n.act_cy, n.gm), term)
+    at(9, n.dC_own, (n.act_own, n.gm, n.dC_rc), term)
+    at(10, n.dC_y, (n.act_y, n.gm, n.dC_rcy), term)
 
     total = ()
-    for index, (name, tick) in enumerate((("own", 9), ("c", 10), ("cy", 11), ("y", 12))):
-        ins = (f"in_{name}", f"act_{name}", "gm", f"B{name}", f"C{name}") + total
-        total = (f"out{index}", f"back{index}")
-        at(tick, (f"gi_{name}", f"sum_{name}") + total, ins, layer.shrink)
-    at(10, "dB_c", ("n2", "gi_c"), term)
-    at(11, "dB_cy", ("n2", "gi_cy"), term)
-    at(12, "dB_own", ("n2", "gi_own", "dB_rc"), term)
-    at(13, "dB_y", ("n2", "gi_y", "dB_rcy"), term)
-
-    at(13, ("layer_out", "middle_slope", "branch_low", "later"),
-       ("middle", "branch", "out3", "back3", "shr_bias", "mod"), layer.finish)
-    at(13, "g_att", ("branch_low", "W"), lambda b, w: low(times_transposed(b, w[3])))
-    at(14, ("gq", "gk", "gv"), ("g_att", "q", "k", "v", "logs"), layer.attention_back)
-    at(15, ("gradient_hidden", "mod_slope"), ("gq", "gk", "gv", "W", "middle_slope", "mod", "later"),
-       lambda a, b, c, w, ms, mod, later: layer.start_back((a, b, c), w, ms, mod, later))
-
+    for index, (name, tick) in enumerate(((n.own, 9), (n.c, 10), (n.cy, 11), (n.y, 12))):
+        ins = ((n.in_ + str(name)), (n.act_ + str(name)), n.gm, (n.B + str(name)), (n.C + str(name))) + total
+        total = ((n.out + str(index)), (n.back + str(index)))
+        at(tick, ((n.gi_ + str(name)), (n.sum_ + str(name))) + total, ins, layer.shrink)
+    at(10, n.dB_c, (n.n2, n.gi_c), term)
+    at(11, n.dB_cy, (n.n2, n.gi_cy), term)
+    at(12, n.dB_own, (n.n2, n.gi_own, n.dB_rc), term)
+    at(13, n.dB_y, (n.n2, n.gi_y, n.dB_rcy), term)
+
+    at(13, (n.layer_out, n.middle_slope, n.branch_low, n.later),
+       (n.middle, n.branch, n.out3, n.back3, n.shr_bias, n.mod), layer.finish)
+    at(13, n.g_att, (n.branch_low, n.O), lambda b, w: low(times_transposed(b, w)))
+    at(14, (n.gq, n.gk, n.gv, n.head_sums), (n.g_att, n.q, n.k, n.v, n.logs), layer.attention_back)
     def attend_term(index, n1, att, gq, gk, gv, branch_low, *received):
         which = order[index]
         right = lax.select_n(which, gq, gk, gv, branch_low)
         return term(jnp.where(which == 3, att, n1), right, *received)
 
     for index, (name, tick, received) in enumerate(
-        (("own", 16, ("dA_rc",)), ("y", 16, ("dA_rcy",)), ("c", 14, ()), ("cy", 14, ()))
+        ((n.own, 15, ()), (n.y, 15, ()), (n.c, 14, ()), (n.cy, 14, ()))
     ):
-        ins = ("n1", "att", "gq", "gk", "gv", "branch_low") + received
-        at(tick, f"dA_{name}", ins, partial(attend_term, index))
-
-    def slab(step, moved, whole, *parts):
-        cut = lax.dynamic_slice_in_dim(whole, below(step) * (2 * shard), 2 * shard, 0)
-        if parts:
-            cut = low(sum(value.astype(jnp.float32) for value in (cut,) + parts))
-        return moved(cut)
+        ins = (n.n1, n.att, n.gq, n.gk, n.gv, n.branch_low) + received
+        at(tick, (n.dA_ + str(name)), ins, partial(attend_term, index))
+
+    at(16, (n.gradient_hidden, n.first), (n.gq, n.gk, n.gv, n.middle_slope, n.mod) + units_a,
+       lambda a, b, c, ms, mod, *units: layer.start_back((a, b, c), units, order, ms, mod))
+
+    def slab(step, moved, count, *values):
+        first = below(step) * (2 * shard)
+        cuts = [lax.dynamic_slice_in_dim(value, first, 2 * shard, 0) for value in values[:count]]
+        cuts += values[count:]
+        if len(cuts) == 1:
+            return moved(cuts[0])
+        return moved(low(sum(value.astype(jnp.float32) for value in cuts)))
 
     def stay(value):
         return value
 
-    def along_ring(name, start, source, added):
+    def along_ring(name, start, source, added, rest=0):
         for step in range(1, 5):
-            ins = (source,) + tuple(f"{part}{step}" for part in added)
+            ins = source + tuple((str(part) + str(step)) for part in added)
             if step > 1:
-                ins += (f"{name}{step - 1}",)
-            at(start + step - 1, f"{name}{step}", ins, partial(slab, step, up if step < 4 else stay))
-        at(start + 3, f"{name}_in", f"{name}4", lambda total: swap_x(
+                ins += ((str(name) + str(step - 1)),)
+            at(start + step - 1, (str(name) + str(step)), ins, partial(slab, step, up if step < 4 else stay, len(source)))
+        at(start + 3 + rest, (str(name) + n._in), (str(name) + str(4)), lambda total: swap_x(
             lax.dynamic_slice_in_dim(total, (1 - x) * shard, shard, 0)))
-        at(start + 4, f"{name}_sum", (f"{name}4", f"{name}_in"), lambda total, other: low(
+        at(start + 4 + rest, (str(name) + n._sum), ((str(name) + str(4)), (str(name) + n._in)), lambda total, other: low(
             lax.dynamic_slice_in_dim(total, x * shard, shard, 0).astype(jnp.float32)
             + other.astype(jnp.float32)))
-        return f"{name}_sum"
+        return (str(name) + n._sum)
 
     def wide(name, start_own, start_other, late):
-        one = along_ring(f"{name}_o", start_own, f"{name}_own", ())
-        two = along_ring(f"{name}_p", start_other, f"{name}_y", ())
-        at(late, f"{name}_yo", two, swap_y)
-        at(late, f"{name}_yp", one, swap_y)
-        at(late + 1, f"{name}_0", (one, f"{name}_yo"), add)
-        at(late + 1, f"{name}_1", (two, f"{name}_yp"), add)
-        at(late + 1, f"{name}_2", f"{name}_0", swap_core)
-        at(late + 1, f"{name}_3", f"{name}_1", swap_core)
+        one = along_ring((str(name) + n._o), start_own, ((str(name) + n._own),), ())
+        two = along_ring((str(name) + n._p), start_other, ((str(name) + n._y),), ())
+        at(late, (str(name) + n._yo), two, swap_y)
+        at(late, (str(name) + n._yp), one, swap_y)
+        at(late + 1, (str(name) + n._0), (one, (str(name) + n._yo)), add)
+        at(late + 1, (str(name) + n._1), (two, (str(name) + n._yp)), add)
+        at(late + 1, (str(name) + n._2), (str(name) + n._0), swap_core)
+        at(late + 1, (str(name) + n._3), (str(name) + n._1), swap_core)
         return late + 2
 
-    def halved(name, y_ticks, start_ring, late):
+    def halved(name, cut_ticks, y_ticks, start_ring, late, received=(), rest=0):
         for step, tick in enumerate(y_ticks, 1):
-            at(tick, f"{name}_s{step}", f"{name}_y", partial(slab, step, swap_y))
-        one = along_ring(f"{name}_o", start_ring, f"{name}_own", (f"{name}_s",))
-        at(late, f"{name}_0", one, stay)
-        at(late, f"{name}_1", one, swap_y)
-        at(late + 1, f"{name}_2", one, swap_core)
-        at(late + 1, f"{name}_3", f"{name}_1", swap_core)
+            ins = ((str(name) + n._y),) + tuple((str(name) + n._ + str(part) + n.y) for part in received)
+            at(cut_ticks[step - 1], (str(name) + n._t + str(step)), ins, partial(slab, step, stay, len(ins)))
+            at(tick, (str(name) + n._s + str(step)), (str(name) + n._t + str(step)), swap_y)
+        own = ((str(name) + n._own),) + tuple((str(name) + n._ + str(part)) for part in received)
+        one = along_ring((str(name) + n._o), start_ring, own, ((str(name) + n._s),), rest)
+        at(late, (str(name) + n._0), one, stay)
+        at(late, (str(name) + n._1), one, swap_y)
+        at(late + 1, (str(name) + n._2), one, swap_core)
+        at(late + 1, (str(name) + n._3), (str(name) + n._1), swap_core)
         return late + 2
 
-    for name, tick_one, tick_two in (("dC", 8, 9), ("dB", 11, 12), ("dA", 15, 15)):
-        at(tick_one, f"{name}_rc", f"{name}_c", swap_core)
-        at(tick_two, f"{name}_rcy", f"{name}_cy", swap_core)
-    end_c = wide("dC", 9, 12, 21)
-    end_b = halved("dB", (13, 14, 14, 15), 14, 20)
-    end_a = halved("dA", (16, 17, 18, 19), 17, 21)
-
-    def attend_out(*units):
-        whole = jnp.zeros((4,) + units[0].shape, units[0].dtype)
-        for index, value in zip(order, units):
-            whole = lax.dynamic_update_slice(whole, value[None], (index, 0, 0))
-        whole = whole.astype(jnp.float32)
-        return jnp.concatenate([whole[0], whole[1], whole[2]], 1), whole[3]
+    for name, tick_one, tick_two in ((n.dC, 8, 9), (n.dB, 11, 12), (n.dA, 15, 15)):
+        at(tick_one, (str(name) + n._rc), (str(name) + n._c), swap_core)
+        at(tick_two, (str(name) + n._rcy), (str(name) + n._cy), swap_core)
+    end_c = wide(n.dC, 9, 12, 20)
+    end_b = halved(n.dB, (13, 14, 14, 15), (13, 14, 14, 15), 14, 20, rest=1)
+    end_a = halved(n.dA, (16, 17, 18, 19), (16, 17, 18, 19), 17, 21, (n.rc,))
 
     def shrink_out(*units):
         whole = assemble([(unit[None], 0) for unit in units], order, 4)
         return whole.reshape(-1, width).astype(jnp.float32)
 
     def four(name):
-        return tuple(f"{name}_{i}" for i in range(4))
-
-    at(end_c, "shr_weight", four("dC"), shrink_out)
-    at(end_b, "exp_weight", four("dB"), lambda *units: spread(units, order, dp))
-    at(end_a, ("att_weight", "out_weight"), four("dA"), attend_out)
+        return tuple((str(name) + n._ + str(i)) for i in range(4))
+
+    at(end_c, n.shr_weight, four(n.dC), shrink_out)
+    at(end_b, n.exp_weight, four(n.dB), lambda *units: spread(units, order, dp))
+    at(end_a, (n.att_weight, n.out_weight), four(n.dA), lambda *units: attend_out(units, order))
 
     def join(tick, name, axis):
-        at(tick, name + "_in", name, bits[axis][1])
-        at(tick, name + "+", (name, name + "_in"), pair)
+        at(tick, name + n._in, name, bits[axis][1])
+        at(tick, name + "+", (name, name + n._in), pair)
         return name + "+"
 
     mod_size = 6 * width
-    def bias_terms(gq, gv, branch_low, gm, *sums):
-        unit_sums = jnp.zeros((4, width), jnp.float32)
-        for index, value in zip(order, sums):
-            unit_sums = lax.dynamic_update_slice(unit_sums, value, (index, 0))
-        others = jnp.stack([column_sums(value) for value in (gq, gv, branch_low, gm)])
-        return low(pair(others, unit_sums)).reshape(slots, -1)
-
-    at(15, "sums", ("gq", "gv", "branch_low", "gm", "sum_own", "sum_y", "sum_c", "sum_cy"), bias_terms)
-    at(16, "sent", ("mod_slope", "sums"), lambda m, sums: jnp.concatenate([m, condition, sums], 1))
-    sent = "sent"
-    for tick, axis in ((16, "y"), (17, "far"), (18, "near"), (19, "x"), (19, "core")):
+    at(16, n.sent, (n.first, n.later, n.head_sums, n.sum_own, n.sum_y, n.sum_c, n.sum_cy),
+       lambda first, later, heads, *units: pack_slopes(
+           order, first, later, heads, condition, units))
+    sent = n.sent
+    both_ways = [(4 * i + j, 4 * (i ^ 4) + (j ^ 2)) for i in range(dp) for j in range(4)]
+    at(17, n.sent_far, sent, partial(swap_z, 2))
+    at(17, n.sent_y, sent, swap_y)
+    at(17, n.sent_both, sent, lambda rows: lax.ppermute(rows, (n.dp, n.rep), both_ways))
+    at(17, n.rows, (sent, n.sent_far, n.sent_y, n.sent_both), lambda *rows: jnp.concatenate(rows))
+    sent = n.rows
+    for tick, axis in ((18, n.near), (19, n.x), (20, n.core)):
         sent = join(tick, sent, axis)
 
     def modulation_terms(sent):
@@ -1011,45 +1148,41 @@
         sums = times(picked, sent[:, mod_size + width :]).reshape(-1, width)
         return (weight, bias) + bias_tail(sums, here, shard)
 
-    at(20, "columns", sent, lambda sent: times_transposed(sent[:, :mod_size], modulation_weight))
-    at(20, ("mod_weight", "mod_bias_out", "att_bias_out", "out_bias_out", "exp_bias_out", "shr_bias_out"),
+    at(20, n.columns, sent, lambda sent: times_transposed(sent[:, :mod_size], modulation_weight))
+    at(20, (n.mod_weight, n.mod_bias_out, n.att_bias_out, n.out_bias_out, n.exp_bias_out, n.shr_bias_out),
        sent, modulation_terms)
 
-    def trade(tick, name, axis, swap):
-        at(tick, name + "_in", name, lambda held: swap(jnp.split(held, 2, axis)[1]))
-        at(tick, name + "+", (name, name + "_in"), lambda held, got: jnp.stack(
-            [jnp.split(held, 2, axis)[0], got]))
-        return name + "+"
-
-    at(20, "traded", "columns", lambda columns: columns.reshape(
-        2, 2, 2, 2, 2, slots, shard)[0, :, :, :, 0])
-    traded = trade(20, "traded", 0, swap_x)
-    traded = trade(21, traded, 2, partial(swap_z, 1))
-    traded = trade(22, traded, 4, partial(swap_z, 2))
-
-    def condition_slope(held):
-        for axis, bit in enumerate((z // 2, z % 2, x)):
+    at(20, n.traded, n.columns, lambda columns: columns.reshape(
+        2, 2, 2, 2, 2, slots, shard)[0, :, :, 0])
+    at(20, n.traded_x, n.traded, lambda held: swap_x(held[1]))
+    at(21, n.held, (n.traded, n.traded_x), lambda held, got: jnp.stack([held[0], got]))
+    for step in (1, 2, 3):
+        at(21, (n.held + str(step)), n.held, lambda held, step=step: swap_z(step, held[:, step % 2, step // 2]))
+
+    def condition_slope(held, near, far, both):
+        held = jnp.stack([held[:, 0, 0], far, near, both]).reshape(2, 2, 2, slots, shard)
+        for axis, bit in enumerate((z % 2, z // 2, x)):
             held = jnp.where(bit == 1, jnp.flip(held, axis), held)
-        held = held.reshape(dp, slots, shard).transpose(1, 0, 2)
+        held = held.transpose(3, 1, 0, 2, 4)
         return layer.condition_back(held.reshape(slots, width))
 
-    at(23, "gradient_condition", traded, condition_slope)
+    at(22, n.gradient_condition, (n.held, n.held1, n.held2, n.held3), condition_slope)
     return tuple(
         ticks.run(
             [
-                "layer_out",
-                "gradient_hidden",
-                "gradient_condition",
-                "mod_weight",
-                "mod_bias_out",
-                "att_weight",
-                "att_bias_out",
-                "out_weight",
-                "out_bias_out",
-                "exp_weight",
-                "exp_bias_out",
-                "shr_weight",
-                "shr_bias_out",
+                n.layer_out,
+                n.gradient_hidden,
+                n.gradient_condition,
+                n.mod_weight,
+                n.mod_bias_out,
+                n.att_weight,
+                n.att_bias_out,
+                n.out_weight,
+                n.out_bias_out,
+                n.exp_weight,
+                n.exp_bias_out,
+                n.shr_weight,
+                n.shr_bias_out,
             ]
         )
     )

time: 536 us -> 523 us (0.976)
  waiting for transfers between devices: 185 us -> 168 us
  Pallas kernels: 69.2 us -> 83.4 us
  starting transfers between devices: 76.5 us -> 86.7 us
  local copies, waits for them, and re-layouts: 41 us -> 31.5 us
  other arithmetic: 50.8 us -> 44.9 us
    ppermute x92 -> x90, waiting for transfers between devices: 185 us -> 168 us  [the longest x21 54.5 us: swap_y(): return lax.ppermute(value, n.rep, [(i, i ^ 2) for i in range(4)])]
    ppermute x92 -> x90, starting transfers between devices: 76.5 us -> 86.7 us  [the longest x21 26.6 us: up(): return lax.ppermute(value, n.dp, [(i, (i + 2) % dp) for i in range(dp)])]
    pallas_call x1 -> x3, Pallas kernels: 5.7 us -> 14.4 us  [the longest x1 10.1 us: project(): pl.pallas_call(project_kernel, in_specs=[pl.BlockSpec(memory_space=pltpu....]
    unnamed x230 -> x190, local copies, waits for them, and re-layouts: 17.4 us -> 10.5 us
    dot_general x13, matrix products: 39.2 us -> 33.6 us  [inner_rows(): lax.dot_general(left_side, right_side, (((0,), (0,)), ((), ())), preferre...]
    reduce_sum x9 -> x5, other arithmetic: 11.9 us -> 8.37 us  [column_sums(): return jnp.sum(values, 0, dtype=jnp.float32)]
    dot_general x13 -> x10, matrix products: 35.8 us -> 34.4 us  [times(): return jnp.dot(left_side, right_side, preferred_element_type=jnp.float32)]
    convert_element_type x22 -> x26, other arithmetic: 21 us -> 19.8 us  [low(): return values.astype(jnp.bfloat16)]
  transfers between devices with their start and end apart: 92 -> 90, of which waited for: 35 -> 32; matrix products, arithmetic and copies ran while one was open for 30% -> 29% of each run, Pallas kernels for 11% -> 14%
where the time goes in v3:
time: 523 us; the launch traced here: 517 us
  waiting for transfers between devices  168 us (32%)
  matrix products  99 us (19%)
  starting transfers between devices  86.7 us (17%)
  Pallas kernels  83.4 us (16%)
  other arithmetic  44.9 us (9%)
  local copies, waits for them, and re-layouts  31.5 us (6%)
    ppermute x21, waiting for transfers between devices, swap_y(): return lax.ppermute(value, n.rep, [(i, i ^ 2) for i in range(4)])  54.5 us
    ppermute x9, waiting for transfers between devices, swap_z(): return lax.ppermute(value, n.dp, [(i, i ^ 2 * distance) for i in range(dp)])  44.1 us
    ppermute x21, waiting for transfers between devices, up(): return lax.ppermute(value, n.dp, [(i, (i + 2) % dp) for i in range(dp)])  37.9 us
    dot_general x10, matrix products, times(): return jnp.dot(left_side, right_side, preferred_element_type=jnp.float32)  34.4 us
    dot_general x13, matrix products, inner_rows(): lax.dot_general(left_side, right_side, (((0,), (0,)), ((), ())), preferre...  33.6 us
    ppermute x19, waiting for transfers between devices, swap_x(): return lax.ppermute(value, n.dp, [(i, i ^ 1) for i in range(dp)])  31.2 us
    dot_general x10, matrix products, times_transposed(): lax.dot_general(left_side, right_side, (((1,), (1,)), ((), ())), preferre...  31 us
    pallas_call x3, Pallas kernels, per_image(): pl.pallas_call(kernel, grid=(self.slots,), in_specs=[spec(kind, array.sha...  28.1 us
  transfers between devices with their start and end apart: 90, of which 32 were waited for; matrix products, arithmetic and copies ran while one was open for 29% of the time, Pallas kernels for 14%

profile of v3, /device:TPU:0, one launch (start us, length us, event | category | flops | bytes accessed | tf_op | source)
XLA Modules:
  0.0 516.8 jit_solution(15253790473887236628)
XLA Ops:
  14.7 10.9 %collective-permute-done.2 = bf16[1,4320]{1,0:T(2,128)(2,1)S(1)} collective-permute-done((bf16[1,4320]{1,0:T(2,128)(2,1)S(1)}, bf16[1,4320]{1,0:T(2,128)(2,1)S(1)}, u32[]{:S(2)}, u32[]{:S(2)}) %collective-permute-start.2) | collective-permute-done | bytes 8672 | tf_op jit(solution)/shard_map/ppermute | solution.py:844
  35.3 8.8 %collective-permute-done.6 = bf16[2,4320]{1,0:T(2,128)(2,1)S(1)} collective-permute-done((bf16[2,4320]{1,0:T(2,128)(2,1)S(1)}, bf16[2,4320]{1,0:T(2,128)(2,1)S(1)}, u32[]{:S(2)}, u32[]{:S(2)}) %collective-permute-start.6) | collective-permute-done | bytes 17312 | tf_op jit(solution)/shard_map/ppermute | solution.py:947
  54.6 10.9 %collective-permute-done.10 = bf16[4,4320]{1,0:T(4,128)(2,1)S(1)} collective-permute-done((bf16[4,4320]{1,0:T(4,128)(2,1)S(1)}, bf16[4,4320]{1,0:T(4,128)(2,1)S(1)}, u32[]{:S(2)}, u32[]{:S(2)}) %collective-permute-start.10) | collective-permute-done | bytes 34592 | tf_op jit(solution)/shard_map/ppermute | solution.py:947
  77.8 10.7 %collective-permute-done.15 = f32[8,6912]{1,0:T(8,128)} collective-permute-done((f32[8,6912]{1,0:T(8,128)}, f32[8,6912]{1,0:T(8,128)}, u32[]{:S(2)}, u32[]{:S(2)}) %collective-permute-start.15) | collective-permute-done | bytes 221216 | tf_op jit(solution)/shard_map/ppermute | solution.py:844
  116.2 9.0 %collective-permute-done.24 = f32[2,6912]{1,0:T(2,128)} collective-permute-done((f32[2,6912]{1,0:T(2,128)S(1)}, f32[2,6912]{1,0:T(2,128)}, u32[]{:S(2)}, u32[]{:S(2)}) %collective-permute-start.24) | collective-permute-done | bytes 55328 | tf_op jit(solution)/shard_map/ppermute | solution.py:947
  136.0 10.1 %shard_map.251 = (bf16[512,1152]{1,0:T(8,128)(2,1)S(1)}, bf16[512,1152]{1,0:T(8,128)(2,1)S(1)}, bf16[512,1152]{1,0:T(8,128)(2,1)S(1)}, bf16[1152,1152]{1,0:T(8,128)(2,1)S(1)}) custom-call(s32[4]{0:T(128)S(1)} %pad_add_fusion.order_ref.place_ref, bf16[512,1152]{1,0:T(8,128)(2,1)S(1)} %bitcast.146, f32[2,1152]{1,0:T(2,128)S(1)} %copy-done.34, ...), custom_call_target="tpu_custom_call" | custom-call | tf_op jit(solution)/shard_map/pallas_call | solution.py:223
  146.2 5.2 shard_map.252
  166.1 6.5 %shard_map.254 = (f32[512,1152]{1,0:T(8,128)}, f32[512,1152]{1,0:T(8,128)}, bf16[512,1152]{1,0:T(8,128)(2,1)}) custom-call(bf16[512,1152]{1,0:T(8,128)(2,1)} %copy-done.21, bf16[1152,1152]{1,0:T(8,128)(2,1)} %copy-done.9, f32[1,1152]{1,0:T(1,128)} %get-tuple-element.735.bias_ref, bf16[512,1152]{1,0:T(8,128)(2,1)} %bitcast.159, f32[2,6,1152]{2,1,0:T(8,128)} %reshape.152.mod_ref), custom_call_target="tpu_custom_call" | custom-call | tf_op jit(solution)/shard_map/pallas_call | solution.py:504
  172.7 5.5 %fusion.45 = (bf16[512,1152]{1,0:T(8,128)(2,1)S(1)}, f32[512,1152]{1,0:T(8,128)}) fusion(f32[1152]{0:T(1024)S(1)} %get-tuple-element.1178, bf16[512,1152]{1,0:T(8,128)(2,1)} %get-tuple-element.947, bf16[1152,1152]{1,0:T(8,128)(2,1)} %collective-permute-done.25), kind=kOutput, calls=%fused_computation.82 | convolution fusion | flops 1364852736 | bytes 7377408 | tf_op jit(solution)/shard_map/dot_general | solution.py:43
  178.2 6.0 %fusion.53 = (bf16[512,1152]{1,0:T(8,128)(2,1)}, f32[512,1152]{1,0:T(8,128)}) fusion(f32[1152]{0:T(1024)S(1)} %get-tuple-element.1177, bf16[512,1152]{1,0:T(8,128)(2,1)S(1)} %copy-done.80, bf16[1152,1152]{1,0:T(8,128)(2,1)} %bitcast.21), kind=kOutput, calls=%fused_computation.90 | convolution fusion | flops 1364852736 | bytes 7377408 | tf_op jit(solution)/shard_map/dot_general | solution.py:43
  193.6 4.2 fusion.61
  197.8 5.2 %fusion.69 = (bf16[512,1152]{1,0:T(8,128)(2,1)}, f32[512,1152]{1,0:T(8,128)S(1)}) fusion(f32[1152]{0:T(1024)S(1)} %get-tuple-element.1175, bf16[512,1152]{1,0:T(8,128)(2,1)S(1)} %copy-done.81, bf16[1152,1152]{1,0:T(8,128)(2,1)} %bitcast.29), kind=kOutput, calls=%fused_computation.106 | convolution fusion | flops 1364852736 | bytes 7377408 | tf_op jit(solution)/shard_map/dot_general | solution.py:43
  204.7 4.3 collective-permute-done.35.refs_3_.refs_5_
  211.3 3.9 fusion
  226.3 5.1 fusion.153
  234.1 4.2 collective-permute-done.39.refs_6_.refs_7_
  254.8 5.1 convolution_add_fusion.9
  272.7 6.8 %collective-permute-done.45 = bf16[288,1152]{1,0:T(8,128)(2,1)S(1)} collective-permute-done((bf16[288,1152]{1,0:T(8,128)(2,1)S(1)}, bf16[288,1152]{1,0:T(8,128)(2,1)S(1)}, u32[]{:S(2)}, u32[]{:S(2)}) %collective-permute-start.45) | collective-permute-done | bytes 663584 | tf_op jit(solution)/shard_map/ppermute | solution.py:838
  288.2 5.5 %convolution_add_fusion.5.back_ref = f32[512,1152]{1,0:T(8,128)} fusion(f32[512,1152]{1,0:T(8,128)S(1)} %convolution_add_fusion.7, bf16[512,1152]{1,0:T(8,128)(2,1)S(1)} %get-tuple-element.948, bf16[1152,1152]{1,0:T(8,128)(2,1)} %bitcast.29), kind=kOutput, calls=%fused_computation.29 | convolution fusion | flops 1359544320 | bytes 8552448 | tf_op jit(solution)/shard_map/dot_general | solution.py:47
  304.6 4.2 fusion.3
  310.5 8.0 %shard_map.257 = (bf16[512,1152]{1,0:T(8,128)(2,1)}, f32[512,1152]{1,0:T(8,128)}, bf16[512,1152]{1,0:T(8,128)(2,1)}, f32[2,6,1152]{2,1,0:T(8,128)}) custom-call(f32[2]{0:T(128)} %copy-done.73, f32[512,1152]{1,0:T(8,128)} %get-tuple-element.939.middle_ref, f32[512,1152]{1,0:T(8,128)} %get-tuple-element.940.branch_ref, ...), custom_call_target="tpu_custom_call" | custom-call | tf_op jit(solution)/shard_map/pallas_call | solution.py:504
  332.7 13.6 %shard_map.258 = (bf16[512,1152]{1,0:T(8,128)(2,1)S(1)}, bf16[512,1152]{1,0:T(8,128)(2,1)S(1)}, bf16[512,1152]{1,0:T(8,128)(2,1)S(1)}, f32[2,2,1152]{2,1,0:T(2,128)S(1)}) custom-call(bf16[512,1152]{1,0:T(8,128)(2,1)S(1)} %get-tuple-element.974.query_ref, bf16[512,1152]{1,0:T(8,128)(2,1)S(1)} %copy-done.2, bf16[512,1152]{1,0:T(8,128)(2,1)S(1)} %copy-done.4, ...), custom_call_target="tpu_custom_call" | custom-call | tf_op jit(solution)/shard_map/pallas_call | solution.py:162
  350.1 6.8 %collective-permute-done.53 = bf16[288,1152]{1,0:T(8,128)(2,1)S(1)} collective-permute-done((bf16[288,1152]{1,0:T(8,128)(2,1)S(1)}, bf16[288,1152]{1,0:T(8,128)(2,1)S(1)}, u32[]{:S(2)}, u32[]{:S(2)}) %collective-permute-start.53) | collective-permute-done | bytes 663584 | tf_op jit(solution)/shard_map/ppermute | solution.py:847
  370.1 9.8 %collective-permute-done.57 = bf16[288,1152]{1,0:T(8,128)(2,1)S(1)} collective-permute-done((bf16[288,1152]{1,0:T(8,128)(2,1)S(1)}, bf16[288,1152]{1,0:T(8,128)(2,1)S(1)}, u32[]{:S(2)}, u32[]{:S(2)}) %collective-permute-start.57) | collective-permute-done | bytes 663584 | tf_op jit(solution)/shard_map/ppermute | solution.py:838
  385.7 13.7 %shard_map.259 = (f32[512,1152]{1,0:T(8,128)}, f32[2,2,1152]{2,1,0:T(2,128)}) custom-call(s32[4]{0:T(128)} %copy-done.31, bf16[512,1152]{1,0:T(8,128)(2,1)} %copy-done.18, bf16[512,1152]{1,0:T(8,128)(2,1)} %copy-done.19, bf16[512,1152]{1,0:T(8,128)(2,1)} %copy-done.20, f32[512,1152]{1,0:T(8,128)} %get-tuple-element.1040.middle_slope_ref, ...), custom_call_target="tpu_custom_call" | custom-call | tf_op jit(solution)/shard_map/pallas_call | solution.py:504
  412.4 10.0 %collective-permute-done.63 = bf16[288,1152]{1,0:T(8,128)(2,1)S(1)} collective-permute-done((bf16[288,1152]{1,0:T(8,128)(2,1)S(1)}, bf16[288,1152]{1,0:T(8,128)(2,1)S(1)}, u32[]{:S(2)}, u32[]{:S(2)}) %collective-permute-start.63) | collective-permute-done | bytes 663584 | tf_op jit(solution)/shard_map/ppermute | solution.py:847
  422.4 5.3 %collective-permute-done.62 = bf16[288,1152]{1,0:T(8,128)(2,1)S(1)} collective-permute-done((bf16[288,1152]{1,0:T(8,128)(2,1)S(1)}, bf16[288,1152]{1,0:T(8,128)(2,1)S(1)}, u32[]{:S(2)}, u32[]{:S(2)}) %collective-permute-start.62) | collective-permute-done | bytes 663584 | tf_op jit(solution)/shard_map/ppermute | solution.py:838
  432.0 13.6 %collective-permute-done.70 = bf16[8,12672]{1,0:T(8,128)(2,1)S(1)} collective-permute-done((bf16[8,12672]{1,0:T(8,128)(2,1)S(1)}, bf16[8,12672]{1,0:T(8,128)(2,1)S(1)}, u32[]{:S(2)}, u32[]{:S(2)}) %collective-permute-start.70) | collective-permute-done | bytes 202784 | tf_op jit(solution)/shard_map/ppermute | solution.py:947
  447.9 5.7 %collective-permute-done.73 = bf16[16,12672]{1,0:T(8,128)(2,1)S(1)} collective-permute-done((bf16[16,12672]{1,0:T(8,128)(2,1)S(1)}, bf16[16,12672]{1,0:T(8,128)(2,1)S(1)}, u32[]{:S(2)}, u32[]{:S(2)}) %collective-permute-start.73) | collective-permute-done | bytes 405536 | tf_op jit(solution)/shard_map/ppermute | solution.py:844
  481.2 6.4 %collective-permute-done.78 = bf16[144,1152]{1,0:T(8,128)(2,1)} collective-permute-done((bf16[144,1152]{1,0:T(8,128)(2,1)S(1)}, bf16[144,1152]{1,0:T(8,128)(2,1)}, u32[]{:S(2)}, u32[]{:S(2)}) %collective-permute-start.78) | collective-permute-done | bytes 331808 | tf_op jit(solution)/shard_map/ppermute | solution.py:847
  487.8 4.3 collective-permute-start.87
  497.7 8.3 %collective-permute-done.80.refs_1_ = bf16[144,1152]{1,0:T(8,128)(2,1)} collective-permute-done((bf16[144,1152]{1,0:T(8,128)(2,1)S(1)}, bf16[144,1152]{1,0:T(8,128)(2,1)}, u32[]{:S(2)}, u32[]{:S(2)}) %collective-permute-start.80) | collective-permute-done | bytes 331808 | tf_op jit(solution)/shard_map/ppermute | solution.py:847
  (514 shorter events, 275.7 us)
Async XLA Ops:
  5.8 20.0 %collective-permute-start = (bf16[2,144,1152]{2,1,0:T(8,128)(2,1)S(1)}, bf16[2,144,1152]{2,1,0:T(8,128)(2,1)S(1)}, u32[]{:S(2)}, u32[]{:S(2)}) collective-permute-start(bf16[2,144,1152]{2,1,0:T(8,128)(2,1)S(1)} %pad_maximum_fusion.1.refs_0_), channel_id=1, source_target_pairs={{0,8},{4,12},{8,16},{12,20},{16,24},{20,28},{24,0},{28,4},{1,9},{5... | collective-permute-start | bytes 1990664 | tf_op jit(solution)/shard_map/ppermute | solution.py:838
  25.8 21.7 %collective-permute-start.3 = (bf16[2,144,1152]{2,1,0:T(8,128)(2,1)S(1)}, bf16[2,144,1152]{2,1,0:T(8,128)(2,1)}, u32[]{:S(2)}, u32[]{:S(2)}) collective-permute-start(bf16[2,144,1152]{2,1,0:T(8,128)(2,1)S(1)} %collective-permute-done.refs_1_), channel_id=1, source_target_pairs={{0,8},{4,12},{8,16},{12,20},{16,24},{20,28},{24,0},{28,4},{1,9},{5... | collective-permute-start | bytes 1990664 | tf_op jit(solution)/shard_map/ppermute | solution.py:838
  27.3 20.2 %collective-permute-start.4 = (bf16[2,144,1152]{2,1,0:T(8,128)(2,1)S(1)}, bf16[2,144,1152]{2,1,0:T(8,128)(2,1)}, u32[]{:S(2)}, u32[]{:S(2)}) collective-permute-start(bf16[2,144,1152]{2,1,0:T(8,128)(2,1)S(1)} %collective-permute-done.refs_1_), channel_id=1, source_target_pairs={{0,4},{4,0},{8,12},{12,8},{16,20},{20,16},{24,28},{28,24},{1,5},{5... | collective-permute-start | bytes 1990664 | tf_op jit(solution)/shard_map/ppermute | solution.py:844
  68.1 24.2 %collective-permute-start.11 = (bf16[2,144,1152]{2,1,0:T(8,128)(2,1)}, bf16[2,144,1152]{2,1,0:T(8,128)(2,1)}, u32[]{:S(2)}, u32[]{:S(2)}) collective-permute-start(bf16[2,144,1152]{2,1,0:T(8,128)(2,1)} %collective-permute-done.7.refs_3_), channel_id=1, source_target_pairs={{0,4},{4,0},{8,12},{12,8},{16,20},{20,16},{24,28},{28,24},{1,5},{5... | collective-permute-start | bytes 1990664 | tf_op jit(solution)/shard_map/ppermute | solution.py:844
  72.9 19.4 %collective-permute-start.12 = (bf16[2,144,1152]{2,1,0:T(8,128)(2,1)}, bf16[2,144,1152]{2,1,0:T(8,128)(2,1)}, u32[]{:S(2)}, u32[]{:S(2)}) collective-permute-start(bf16[2,144,1152]{2,1,0:T(8,128)(2,1)} %broadcast_select_fusion), channel_id=1, source_target_pairs={{0,2},{1,3},{2,0},{3,1},{4,6},{5,7},{6,4},{7,5},{8,10},{9,11},{10,... | collective-permute-start | bytes 1990664 | tf_op jit(solution)/shard_map/ppermute | solution.py:847
  126.8 26.9 %collective-permute-start.26 = (bf16[1,144,1152]{2,1,0:T(8,128)(2,1)}, bf16[1,144,1152]{2,1,0:T(8,128)(2,1)}, u32[]{:S(2)}, u32[]{:S(2)}) collective-permute-start(bf16[1,144,1152]{2,1,0:T(8,128)(2,1)} %collective-permute-done.13.refs_1_), channel_id=1, source_target_pairs={{0,2},{1,3},{2,0},{3,1},{4,6},{5,7},{6,4},{7,5},{8,10},{9,11},{10,... | collective-permute-start | bytes 995336 | tf_op jit(solution)/shard_map/ppermute | solution.py:847
  128.4 25.4 %collective-permute-start.27 = (bf16[1,144,1152]{2,1,0:T(8,128)(2,1)}, bf16[1,144,1152]{2,1,0:T(8,128)(2,1)}, u32[]{:S(2)}, u32[]{:S(2)}) collective-permute-start(bf16[1,144,1152]{2,1,0:T(8,128)(2,1)} %collective-permute-done.13.refs_1_), channel_id=1, source_target_pairs={{0,8},{4,12},{8,16},{12,20},{16,24},{20,28},{24,0},{28,4},{1,9},{5... | collective-permute-start | bytes 995336 | tf_op jit(solution)/shard_map/ppermute | solution.py:838
  131.7 25.9 %collective-permute-start.25 = (bf16[1152,1152]{1,0:T(8,128)(2,1)}, bf16[1152,1152]{1,0:T(8,128)(2,1)}, u32[]{:S(2)}, u32[]{:S(2)}) collective-permute-start(bf16[1152,1152]{1,0:T(8,128)(2,1)} %bitcast.21), channel_id=1, source_target_pairs={{0,1},{1,0},{2,3},{3,2},{4,5},{5,4},{6,7},{7,6},{8,9},{9,8},{10,11... | collective-permute-start | bytes 7962632 | tf_op jit(solution)/shard_map/ppermute | solution.py:850
  133.3 24.4 %collective-permute-start.29 = (bf16[2,144,1152]{2,1,0:T(8,128)(2,1)S(1)}, bf16[2,144,1152]{2,1,0:T(8,128)(2,1)S(1)}, u32[]{:S(2)}, u32[]{:S(2)}) collective-permute-start(bf16[2,144,1152]{2,1,0:T(8,128)(2,1)S(1)} %pad_maximum_fusion.2), channel_id=1, source_target_pairs={{0,4},{4,0},{8,12},{12,8},{16,20},{20,16},{24,28},{28,24},{1,5},{5... | collective-permute-start | bytes 1990664 | tf_op jit(solution)/shard_map/ppermute | solution.py:844
  135.1 22.5 %collective-permute-start.28 = (bf16[1,144,1152]{2,1,0:T(8,128)(2,1)}, bf16[1,144,1152]{2,1,0:T(8,128)(2,1)S(1)}, u32[]{:S(2)}, u32[]{:S(2)}) collective-permute-start(bf16[1,144,1152]{2,1,0:T(8,128)(2,1)} %get-tuple-element.794.refs_0_), channel_id=1, source_target_pairs={{0,4},{4,0},{8,12},{12,8},{16,20},{20,16},{24,28},{28,24},{1,5},{5... | collective-permute-start | bytes 995336 | tf_op jit(solution)/shard_map/ppermute | solution.py:844
  160.6 28.4 %collective-permute-start.30 = (bf16[1152,1152]{1,0:T(8,128)(2,1)}, bf16[1152,1152]{1,0:T(8,128)(2,1)}, u32[]{:S(2)}, u32[]{:S(2)}) collective-permute-start(bf16[1152,1152]{1,0:T(8,128)(2,1)} %bitcast.29), channel_id=1, source_target_pairs={{0,1},{1,0},{2,3},{3,2},{4,5},{5,4},{6,7},{7,6},{8,9},{9,8},{10,11... | collective-permute-start | bytes 7962632 | tf_op jit(solution)/shard_map/ppermute | solution.py:850
  160.6 26.8 %collective-permute-start.31 = (bf16[1,144,1152]{2,1,0:T(8,128)(2,1)}, bf16[1,144,1152]{2,1,0:T(8,128)(2,1)}, u32[]{:S(2)}, u32[]{:S(2)}) collective-permute-start(bf16[1,144,1152]{2,1,0:T(8,128)(2,1)} %collective-permute-done.27.refs_2_), channel_id=1, source_target_pairs={{0,8},{4,12},{8,16},{12,20},{16,24},{20,28},{24,0},{28,4},{1,9},{5... | collective-permute-start | bytes 995336 | tf_op jit(solution)/shard_map/ppermute | solution.py:838
  161.0 26.5 %collective-permute-start.34 = (bf16[1,144,1152]{2,1,0:T(8,128)(2,1)}, bf16[1,144,1152]{2,1,0:T(8,128)(2,1)}, u32[]{:S(2)}, u32[]{:S(2)}) collective-permute-start(bf16[1,144,1152]{2,1,0:T(8,128)(2,1)} %collective-permute-done.27.refs_2_), channel_id=1, source_target_pairs={{0,4},{4,0},{8,12},{12,8},{16,20},{20,16},{24,28},{28,24},{1,5},{5... | collective-permute-start | bytes 995336 | tf_op jit(solution)/shard_map/ppermute | solution.py:844
  165.2 22.2 %collective-permute-start.32 = (bf16[2,144,1152]{2,1,0:T(8,128)(2,1)S(1)}, bf16[2,144,1152]{2,1,0:T(8,128)(2,1)S(1)}, u32[]{:S(2)}, u32[]{:S(2)}) collective-permute-start(bf16[2,144,1152]{2,1,0:T(8,128)(2,1)S(1)} %pad_maximum_fusion.3), channel_id=1, source_target_pairs={{0,2},{1,3},{2,0},{3,1},{4,6},{5,7},{6,4},{7,5},{8,10},{9,11},{10,... | collective-permute-start | bytes 1990664 | tf_op jit(solution)/shard_map/ppermute | solution.py:847
  165.8 21.7 %collective-permute-start.33 = (bf16[1,144,1152]{2,1,0:T(8,128)(2,1)}, bf16[1,144,1152]{2,1,0:T(8,128)(2,1)S(1)}, u32[]{:S(2)}, u32[]{:S(2)}) collective-permute-start(bf16[1,144,1152]{2,1,0:T(8,128)(2,1)} %collective-permute-done.13.refs_1_), channel_id=1, source_target_pairs={{0,4},{4,0},{8,12},{12,8},{16,20},{20,16},{24,28},{28,24},{1,5},{5... | collective-permute-start | bytes 995336 | tf_op jit(solution)/shard_map/ppermute | solution.py:844
  189.0 20.0 %collective-permute-start.37 = (bf16[1152,1152]{1,0:T(8,128)(2,1)}, bf16[1152,1152]{1,0:T(8,128)(2,1)}, u32[]{:S(2)}, u32[]{:S(2)}) collective-permute-start(bf16[1152,1152]{1,0:T(8,128)(2,1)} %convolution_convert_fusion.7), channel_id=1, source_target_pairs={{0,1},{1,0},{2,3},{3,2},{4,5},{5,4},{6,7},{7,6},{8,9},{9,8},{10,11... | collective-permute-start | bytes 7962632 | tf_op jit(solution)/shard_map/ppermute | solution.py:850
  210.7 27.5 %collective-permute-start.38 = (bf16[1152,1152]{1,0:T(8,128)(2,1)S(1)}, bf16[1152,1152]{1,0:T(8,128)(2,1)S(1)}, u32[]{:S(2)}, u32[]{:S(2)}) collective-permute-start(bf16[1152,1152]{1,0:T(8,128)(2,1)S(1)} %bitcast.151), channel_id=1, source_target_pairs={{0,1},{1,0},{2,3},{3,2},{4,5},{5,4},{6,7},{7,6},{8,9},{9,8},{10,11... | collective-permute-start | bytes 7962632 | tf_op jit(solution)/shard_map/ppermute | solution.py:850
  210.8 27.4 %collective-permute-start.41 = (bf16[1152,1152]{1,0:T(8,128)(2,1)S(1)}, bf16[1152,1152]{1,0:T(8,128)(2,1)S(1)}, u32[]{:S(2)}, u32[]{:S(2)}) collective-permute-start(bf16[1152,1152]{1,0:T(8,128)(2,1)S(1)} %convolution_convert_fusion.6), channel_id=1, source_target_pairs={{0,1},{1,0},{2,3},{3,2},{4,5},{5,4},{6,7},{7,6},{8,9},{9,8},{10,11... | collective-permute-start | bytes 7962632 | tf_op jit(solution)/shard_map/ppermute | solution.py:850
  238.5 21.4 %collective-permute-start.43 = (bf16[288,1152]{1,0:T(8,128)(2,1)S(1)}, bf16[288,1152]{1,0:T(8,128)(2,1)S(1)}, u32[]{:S(2)}, u32[]{:S(2)}) collective-permute-start(bf16[288,1152]{1,0:T(8,128)(2,1)S(1)} %add_convert_fusion.17), channel_id=1, source_target_pairs={{0,8},{4,12},{8,16},{12,20},{16,24},{20,28},{24,0},{28,4},{1,9},{5... | collective-permute-start | bytes 1990664 | tf_op jit(solution)/shard_map/ppermute | solution.py:838
  259.8 19.6 %collective-permute-start.44 = (bf16[1152,1152]{1,0:T(8,128)(2,1)S(1)}, bf16[1152,1152]{1,0:T(8,128)(2,1)S(1)}, u32[]{:S(2)}, u32[]{:S(2)}) collective-permute-start(bf16[1152,1152]{1,0:T(8,128)(2,1)S(1)} %convolution_convert_fusion.5), channel_id=1, source_target_pairs={{0,1},{1,0},{2,3},{3,2},{4,5},{5,4},{6,7},{7,6},{8,9},{9,8},{10,11... | collective-permute-start | bytes 7962632 | tf_op jit(solution)/shard_map/ppermute | solution.py:850
  260.5 18.9 %collective-permute-start.45 = (bf16[288,1152]{1,0:T(8,128)(2,1)S(1)}, bf16[288,1152]{1,0:T(8,128)(2,1)S(1)}, u32[]{:S(2)}, u32[]{:S(2)}) collective-permute-start(bf16[288,1152]{1,0:T(8,128)(2,1)S(1)} %add_convert_fusion.16), channel_id=1, source_target_pairs={{0,8},{4,12},{8,16},{12,20},{16,24},{20,28},{24,0},{28,4},{1,9},{5... | collective-permute-start | bytes 1990664 | tf_op jit(solution)/shard_map/ppermute | solution.py:838
  280.9 20.3 %collective-permute-start.46 = (bf16[1152,1152]{1,0:T(8,128)(2,1)S(1)}, bf16[1152,1152]{1,0:T(8,128)(2,1)}, u32[]{:S(2)}, u32[]{:S(2)}) collective-permute-start(bf16[1152,1152]{1,0:T(8,128)(2,1)S(1)} %convolution_convert_fusion.4), channel_id=1, source_target_pairs={{0,1},{1,0},{2,3},{3,2},{4,5},{5,4},{6,7},{7,6},{8,9},{9,8},{10,11... | collective-permute-start | bytes 7962632 | tf_op jit(solution)/shard_map/ppermute | solution.py:850
  281.0 19.4 %collective-permute-start.48 = (bf16[288,1152]{1,0:T(8,128)(2,1)S(1)}, bf16[288,1152]{1,0:T(8,128)(2,1)S(1)}, u32[]{:S(2)}, u32[]{:S(2)}) collective-permute-start(bf16[288,1152]{1,0:T(8,128)(2,1)S(1)} %constant_dynamic-slice_fusion.8), channel_id=1, source_target_pairs={{0,8},{4,12},{8,16},{12,20},{16,24},{20,28},{24,0},{28,4},{1,9},{5... | collective-permute-start | bytes 1990664 | tf_op jit(solution)/shard_map/ppermute | solution.py:838
  304.2 19.1 %collective-permute-start.50 = (bf16[288,1152]{1,0:T(8,128)(2,1)}, bf16[288,1152]{1,0:T(8,128)(2,1)}, u32[]{:S(2)}, u32[]{:S(2)}) collective-permute-start(bf16[288,1152]{1,0:T(8,128)(2,1)} %add_convert_fusion.14), channel_id=1, source_target_pairs={{0,8},{4,12},{8,16},{12,20},{16,24},{20,28},{24,0},{28,4},{1,9},{5... | collective-permute-start | bytes 1990664 | tf_op jit(solution)/shard_map/ppermute | solution.py:838
  326.8 23.3 %collective-permute-start.54 = (bf16[288,1152]{1,0:T(8,128)(2,1)S(1)}, bf16[288,1152]{1,0:T(8,128)(2,1)S(1)}, u32[]{:S(2)}, u32[]{:S(2)}) collective-permute-start(bf16[288,1152]{1,0:T(8,128)(2,1)S(1)} %add_convert_fusion.12), channel_id=1, source_target_pairs={{0,8},{4,12},{8,16},{12,20},{16,24},{20,28},{24,0},{28,4},{1,9},{5... | collective-permute-start | bytes 1990664 | tf_op jit(solution)/shard_map/ppermute | solution.py:838
  327.0 23.1 %collective-permute-start.52 = (bf16[288,1152]{1,0:T(8,128)(2,1)S(1)}, bf16[288,1152]{1,0:T(8,128)(2,1)S(1)}, u32[]{:S(2)}, u32[]{:S(2)}) collective-permute-start(bf16[288,1152]{1,0:T(8,128)(2,1)S(1)} %get-tuple-element.1188), channel_id=1, source_target_pairs={{0,2},{1,3},{2,0},{3,1},{4,6},{5,7},{6,4},{7,5},{8,10},{9,11},{10,... | collective-permute-start | bytes 1990664 | tf_op jit(solution)/shard_map/ppermute | solution.py:847
  328.6 28.3 %collective-permute-start.53 = (bf16[288,1152]{1,0:T(8,128)(2,1)S(1)}, bf16[288,1152]{1,0:T(8,128)(2,1)S(1)}, u32[]{:S(2)}, u32[]{:S(2)}) collective-permute-start(bf16[288,1152]{1,0:T(8,128)(2,1)S(1)} %get-tuple-element.1187), channel_id=1, source_target_pairs={{0,2},{1,3},{2,0},{3,1},{4,6},{5,7},{6,4},{7,5},{8,10},{9,11},{10,... | collective-permute-start | bytes 1990664 | tf_op jit(solution)/shard_map/ppermute | solution.py:847
  329.3 29.2 %collective-permute-start.51 = (bf16[288,1152]{1,0:T(8,128)(2,1)S(1)}, bf16[288,1152]{1,0:T(8,128)(2,1)S(1)}, u32[]{:S(2)}, u32[]{:S(2)}) collective-permute-start(bf16[288,1152]{1,0:T(8,128)(2,1)S(1)} %add_convert_fusion.13), channel_id=1, source_target_pairs={{0,8},{4,12},{8,16},{12,20},{16,24},{20,28},{24,0},{28,4},{1,9},{5... | collective-permute-start | bytes 1990664 | tf_op jit(solution)/shard_map/ppermute | solution.py:838
  358.5 21.4 %collective-permute-start.55 = (bf16[1152,1152]{1,0:T(8,128)(2,1)S(1)}, bf16[1152,1152]{1,0:T(8,128)(2,1)S(1)}, u32[]{:S(2)}, u32[]{:S(2)}) collective-permute-start(bf16[1152,1152]{1,0:T(8,128)(2,1)S(1)} %convolution_convert_fusion.3), channel_id=1, source_target_pairs={{0,1},{1,0},{2,3},{3,2},{4,5},{5,4},{6,7},{7,6},{8,9},{9,8},{10,11... | collective-permute-start | bytes 7962632 | tf_op jit(solution)/shard_map/ppermute | solution.py:850
  358.5 21.4 %collective-permute-start.56 = (bf16[1152,1152]{1,0:T(8,128)(2,1)S(1)}, bf16[1152,1152]{1,0:T(8,128)(2,1)S(1)}, u32[]{:S(2)}, u32[]{:S(2)}) collective-permute-start(bf16[1152,1152]{1,0:T(8,128)(2,1)S(1)} %convolution_convert_fusion.2), channel_id=1, source_target_pairs={{0,1},{1,0},{2,3},{3,2},{4,5},{5,4},{6,7},{7,6},{8,9},{9,8},{10,11... | collective-permute-start | bytes 7962632 | tf_op jit(solution)/shard_map/ppermute | solution.py:850
  381.6 19.5 %collective-permute-start.61 = (bf16[288,1152]{1,0:T(8,128)(2,1)}, bf16[288,1152]{1,0:T(8,128)(2,1)}, u32[]{:S(2)}, u32[]{:S(2)}) collective-permute-start(bf16[288,1152]{1,0:T(8,128)(2,1)} %add_convert_fusion.8), channel_id=1, source_target_pairs={{0,8},{4,12},{8,16},{12,20},{16,24},{20,28},{24,0},{28,4},{1,9},{5... | collective-permute-start | bytes 1990664 | tf_op jit(solution)/shard_map/ppermute | solution.py:838
  465.4 22.2 %collective-permute-start.78 = (bf16[144,1152]{1,0:T(8,128)(2,1)S(1)}, bf16[144,1152]{1,0:T(8,128)(2,1)}, u32[]{:S(2)}, u32[]{:S(2)}) collective-permute-start(bf16[144,1152]{1,0:T(8,128)(2,1)S(1)} %copy-done.59), channel_id=1, source_target_pairs={{0,2},{1,3},{2,0},{3,1},{4,6},{5,7},{6,4},{7,5},{8,10},{9,11},{10,... | collective-permute-start | bytes 995336 | tf_op jit(solution)/shard_map/ppermute | solution.py:847
  (151 other events, 1585.7 us)

commit v4 on v3

--- a/solution.py
+++ b/solution.py
@@ -13,16 +13,6 @@
 
 epsilon = 1e-06
 masked_score = -1e30
-
-
-def layer_norm(values):
-    centered = values - jnp.mean(values, -1, keepdims=True)
-    variance = jnp.mean(centered * centered, -1, keepdims=True)
-    return centered * lax.rsqrt(variance + epsilon)
-
-
-def modulate(values, shift_part, scale_part):
-    return layer_norm(values) * (1.0 + scale_part) + shift_part
 
 
 def gelu(values):
@@ -234,18 +224,31 @@
     )(jnp.stack(order).astype(jnp.int32), normed, bias, *units)
 
 
-def middle_kernel(attended_ref, weight_ref, bias_ref, hidden_ref, mod_ref, branch_ref, middle_ref, normed_ref):
+def start_kernel(
+    live_ref, terms_ref, bias_ref, hidden_ref, cotangent_ref, normed_ref, slope_ref, mod_ref
+):
+    slot = pl.program_id(0)
+    width = hidden_ref.shape[1]
+    modulation = terms_ref[pl.ds(slot, 1), :] + bias_ref[...]
+    cuts = [modulation[:, i * width : (i + 1) * width] for i in range(6)]
+    for i in range(6):
+        mod_ref[0, i : i + 1] = cuts[i]
+    normed = norm_parts(hidden_ref[...].astype(jnp.float32))[0]
+    normed_ref[...] = low(normed * (1.0 + cuts[1]) + cuts[0])
+    slope_ref[...] = low(cotangent_ref[...].astype(jnp.float32) * live_ref[slot] * cuts[5])
+
+
+def middle_kernel(attended_ref, weight_ref, bias_ref, hidden_ref, mod_ref, branch_ref, normed_ref):
     gate_one, shift_two, scale_two = [mod_ref[0, i : i + 1] for i in (2, 3, 4)]
     branch = times(attended_ref[...], weight_ref[...]) + bias_ref[...]
     branch_ref[...] = branch
     middle = hidden_ref[...].astype(jnp.float32) + gate_one * branch
-    middle_ref[...] = middle
     normed_ref[...] = low(norm_parts(middle)[0] * (1.0 + scale_two) + shift_two)
 
 
 def finish_kernel(
     live_ref,
-    middle_ref,
+    hidden_ref,
     branch_ref,
     out_ref,
     back_ref,
@@ -259,7 +262,8 @@
 ):
     gate_one, shift_two, scale_two, gate_two = [mod_ref[0, i : i + 1] for i in (2, 3, 4, 5)]
     live = live_ref[pl.program_id(0)]
-    middle = middle_ref[...]
+    branch = branch_ref[...]
+    middle = hidden_ref[...].astype(jnp.float32) + gate_one * branch
     mlp_out = out_ref[...] + bias_ref[...]
     layer_ref[...] = low(live * (middle + gate_two * mlp_out))
     slope = cotangent_ref[...].astype(jnp.float32) * live
@@ -270,7 +274,7 @@
     slopes_ref[0, 2:3] = patch_sums(back * normed)
     middle_slope = slope + norm_back(normed, inverse, back * (1.0 + scale_two))
     middle_slope_ref[...] = middle_slope
-    slopes_ref[0, 0:1] = patch_sums(middle_slope * branch_ref[...])
+    slopes_ref[0, 0:1] = patch_sums(middle_slope * branch)
     branch_low = low(middle_slope * gate_one)
     branch_low_ref[...] = branch_low
     slopes_ref[0, 4:5] = patch_sums(branch_low.astype(jnp.float32))
@@ -421,6 +425,22 @@
     )(jnp.stack(order).astype(jnp.int32), *units)
 
 
+def shrink_out_kernel(order_ref, *refs):
+    for index in range(4):
+        refs[4][order_ref[index]] = refs[index][...].astype(jnp.float32)
+
+
+def shrink_out(units, order):
+    rows, width = units[0].shape
+    vmem = pl.BlockSpec(memory_space=pltpu.VMEM)
+    return pl.pallas_call(
+        shrink_out_kernel,
+        in_specs=[pl.BlockSpec(memory_space=pltpu.SMEM)] + [vmem] * 4,
+        out_specs=vmem,
+        out_shape=jax.ShapeDtypeStruct((4, rows, width), jnp.float32),
+    )(jnp.stack(order).astype(jnp.int32), *units).reshape(4 * rows, width)
+
+
 def spread_kernel(parts, order_ref, *refs):
     units, out_ref, held = refs[:4], refs[4], refs[5]
     for index in range(4):
@@ -464,18 +484,18 @@
     def flat(self, values):
         return values.reshape(self.rows, self.width)
 
-    def pieces(self, modulation):
-        cut = modulation.reshape(self.slots, 6, 1, self.width)
-        return [cut[:, i] for i in range(6)]
-
-    def start(self, modulation):
-        shift_one, scale_one = self.pieces(modulation)[:2]
-        normed = modulate(self.hidden_in.astype(jnp.float32), shift_one, scale_one)
-        return self.flat(low(normed))
-
-    def shrink_slope(self, modulation):
-        slope = self.cotangent.astype(jnp.float32) * self.live[:, None, None]
-        return self.flat(low(slope * self.pieces(modulation)[5]))
+    def start(self, terms, bias):
+        return self.per_image(
+            start_kernel,
+            [("rows", jnp.bfloat16), ("rows", jnp.bfloat16), (6, jnp.float32)],
+            [
+                ("scalar", self.live),
+                ("all", terms),
+                ("all", bias),
+                ("rows", self.hidden),
+                ("rows", self.flat(self.cotangent)),
+            ],
+        )
 
     def attention(self, normed_one, units, order, attend_bias):
         queries, keys_all, values_all, output_full = project(
@@ -511,19 +531,16 @@
             compiler_params=pltpu.CompilerParams(vmem_limit_bytes=56 << 20),
         )(*[array for _, array in ins])
 
-    def six(self, modulation):
-        return "mod", modulation.reshape(self.slots, 6, self.width)
-
     def middle(self, attended, output_full, output_bias, modulation):
         return self.per_image(
             middle_kernel,
-            [("rows", jnp.float32), ("rows", jnp.float32), ("rows", jnp.bfloat16)],
+            [("rows", jnp.float32), ("rows", jnp.bfloat16)],
             [
                 ("rows", attended),
                 ("all", output_full),
                 ("all", output_bias),
                 ("rows", self.hidden),
-                self.six(modulation),
+                ("mod", modulation),
             ],
         )
 
@@ -539,9 +556,10 @@
         back = times_transposed(inner_slope, expand_unit)
         if totals:
             out, back = out + totals[0], back + totals[1]
-        return inner_slope, column_sums(inner_slope)[None], out, back
-
-    def finish(self, middle, branch, out, back, shrink_bias, modulation):
+        ones = jnp.ones((8, self.rows), jnp.bfloat16)
+        return inner_slope, times(ones, inner_slope), out, back
+
+    def finish(self, branch, out, back, shrink_bias, modulation):
         layer_out, *others = self.per_image(
             finish_kernel,
             [
@@ -552,13 +570,13 @@
             ],
             [
                 ("scalar", self.live),
-                ("rows", middle),
+                ("rows", self.hidden),
                 ("rows", branch),
                 ("rows", out),
                 ("rows", back),
                 ("rows", self.flat(self.cotangent)),
                 ("all", shrink_bias),
-                self.six(modulation),
+                ("mod", modulation),
             ],
         )
         return layer_out.reshape(self.hidden_in.shape), *others
@@ -572,7 +590,7 @@
             [("rows", jnp.float32), (2, jnp.float32)],
             [("scalar", jnp.stack(order).astype(jnp.int32))]
             + [("rows", slope) for slope in slopes]
-            + [("rows", middle_slope), ("rows", self.hidden), self.six(modulation)]
+            + [("rows", middle_slope), ("rows", self.hidden), ("mod", modulation)]
             + [("any", unit) for unit in units],
             [
                 pltpu.VMEM((4, self.width, self.width), jnp.bfloat16),
@@ -625,7 +643,7 @@
 def pack_slopes_kernel(order_ref, first_ref, later_ref, head_ref, condition_ref, *refs):
     units, out_ref, held_ref = refs[:4], refs[4], refs[5]
     for index, unit in enumerate(units):
-        held_ref[pl.ds(order_ref[index], 1), :] = unit[...]
+        held_ref[pl.ds(order_ref[index], 1), :] = unit[0:1, :]
     slots, width = condition_ref.shape
     sums = [head_ref[0, i : i + 1] + head_ref[1, i : i + 1] for i in range(2)]
     sums += [later_ref[0, i : i + 1] + later_ref[1, i : i + 1] for i in (4, 5)]
@@ -709,17 +727,16 @@
     biases = unpack(packed, shard)
     expand_biases = biases[3].reshape(4, dp, shard).transpose(1, 0, 2).reshape(4, width)
     terms = times(act_rows(conditions, here, shard), modulation_weight)
-    modulation = lax.psum_scatter(terms, "dp", scatter_dimension=0, tiled=True) + biases[0]
+    terms = lax.psum_scatter(terms, "dp", scatter_dimension=0, tiled=True)
+    normed_one, shrink_slope, modulation = layer.start(terms, biases[0])
     weights = whole(jnp.concatenate([attend_weight, output_weight], 1))
     weights = [weights[:, unit * width : (unit + 1) * width] for unit in range(4)]
     natural = [jnp.int32(unit) for unit in range(4)]
     expand_full, shrink_full = whole(expand_weight), whole(shrink_weight)
-    normed_one = layer.start(modulation)
-    shrink_slope = layer.shrink_slope(modulation)
     queries, keys_all, values_all, output_full, attended, logs = layer.attention(
         normed_one, weights, natural, biases[1]
     )
-    branch, middle, normed_two = layer.middle(attended, output_full, biases[2], modulation)
+    branch, normed_two = layer.middle(attended, output_full, biases[2], modulation)
     totals = ()
     expand_terms, shrink_terms, inner_sums = [], [], []
     for unit in range(4):
@@ -730,9 +747,9 @@
         )
         expand_terms.append(low(inner_rows(normed_two, inner_slope)))
         shrink_terms.append(low(inner_rows(active, shrink_slope)))
-        inner_sums.append(inner_sum)
+        inner_sums.append(inner_sum[:1])
     layer_out, middle_slope, branch_low, later = layer.finish(
-        middle, branch, *totals, biases[4], modulation
+        branch, *totals, biases[4], modulation
     )
     attended_slope = low(times_transposed(branch_low, output_full))
     *slopes, head_sums = layer.attention_back(
@@ -928,7 +945,7 @@
         )
 
     for name, stream, row, tick in (
-        (n.Aown, n.AB, 0, 5), (n.Bown, n.AB, 1, 6), (n.Cown, n.C, 0, 9)
+        (n.Aown, n.AB, 0, 4), (n.Bown, n.AB, 1, 5), (n.Cown, n.C, 0, 9)
     ):
         parts = tuple((str(stream) + str(step)) for step in range(4))
         parts += tuple((str(stream) + n.x + str(step)) for step in range(4))
@@ -1000,14 +1017,12 @@
     terms = shrink_terms(3, n.terms, (n.x,))
     terms = shrink_terms(4, terms, (n.near,))
     terms = shrink_terms(5, terms, (n.far,))
-    at(6, n.mod, (str(terms), n.mod_bias), lambda terms, bias: terms + bias)
-    at(6, n.n1, n.mod, layer.start)
-    at(6, n.gm, n.mod, layer.shrink_slope)
+    at(6, (n.n1, n.gm, n.mod), (terms, n.mod_bias), layer.start)
 
     units_a = (n.Aown, n.Ay, n.Ac, n.Acy)
     at(6, (n.q, n.k, n.v, n.O, n.att, n.logs), (n.n1, n.att_bias) + units_a,
        lambda n1, bias, *units: layer.attention(n1, units, order, bias))
-    at(7, (n.branch, n.middle, n.n2), (n.att, n.O, n.out_bias, n.mod), layer.middle)
+    at(7, (n.branch, n.n2), (n.att, n.O, n.out_bias, n.mod), layer.middle)
 
     def expand(index, n2, weight, biases):
         return layer.expand(n2, weight, biases, order[index])
@@ -1036,7 +1051,7 @@
     at(13, n.dB_y, (n.n2, n.gi_y, n.dB_rcy), term)
 
     at(13, (n.layer_out, n.middle_slope, n.branch_low, n.later),
-       (n.middle, n.branch, n.out3, n.back3, n.shr_bias, n.mod), layer.finish)
+       (n.branch, n.out3, n.back3, n.shr_bias, n.mod), layer.finish)
     at(13, n.g_att, (n.branch_low, n.O), lambda b, w: low(times_transposed(b, w)))
     at(14, (n.gq, n.gk, n.gv, n.head_sums), (n.g_att, n.q, n.k, n.v, n.logs), layer.attention_back)
     def attend_term(index, n1, att, gq, gk, gv, branch_low, *received):
@@ -1105,17 +1120,13 @@
         at(tick_one, (str(name) + n._rc), (str(name) + n._c), swap_core)
         at(tick_two, (str(name) + n._rcy), (str(name) + n._cy), swap_core)
     end_c = wide(n.dC, 9, 12, 20)
-    end_b = halved(n.dB, (13, 14, 14, 15), (13, 14, 14, 15), 14, 20, rest=1)
+    end_b = halved(n.dB, (13, 14, 14, 15), (13, 14, 14, 15), 14, 19, rest=1)
     end_a = halved(n.dA, (16, 17, 18, 19), (16, 17, 18, 19), 17, 21, (n.rc,))
-
-    def shrink_out(*units):
-        whole = assemble([(unit[None], 0) for unit in units], order, 4)
-        return whole.reshape(-1, width).astype(jnp.float32)
 
     def four(name):
         return tuple((str(name) + n._ + str(i)) for i in range(4))
 
-    at(end_c, n.shr_weight, four(n.dC), shrink_out)
+    at(end_c, n.shr_weight, four(n.dC), lambda *units: shrink_out(units, order))
     at(end_b, n.exp_weight, four(n.dB), lambda *units: spread(units, order, dp))
     at(end_a, (n.att_weight, n.out_weight), four(n.dA), lambda *units: attend_out(units, order))
 

time: 523 us -> 496 us (0.948)
  waiting for transfers between devices: 168 us -> 141 us
    ppermute x21, waiting for transfers between devices: 54.5 us -> 38.5 us  [swap_y(): return lax.ppermute(value, n.rep, [(i, i ^ 2) for i in range(4)])]
    ppermute x21, waiting for transfers between devices: 37.9 us -> 27.1 us  [up(): return lax.ppermute(value, n.dp, [(i, (i + 2) % dp) for i in range(dp)])]
    reduce_sum x5 -> x1, other arithmetic: 8.37 us -> 1.6 us  [column_sums(): return jnp.sum(values, 0, dtype=jnp.float32)]
    convert_element_type x26 -> x28, other arithmetic: 19.8 us -> 26 us  [low(): return values.astype(jnp.bfloat16)]
    pallas_call x3 -> x4, Pallas kernels: 28.1 us -> 31 us  [per_image(): pl.pallas_call(kernel, grid=(self.slots,), in_specs=[spec(kind, array.sha...]
    dot_general x10 -> x14, matrix products: 34.4 us -> 36.5 us  [times(): return jnp.dot(left_side, right_side, preferred_element_type=jnp.float32)]
    unnamed x190 -> x187, local copies, waits for them, and re-layouts: 10.5 us -> 11.8 us
    pallas_call x7 -> x6, Pallas kernels: 16.5 us -> 15.4 us  [assemble(): pl.pallas_call(assemble_kernel, grid=(1,), in_specs=[pl.BlockSpec(memory_...]
  transfers between devices with their start and end apart: 90 -> 90, of which waited for: 32 -> 29; matrix products, arithmetic and copies ran while one was open for 29% -> 28% of each run, Pallas kernels for 14% -> 16%
where the time goes in v4:
time: 496 us; the launch traced here: 489 us
  waiting for transfers between devices  141 us (28%)
  matrix products  97.7 us (20%)
  starting transfers between devices  90.4 us (18%)
  Pallas kernels  87.3 us (18%)
  other arithmetic  41.2 us (8%)
  local copies, waits for them, and re-layouts  27.8 us (6%)
    ppermute x9, waiting for transfers between devices, swap_z(): return lax.ppermute(value, n.dp, [(i, i ^ 2 * distance) for i in range(dp)])  48.6 us
    ppermute x21, waiting for transfers between devices, swap_y(): return lax.ppermute(value, n.rep, [(i, i ^ 2) for i in range(4)])  38.5 us
    dot_general x14, matrix products, times(): return jnp.dot(left_side, right_side, preferred_element_type=jnp.float32)  36.5 us
    pallas_call x4, Pallas kernels, per_image(): pl.pallas_call(kernel, grid=(self.slots,), in_specs=[spec(kind, array.sha...  31 us
    dot_general x13, matrix products, inner_rows(): lax.dot_general(left_side, right_side, (((0,), (0,)), ((), ())), preferre...  30.8 us
    dot_general x10, matrix products, times_transposed(): lax.dot_general(left_side, right_side, (((1,), (1,)), ((), ())), preferre...  30.5 us
    ppermute x21, starting transfers between devices, up(): return lax.ppermute(value, n.dp, [(i, (i + 2) % dp) for i in range(dp)])  29 us
    ppermute x19, waiting for transfers between devices, swap_x(): return lax.ppermute(value, n.dp, [(i, i ^ 1) for i in range(dp)])  27.2 us
  transfers between devices with their start and end apart: 90, of which 29 were waited for; matrix products, arithmetic and copies ran while one was open for 28% of the time, Pallas kernels for 16%

profile of v4, /device:TPU:0, one launch (start us, length us, event | category | flops | bytes accessed | tf_op | source)
XLA Modules:
  0.0 489.4 jit_solution(3047616290114222135)
XLA Ops:
  13.2 12.4 %collective-permute-done.2 = bf16[1,4320]{1,0:T(2,128)(2,1)S(1)} collective-permute-done((bf16[1,4320]{1,0:T(2,128)(2,1)S(1)}, bf16[1,4320]{1,0:T(2,128)(2,1)S(1)}, u32[]{:S(2)}, u32[]{:S(2)}) %collective-permute-start.2) | collective-permute-done | bytes 8672 | tf_op jit(solution)/shard_map/ppermute | solution.py:861
  33.9 13.2 %collective-permute-done.6 = bf16[2,4320]{1,0:T(2,128)(2,1)S(1)} collective-permute-done((bf16[2,4320]{1,0:T(2,128)(2,1)S(1)}, bf16[2,4320]{1,0:T(2,128)(2,1)S(1)}, u32[]{:S(2)}, u32[]{:S(2)}) %collective-permute-start.6) | collective-permute-done | bytes 17312 | tf_op jit(solution)/shard_map/ppermute | solution.py:964
  54.1 14.1 %collective-permute-done.10 = bf16[4,4320]{1,0:T(4,128)(2,1)S(1)} collective-permute-done((bf16[4,4320]{1,0:T(4,128)(2,1)S(1)}, bf16[4,4320]{1,0:T(4,128)(2,1)S(1)}, u32[]{:S(2)}, u32[]{:S(2)}) %collective-permute-start.10) | collective-permute-done | bytes 34592 | tf_op jit(solution)/shard_map/ppermute | solution.py:964
  79.4 10.1 %collective-permute-done.15 = f32[8,6912]{1,0:T(8,128)} collective-permute-done((f32[8,6912]{1,0:T(8,128)}, f32[8,6912]{1,0:T(8,128)}, u32[]{:S(2)}, u32[]{:S(2)}) %collective-permute-start.15) | collective-permute-done | bytes 221216 | tf_op jit(solution)/shard_map/ppermute | solution.py:861
  116.9 5.0 %collective-permute-done.24 = f32[2,6912]{1,0:T(2,128)} collective-permute-done((f32[2,6912]{1,0:T(2,128)S(1)}, f32[2,6912]{1,0:T(2,128)}, u32[]{:S(2)}, u32[]{:S(2)}) %collective-permute-start.24) | collective-permute-done | bytes 55328 | tf_op jit(solution)/shard_map/ppermute | solution.py:964
  134.0 10.1 %shard_map.252 = (bf16[512,1152]{1,0:T(8,128)(2,1)S(1)}, bf16[512,1152]{1,0:T(8,128)(2,1)S(1)}, bf16[512,1152]{1,0:T(8,128)(2,1)S(1)}, bf16[1152,1152]{1,0:T(8,128)(2,1)S(1)}) custom-call(s32[4]{0:T(128)S(1)} %pad_add_fusion.order_ref, bf16[512,1152]{1,0:T(8,128)(2,1)S(1)} %copy-done.26, f32[2,1152]{1,0:T(2,128)S(1)} %copy-done.44, ...), custom_call_target="tpu_custom_call" | custom-call | tf_op jit(solution)/shard_map/pallas_call | solution.py:213
  144.3 5.2 %shard_map.253 = (bf16[512,1152]{1,0:T(8,128)(2,1)S(1)}, f32[512,16]{1,0:T(8,128)S(1)}) custom-call(bf16[512,1152]{1,0:T(8,128)(2,1)S(1)} %get-tuple-element.954.query_ref, bf16[512,1152]{1,0:T(8,128)(2,1)S(1)} %get-tuple-element.955.key_ref, bf16[512,1152]{1,0:T(8,128)(2,1)S(1)} %get-tuple-element.956.value_ref, s32[2,1,256]{2,1,0:T(1,128)S(1)} %broadcast_in_dim.107.mask_ref), custom_call_target="tpu_custom_call" | custom-call | tf_op jit(solution)/shard_map/pallas_call | solution.py:91
  158.5 6.1 %shard_map.255 = (f32[512,1152]{1,0:T(8,128)}, bf16[512,1152]{1,0:T(8,128)(2,1)}) custom-call(bf16[512,1152]{1,0:T(8,128)(2,1)} %copy-done.28, bf16[1152,1152]{1,0:T(8,128)(2,1)} %copy-done.7, f32[1,1152]{1,0:T(1,128)} %get-tuple-element.722.bias_ref, bf16[512,1152]{1,0:T(8,128)(2,1)} %bitcast.140, f32[2,6,1152]{2,1,0:T(8,128)} %get-tuple-element.1021.mod_ref), custom_call_target="tpu_custom_call" | custom-call | tf_op jit(solution)/shard_map/pallas_call | solution.py:524
  164.7 5.6 %fusion.39 = (bf16[512,1152]{1,0:T(8,128)(2,1)S(1)}, f32[512,1152]{1,0:T(8,128)}) fusion(f32[1152]{0:T(1024)S(1)} %get-tuple-element.1158, bf16[512,1152]{1,0:T(8,128)(2,1)} %get-tuple-element.927, bf16[1152,1152]{1,0:T(8,128)(2,1)} %collective-permute-done.25), kind=kOutput, calls=%fused_computation.74 | convolution fusion | flops 1364852736 | bytes 7377408 | tf_op jit(solution)/shard_map/dot_general | solution.py:33
  170.3 5.9 %fusion.47 = (bf16[512,1152]{1,0:T(8,128)(2,1)}, f32[512,1152]{1,0:T(8,128)}) fusion(f32[1152]{0:T(1024)S(1)} %get-tuple-element.1157, bf16[512,1152]{1,0:T(8,128)(2,1)S(1)} %copy-done.79, bf16[1152,1152]{1,0:T(8,128)(2,1)} %bitcast.21), kind=kOutput, calls=%fused_computation.82 | convolution fusion | flops 1364852736 | bytes 7377408 | tf_op jit(solution)/shard_map/dot_general | solution.py:33
  185.6 4.2 fusion.55
  189.8 5.2 %fusion.63 = (bf16[512,1152]{1,0:T(8,128)(2,1)}, f32[512,1152]{1,0:T(8,128)S(1)}) fusion(f32[1152]{0:T(1024)S(1)} %get-tuple-element.1155, bf16[512,1152]{1,0:T(8,128)(2,1)S(1)} %copy-done.80, bf16[1152,1152]{1,0:T(8,128)(2,1)} %bitcast.29), kind=kOutput, calls=%fused_computation.98 | convolution fusion | flops 1364852736 | bytes 7377408 | tf_op jit(solution)/shard_map/dot_general | solution.py:33
  196.8 4.4 collective-permute-done.35.refs_3_.refs_5_
  201.2 3.6 fusion
  217.1 5.1 %fusion.154 = f32[512,1152]{1,0:T(8,128)} fusion(bf16[512,1152]{1,0:T(8,128)(2,1)S(1)} %fusion.10, bf16[1152,1152]{1,0:T(8,128)(2,1)} %bitcast.21), kind=kOutput, calls=%fused_computation.290 | convolution fusion | flops 1358954496 | bytes 6193152 | tf_op jit(solution)/shard_map/dot_general | solution.py:37
  225.2 4.3 collective-permute-start.43
  240.8 5.0 %convolution_add_fusion.9 = f32[512,1152]{1,0:T(8,128)} fusion(f32[512,1152]{1,0:T(8,128)S(1)} %copy-done.90, bf16[512,1152]{1,0:T(8,128)(2,1)S(1)} %fusion.17, bf16[1152,1152]{1,0:T(8,128)(2,1)} %collective-permute-done.25), kind=kOutput, calls=%fused_computation.33 | convolution fusion | flops 1359544320 | bytes 8552448 | tf_op jit(solution)/shard_map/dot_general | solution.py:37
  254.9 3.7 convolution_add_fusion.7
  258.6 6.8 %collective-permute-done.45 = bf16[288,1152]{1,0:T(8,128)(2,1)S(1)} collective-permute-done((bf16[288,1152]{1,0:T(8,128)(2,1)S(1)}, bf16[288,1152]{1,0:T(8,128)(2,1)S(1)}, u32[]{:S(2)}, u32[]{:S(2)}) %collective-permute-start.45) | collective-permute-done | bytes 663584 | tf_op jit(solution)/shard_map/ppermute | solution.py:855
  273.3 5.1 %convolution_add_fusion.5.back_ref = f32[512,1152]{1,0:T(8,128)} fusion(f32[512,1152]{1,0:T(8,128)S(1)} %convolution_add_fusion.7, bf16[512,1152]{1,0:T(8,128)(2,1)S(1)} %fusion.31, bf16[1152,1152]{1,0:T(8,128)(2,1)} %bitcast.29), kind=kOutput, calls=%fused_computation.29 | convolution fusion | flops 1359544320 | bytes 8552448 | tf_op jit(solution)/shard_map/dot_general | solution.py:37
  290.7 7.7 %shard_map.258 = (bf16[512,1152]{1,0:T(8,128)(2,1)}, f32[512,1152]{1,0:T(8,128)}, bf16[512,1152]{1,0:T(8,128)(2,1)}, f32[2,6,1152]{2,1,0:T(8,128)}) custom-call(f32[2]{0:T(128)} %compare_convert_fusion.live_ref, bf16[512,1152]{1,0:T(8,128)(2,1)} %bitcast.141, f32[512,1152]{1,0:T(8,128)} %get-tuple-element.920.branch_ref, ...), custom_call_target="tpu_custom_call" | custom-call | tf_op jit(solution)/shard_map/pallas_call | solution.py:524
  309.0 4.5 collective-permute-start.51
  313.5 13.6 %shard_map.259 = (bf16[512,1152]{1,0:T(8,128)(2,1)S(1)}, bf16[512,1152]{1,0:T(8,128)(2,1)S(1)}, bf16[512,1152]{1,0:T(8,128)(2,1)S(1)}, f32[2,2,1152]{2,1,0:T(2,128)S(1)}) custom-call(bf16[512,1152]{1,0:T(8,128)(2,1)S(1)} %get-tuple-element.954.query_ref, bf16[512,1152]{1,0:T(8,128)(2,1)S(1)} %copy-done.2, bf16[512,1152]{1,0:T(8,128)(2,1)S(1)} %copy-done.4, ...), custom_call_target="tpu_custom_call" | custom-call | tf_op jit(solution)/shard_map/pallas_call | solution.py:152
  330.9 5.9 %collective-permute-done.53 = bf16[288,1152]{1,0:T(8,128)(2,1)S(1)} collective-permute-done((bf16[288,1152]{1,0:T(8,128)(2,1)S(1)}, bf16[288,1152]{1,0:T(8,128)(2,1)S(1)}, u32[]{:S(2)}, u32[]{:S(2)}) %collective-permute-start.53) | collective-permute-done | bytes 663584 | tf_op jit(solution)/shard_map/ppermute | solution.py:864
  339.9 4.3 collective-permute-start.57
  351.0 7.5 %collective-permute-done.57 = bf16[288,1152]{1,0:T(8,128)(2,1)S(1)} collective-permute-done((bf16[288,1152]{1,0:T(8,128)(2,1)S(1)}, bf16[288,1152]{1,0:T(8,128)(2,1)S(1)}, u32[]{:S(2)}, u32[]{:S(2)}) %collective-permute-start.57) | collective-permute-done | bytes 663584 | tf_op jit(solution)/shard_map/ppermute | solution.py:855
  365.4 13.7 %shard_map.260 = (f32[512,1152]{1,0:T(8,128)}, f32[2,2,1152]{2,1,0:T(2,128)}) custom-call(s32[4]{0:T(128)} %copy-done.40, bf16[512,1152]{1,0:T(8,128)(2,1)} %copy-done.23, bf16[512,1152]{1,0:T(8,128)(2,1)} %copy-done.24, bf16[512,1152]{1,0:T(8,128)(2,1)} %copy-done.25, f32[512,1152]{1,0:T(8,128)} %get-tuple-element.1020.middle_slope_ref, ...), custom_call_target="tpu_custom_call" | custom-call | tf_op jit(solution)/shard_map/pallas_call | solution.py:524
  393.8 9.8 %collective-permute-done.63 = bf16[288,1152]{1,0:T(8,128)(2,1)S(1)} collective-permute-done((bf16[288,1152]{1,0:T(8,128)(2,1)S(1)}, bf16[288,1152]{1,0:T(8,128)(2,1)S(1)}, u32[]{:S(2)}, u32[]{:S(2)}) %collective-permute-start.63) | collective-permute-done | bytes 663584 | tf_op jit(solution)/shard_map/ppermute | solution.py:864
  403.6 5.1 %collective-permute-done.62 = bf16[288,1152]{1,0:T(8,128)(2,1)S(1)} collective-permute-done((bf16[288,1152]{1,0:T(8,128)(2,1)S(1)}, bf16[288,1152]{1,0:T(8,128)(2,1)S(1)}, u32[]{:S(2)}, u32[]{:S(2)}) %collective-permute-start.62) | collective-permute-done | bytes 663584 | tf_op jit(solution)/shard_map/ppermute | solution.py:855
  413.0 13.4 %collective-permute-done.70 = bf16[8,12672]{1,0:T(8,128)(2,1)S(1)} collective-permute-done((bf16[8,12672]{1,0:T(8,128)(2,1)S(1)}, bf16[8,12672]{1,0:T(8,128)(2,1)S(1)}, u32[]{:S(2)}, u32[]{:S(2)}) %collective-permute-start.70) | collective-permute-done | bytes 202784 | tf_op jit(solution)/shard_map/ppermute | solution.py:964
  429.9 4.5 collective-permute-done.74
  437.7 7.7 %collective-permute-done.72 = bf16[288,1152]{1,0:T(8,128)(2,1)S(1)} collective-permute-done((bf16[288,1152]{1,0:T(8,128)(2,1)S(1)}, bf16[288,1152]{1,0:T(8,128)(2,1)S(1)}, u32[]{:S(2)}, u32[]{:S(2)}) %collective-permute-start.72) | collective-permute-done | bytes 663584 | tf_op jit(solution)/shard_map/ppermute | solution.py:864
  (498 shorter events, 253.2 us)
Async XLA Ops:
  5.8 20.0 %collective-permute-start = (bf16[2,144,1152]{2,1,0:T(8,128)(2,1)S(1)}, bf16[2,144,1152]{2,1,0:T(8,128)(2,1)S(1)}, u32[]{:S(2)}, u32[]{:S(2)}) collective-permute-start(bf16[2,144,1152]{2,1,0:T(8,128)(2,1)S(1)} %pad_maximum_fusion.1.refs_0_), channel_id=1, source_target_pairs={{0,8},{4,12},{8,16},{12,20},{16,24},{20,28},{24,0},{28,4},{1,9},{5... | collective-permute-start | bytes 1990664 | tf_op jit(solution)/shard_map/ppermute | solution.py:855
  27.8 19.4 %collective-permute-start.5 = (bf16[2,144,1152]{2,1,0:T(8,128)(2,1)}, bf16[2,144,1152]{2,1,0:T(8,128)(2,1)}, u32[]{:S(2)}, u32[]{:S(2)}) collective-permute-start(bf16[2,144,1152]{2,1,0:T(8,128)(2,1)} %broadcast_select_fusion.2), channel_id=1, source_target_pairs={{0,2},{1,3},{2,0},{3,1},{4,6},{5,7},{6,4},{7,5},{8,10},{9,11},{10,... | collective-permute-start | bytes 1990664 | tf_op jit(solution)/shard_map/ppermute | solution.py:864
  48.2 20.7 %collective-permute-start.7 = (bf16[2,144,1152]{2,1,0:T(8,128)(2,1)}, bf16[2,144,1152]{2,1,0:T(8,128)(2,1)}, u32[]{:S(2)}, u32[]{:S(2)}) collective-permute-start(bf16[2,144,1152]{2,1,0:T(8,128)(2,1)} %collective-permute-done.3.refs_2_), channel_id=1, source_target_pairs={{0,8},{4,12},{8,16},{12,20},{16,24},{20,28},{24,0},{28,4},{1,9},{5... | collective-permute-start | bytes 1990664 | tf_op jit(solution)/shard_map/ppermute | solution.py:855
  48.6 20.3 %collective-permute-start.8 = (bf16[2,144,1152]{2,1,0:T(8,128)(2,1)}, bf16[2,144,1152]{2,1,0:T(8,128)(2,1)}, u32[]{:S(2)}, u32[]{:S(2)}) collective-permute-start(bf16[2,144,1152]{2,1,0:T(8,128)(2,1)} %collective-permute-done.3.refs_2_), channel_id=1, source_target_pairs={{0,4},{4,0},{8,12},{12,8},{16,20},{20,16},{24,28},{28,24},{1,5},{5... | collective-permute-start | bytes 1990664 | tf_op jit(solution)/shard_map/ppermute | solution.py:861
  70.0 21.0 %collective-permute-start.11 = (bf16[2,144,1152]{2,1,0:T(8,128)(2,1)}, bf16[2,144,1152]{2,1,0:T(8,128)(2,1)}, u32[]{:S(2)}, u32[]{:S(2)}) collective-permute-start(bf16[2,144,1152]{2,1,0:T(8,128)(2,1)} %collective-permute-done.7.refs_3_), channel_id=1, source_target_pairs={{0,4},{4,0},{8,12},{12,8},{16,20},{20,16},{24,28},{28,24},{1,5},{5... | collective-permute-start | bytes 1990664 | tf_op jit(solution)/shard_map/ppermute | solution.py:861
  71.0 18.6 %collective-permute-start.15 = (f32[8,6912]{1,0:T(8,128)}, f32[8,6912]{1,0:T(8,128)}, u32[]{:S(2)}, u32[]{:S(2)}) collective-permute-start(f32[8,6912]{1,0:T(8,128)} %constant_dynamic-slice_fusion.17), channel_id=1, source_target_pairs={{0,4},{4,0},{8,12},{12,8},{16,20},{20,16},{24,28},{28,24},{1,5},{5... | collective-permute-start | bytes 663560 | tf_op jit(solution)/shard_map/ppermute | solution.py:861
  123.4 27.9 %collective-permute-start.25 = (bf16[1152,1152]{1,0:T(8,128)(2,1)}, bf16[1152,1152]{1,0:T(8,128)(2,1)}, u32[]{:S(2)}, u32[]{:S(2)}) collective-permute-start(bf16[1152,1152]{1,0:T(8,128)(2,1)} %bitcast.21), channel_id=1, source_target_pairs={{0,1},{1,0},{2,3},{3,2},{4,5},{5,4},{6,7},{7,6},{8,9},{9,8},{10,11... | collective-permute-start | bytes 7962632 | tf_op jit(solution)/shard_map/ppermute | solution.py:867
  124.4 26.9 %collective-permute-start.29 = (bf16[2,144,1152]{2,1,0:T(8,128)(2,1)}, bf16[2,144,1152]{2,1,0:T(8,128)(2,1)}, u32[]{:S(2)}, u32[]{:S(2)}) collective-permute-start(bf16[2,144,1152]{2,1,0:T(8,128)(2,1)} %pad_maximum_fusion.2), channel_id=1, source_target_pairs={{0,4},{4,0},{8,12},{12,8},{16,20},{20,16},{24,28},{28,24},{1,5},{5... | collective-permute-start | bytes 1990664 | tf_op jit(solution)/shard_map/ppermute | solution.py:861
  126.2 25.2 %collective-permute-start.26 = (bf16[1,144,1152]{2,1,0:T(8,128)(2,1)}, bf16[1,144,1152]{2,1,0:T(8,128)(2,1)}, u32[]{:S(2)}, u32[]{:S(2)}) collective-permute-start(bf16[1,144,1152]{2,1,0:T(8,128)(2,1)} %collective-permute-done.13.refs_1_), channel_id=1, source_target_pairs={{0,2},{1,3},{2,0},{3,1},{4,6},{5,7},{6,4},{7,5},{8,10},{9,11},{10,... | collective-permute-start | bytes 995336 | tf_op jit(solution)/shard_map/ppermute | solution.py:864
  127.5 23.9 %collective-permute-start.27 = (bf16[1,144,1152]{2,1,0:T(8,128)(2,1)}, bf16[1,144,1152]{2,1,0:T(8,128)(2,1)S(1)}, u32[]{:S(2)}, u32[]{:S(2)}) collective-permute-start(bf16[1,144,1152]{2,1,0:T(8,128)(2,1)} %collective-permute-done.13.refs_1_), channel_id=1, source_target_pairs={{0,8},{4,12},{8,16},{12,20},{16,24},{20,28},{24,0},{28,4},{1,9},{5... | collective-permute-start | bytes 995336 | tf_op jit(solution)/shard_map/ppermute | solution.py:855
  127.6 23.7 %collective-permute-start.28 = (bf16[1,144,1152]{2,1,0:T(8,128)(2,1)}, bf16[1,144,1152]{2,1,0:T(8,128)(2,1)}, u32[]{:S(2)}, u32[]{:S(2)}) collective-permute-start(bf16[1,144,1152]{2,1,0:T(8,128)(2,1)} %get-tuple-element.779.refs_0_), channel_id=1, source_target_pairs={{0,4},{4,0},{8,12},{12,8},{16,20},{20,16},{24,28},{28,24},{1,5},{5... | collective-permute-start | bytes 995336 | tf_op jit(solution)/shard_map/ppermute | solution.py:861
  154.4 26.8 %collective-permute-start.30 = (bf16[1152,1152]{1,0:T(8,128)(2,1)}, bf16[1152,1152]{1,0:T(8,128)(2,1)}, u32[]{:S(2)}, u32[]{:S(2)}) collective-permute-start(bf16[1152,1152]{1,0:T(8,128)(2,1)} %bitcast.29), channel_id=1, source_target_pairs={{0,1},{1,0},{2,3},{3,2},{4,5},{5,4},{6,7},{7,6},{8,9},{9,8},{10,11... | collective-permute-start | bytes 7962632 | tf_op jit(solution)/shard_map/ppermute | solution.py:867
  154.5 25.0 %collective-permute-start.31 = (bf16[1,144,1152]{2,1,0:T(8,128)(2,1)S(1)}, bf16[1,144,1152]{2,1,0:T(8,128)(2,1)S(1)}, u32[]{:S(2)}, u32[]{:S(2)}) collective-permute-start(bf16[1,144,1152]{2,1,0:T(8,128)(2,1)S(1)} %collective-permute-done.27.refs_2_), channel_id=1, source_target_pairs={{0,8},{4,12},{8,16},{12,20},{16,24},{20,28},{24,0},{28,4},{1,9},{5... | collective-permute-start | bytes 995336 | tf_op jit(solution)/shard_map/ppermute | solution.py:855
  154.5 24.9 %collective-permute-start.34 = (bf16[1,144,1152]{2,1,0:T(8,128)(2,1)S(1)}, bf16[1,144,1152]{2,1,0:T(8,128)(2,1)S(1)}, u32[]{:S(2)}, u32[]{:S(2)}) collective-permute-start(bf16[1,144,1152]{2,1,0:T(8,128)(2,1)S(1)} %collective-permute-done.27.refs_2_), channel_id=1, source_target_pairs={{0,4},{4,0},{8,12},{12,8},{16,20},{20,16},{24,28},{28,24},{1,5},{5... | collective-permute-start | bytes 995336 | tf_op jit(solution)/shard_map/ppermute | solution.py:861
  157.4 22.9 %collective-permute-start.32 = (bf16[2,144,1152]{2,1,0:T(8,128)(2,1)S(1)}, bf16[2,144,1152]{2,1,0:T(8,128)(2,1)S(1)}, u32[]{:S(2)}, u32[]{:S(2)}) collective-permute-start(bf16[2,144,1152]{2,1,0:T(8,128)(2,1)S(1)} %pad_maximum_fusion.3), channel_id=1, source_target_pairs={{0,2},{1,3},{2,0},{3,1},{4,6},{5,7},{6,4},{7,5},{8,10},{9,11},{10,... | collective-permute-start | bytes 1990664 | tf_op jit(solution)/shard_map/ppermute | solution.py:864
  158.2 21.3 %collective-permute-start.33 = (bf16[1,144,1152]{2,1,0:T(8,128)(2,1)}, bf16[1,144,1152]{2,1,0:T(8,128)(2,1)S(1)}, u32[]{:S(2)}, u32[]{:S(2)}) collective-permute-start(bf16[1,144,1152]{2,1,0:T(8,128)(2,1)} %collective-permute-done.13.refs_1_), channel_id=1, source_target_pairs={{0,4},{4,0},{8,12},{12,8},{16,20},{20,16},{24,28},{28,24},{1,5},{5... | collective-permute-start | bytes 995336 | tf_op jit(solution)/shard_map/ppermute | solution.py:861
  181.2 20.0 %collective-permute-start.37 = (bf16[1152,1152]{1,0:T(8,128)(2,1)}, bf16[1152,1152]{1,0:T(8,128)(2,1)}, u32[]{:S(2)}, u32[]{:S(2)}) collective-permute-start(bf16[1152,1152]{1,0:T(8,128)(2,1)} %convolution_convert_fusion.7), channel_id=1, source_target_pairs={{0,1},{1,0},{2,3},{3,2},{4,5},{5,4},{6,7},{7,6},{8,9},{9,8},{10,11... | collective-permute-start | bytes 7962632 | tf_op jit(solution)/shard_map/ppermute | solution.py:867
  204.8 18.5 %collective-permute-start.40 = (bf16[288,1152]{1,0:T(8,128)(2,1)S(1)}, bf16[288,1152]{1,0:T(8,128)(2,1)S(1)}, u32[]{:S(2)}, u32[]{:S(2)}) collective-permute-start(bf16[288,1152]{1,0:T(8,128)(2,1)S(1)} %constant_dynamic-slice_fusion.10), channel_id=1, source_target_pairs={{0,8},{4,12},{8,16},{12,20},{16,24},{20,28},{24,0},{28,4},{1,9},{5... | collective-permute-start | bytes 1990664 | tf_op jit(solution)/shard_map/ppermute | solution.py:855
  225.2 20.7 %collective-permute-start.43 = (bf16[288,1152]{1,0:T(8,128)(2,1)S(1)}, bf16[288,1152]{1,0:T(8,128)(2,1)S(1)}, u32[]{:S(2)}, u32[]{:S(2)}) collective-permute-start(bf16[288,1152]{1,0:T(8,128)(2,1)S(1)} %add_convert_fusion.17), channel_id=1, source_target_pairs={{0,8},{4,12},{8,16},{12,20},{16,24},{20,28},{24,0},{28,4},{1,9},{5... | collective-permute-start | bytes 1990664 | tf_op jit(solution)/shard_map/ppermute | solution.py:855
  246.0 19.4 %collective-permute-start.45 = (bf16[288,1152]{1,0:T(8,128)(2,1)S(1)}, bf16[288,1152]{1,0:T(8,128)(2,1)S(1)}, u32[]{:S(2)}, u32[]{:S(2)}) collective-permute-start(bf16[288,1152]{1,0:T(8,128)(2,1)S(1)} %add_convert_fusion.16), channel_id=1, source_target_pairs={{0,8},{4,12},{8,16},{12,20},{16,24},{20,28},{24,0},{28,4},{1,9},{5... | collective-permute-start | bytes 1990664 | tf_op jit(solution)/shard_map/ppermute | solution.py:855
  246.4 19.0 %collective-permute-start.44 = (bf16[1152,1152]{1,0:T(8,128)(2,1)S(1)}, bf16[1152,1152]{1,0:T(8,128)(2,1)S(1)}, u32[]{:S(2)}, u32[]{:S(2)}) collective-permute-start(bf16[1152,1152]{1,0:T(8,128)(2,1)S(1)} %convolution_convert_fusion.5), channel_id=1, source_target_pairs={{0,1},{1,0},{2,3},{3,2},{4,5},{5,4},{6,7},{7,6},{8,9},{9,8},{10,11... | collective-permute-start | bytes 7962632 | tf_op jit(solution)/shard_map/ppermute | solution.py:867
  266.1 18.4 %collective-permute-start.48 = (bf16[288,1152]{1,0:T(8,128)(2,1)S(1)}, bf16[288,1152]{1,0:T(8,128)(2,1)S(1)}, u32[]{:S(2)}, u32[]{:S(2)}) collective-permute-start(bf16[288,1152]{1,0:T(8,128)(2,1)S(1)} %constant_dynamic-slice_fusion.8), channel_id=1, source_target_pairs={{0,8},{4,12},{8,16},{12,20},{16,24},{20,28},{24,0},{28,4},{1,9},{5... | collective-permute-start | bytes 1990664 | tf_op jit(solution)/shard_map/ppermute | solution.py:855
  285.5 18.3 %collective-permute-start.50 = (bf16[288,1152]{1,0:T(8,128)(2,1)}, bf16[288,1152]{1,0:T(8,128)(2,1)}, u32[]{:S(2)}, u32[]{:S(2)}) collective-permute-start(bf16[288,1152]{1,0:T(8,128)(2,1)} %add_convert_fusion.14), channel_id=1, source_target_pairs={{0,8},{4,12},{8,16},{12,20},{16,24},{20,28},{24,0},{28,4},{1,9},{5... | collective-permute-start | bytes 1990664 | tf_op jit(solution)/shard_map/ppermute | solution.py:855
  306.2 24.7 %collective-permute-start.54 = (bf16[288,1152]{1,0:T(8,128)(2,1)S(1)}, bf16[288,1152]{1,0:T(8,128)(2,1)S(1)}, u32[]{:S(2)}, u32[]{:S(2)}) collective-permute-start(bf16[288,1152]{1,0:T(8,128)(2,1)S(1)} %add_convert_fusion.12), channel_id=1, source_target_pairs={{0,8},{4,12},{8,16},{12,20},{16,24},{20,28},{24,0},{28,4},{1,9},{5... | collective-permute-start | bytes 1990664 | tf_op jit(solution)/shard_map/ppermute | solution.py:855
  306.7 24.3 %collective-permute-start.52 = (bf16[288,1152]{1,0:T(8,128)(2,1)S(1)}, bf16[288,1152]{1,0:T(8,128)(2,1)S(1)}, u32[]{:S(2)}, u32[]{:S(2)}) collective-permute-start(bf16[288,1152]{1,0:T(8,128)(2,1)S(1)} %get-tuple-element.1160), channel_id=1, source_target_pairs={{0,2},{1,3},{2,0},{3,1},{4,6},{5,7},{6,4},{7,5},{8,10},{9,11},{10,... | collective-permute-start | bytes 1990664 | tf_op jit(solution)/shard_map/ppermute | solution.py:864
  308.0 28.9 %collective-permute-start.53 = (bf16[288,1152]{1,0:T(8,128)(2,1)S(1)}, bf16[288,1152]{1,0:T(8,128)(2,1)S(1)}, u32[]{:S(2)}, u32[]{:S(2)}) collective-permute-start(bf16[288,1152]{1,0:T(8,128)(2,1)S(1)} %get-tuple-element.1159), channel_id=1, source_target_pairs={{0,2},{1,3},{2,0},{3,1},{4,6},{5,7},{6,4},{7,5},{8,10},{9,11},{10,... | collective-permute-start | bytes 1990664 | tf_op jit(solution)/shard_map/ppermute | solution.py:864
  309.0 28.1 %collective-permute-start.51 = (bf16[288,1152]{1,0:T(8,128)(2,1)S(1)}, bf16[288,1152]{1,0:T(8,128)(2,1)S(1)}, u32[]{:S(2)}, u32[]{:S(2)}) collective-permute-start(bf16[288,1152]{1,0:T(8,128)(2,1)S(1)} %add_convert_fusion.13), channel_id=1, source_target_pairs={{0,8},{4,12},{8,16},{12,20},{16,24},{20,28},{24,0},{28,4},{1,9},{5... | collective-permute-start | bytes 1990664 | tf_op jit(solution)/shard_map/ppermute | solution.py:855
  337.1 23.6 %collective-permute-start.55 = (bf16[1152,1152]{1,0:T(8,128)(2,1)S(1)}, bf16[1152,1152]{1,0:T(8,128)(2,1)S(1)}, u32[]{:S(2)}, u32[]{:S(2)}) collective-permute-start(bf16[1152,1152]{1,0:T(8,128)(2,1)S(1)} %convolution_convert_fusion.3), channel_id=1, source_target_pairs={{0,1},{1,0},{2,3},{3,2},{4,5},{5,4},{6,7},{7,6},{8,9},{9,8},{10,11... | collective-permute-start | bytes 7962632 | tf_op jit(solution)/shard_map/ppermute | solution.py:867
  337.1 23.6 %collective-permute-start.56 = (bf16[1152,1152]{1,0:T(8,128)(2,1)S(1)}, bf16[1152,1152]{1,0:T(8,128)(2,1)S(1)}, u32[]{:S(2)}, u32[]{:S(2)}) collective-permute-start(bf16[1152,1152]{1,0:T(8,128)(2,1)S(1)} %convolution_convert_fusion.2), channel_id=1, source_target_pairs={{0,1},{1,0},{2,3},{3,2},{4,5},{5,4},{6,7},{7,6},{8,9},{9,8},{10,11... | collective-permute-start | bytes 7962632 | tf_op jit(solution)/shard_map/ppermute | solution.py:867
  339.9 18.6 %collective-permute-start.57 = (bf16[288,1152]{1,0:T(8,128)(2,1)S(1)}, bf16[288,1152]{1,0:T(8,128)(2,1)S(1)}, u32[]{:S(2)}, u32[]{:S(2)}) collective-permute-start(bf16[288,1152]{1,0:T(8,128)(2,1)S(1)} %add_convert_fusion.11), channel_id=1, source_target_pairs={{0,8},{4,12},{8,16},{12,20},{16,24},{20,28},{24,0},{28,4},{1,9},{5... | collective-permute-start | bytes 1990664 | tf_op jit(solution)/shard_map/ppermute | solution.py:855
  362.3 20.4 %collective-permute-start.61 = (bf16[288,1152]{1,0:T(8,128)(2,1)}, bf16[288,1152]{1,0:T(8,128)(2,1)}, u32[]{:S(2)}, u32[]{:S(2)}) collective-permute-start(bf16[288,1152]{1,0:T(8,128)(2,1)} %add_convert_fusion.8), channel_id=1, source_target_pairs={{0,8},{4,12},{8,16},{12,20},{16,24},{20,28},{24,0},{28,4},{1,9},{5... | collective-permute-start | bytes 1990664 | tf_op jit(solution)/shard_map/ppermute | solution.py:855
  364.2 18.5 %collective-permute-start.60 = (bf16[288,1152]{1,0:T(8,128)(2,1)}, bf16[288,1152]{1,0:T(8,128)(2,1)}, u32[]{:S(2)}, u32[]{:S(2)}) collective-permute-start(bf16[288,1152]{1,0:T(8,128)(2,1)} %add_convert_fusion.9), channel_id=1, source_target_pairs={{0,2},{1,3},{2,0},{3,1},{4,6},{5,7},{6,4},{7,5},{8,10},{9,11},{10,... | collective-permute-start | bytes 1990664 | tf_op jit(solution)/shard_map/ppermute | solution.py:864
  (151 other events, 1532.5 us)

commit v5 on v4

--- a/solution.py
+++ b/solution.py
@@ -190,52 +190,54 @@
     return copies
 
 
-def project_kernel(
-    order_ref, normed_ref, bias_ref, *refs
+def begin_kernel(
+    order_ref, live_ref, terms_ref, bias_ref, hidden_ref, cotangent_ref, attend_bias_ref, *refs
 ):
-    units, outs, last_ref, held, sems = refs[:4], refs[4:7], refs[7], refs[8], refs[9]
-    for copy in fetch(units, held, sems, order_ref):
+    units = refs[:4]
+    normed_ref, slope_ref, mod_ref, query_ref, key_ref, value_ref = refs[4:10]
+    last_ref, held, sems = refs[10:]
+    copies = fetch(units, held, sems, order_ref)
+    slots, _, width = mod_ref.shape
+    patches = hidden_ref.shape[0] // slots
+    for slot in range(slots):
+        rows = slice(slot * patches, (slot + 1) * patches)
+        modulation = terms_ref[slot : slot + 1, :] + bias_ref[...]
+        cuts = [modulation[:, i * width : (i + 1) * width] for i in range(6)]
+        for i in range(6):
+            mod_ref[slot, i : i + 1] = cuts[i]
+        normed = norm_parts(hidden_ref[rows, :].astype(jnp.float32))[0]
+        normed_ref[rows, :] = low(normed * (1.0 + cuts[1]) + cuts[0])
+        slope = cotangent_ref[rows, :].astype(jnp.float32) * live_ref[slot]
+        slope_ref[rows, :] = low(slope * cuts[5])
+    for copy in copies:
         copy.wait()
     copy = pltpu.make_async_copy(held.at[3], last_ref, sems.at[4])
     copy.start()
-    for index, row in ((0, 0), (1, None), (2, 1)):
-        value = times(normed_ref[...], held[index])
-        if row is not None:
-            value = value + bias_ref[row : row + 1, :]
-        outs[index][...] = low(value)
+    query_ref[...] = low(times(normed_ref[...], held[0]) + attend_bias_ref[0:1, :])
+    key_ref[...] = low(times(normed_ref[...], held[1]))
+    value_ref[...] = low(times(normed_ref[...], held[2]) + attend_bias_ref[1:2, :])
     copy.wait()
 
 
-def project(normed, units, order, bias):
-    rows, width = normed.shape
+def begin(order, live, terms, bias, hidden, cotangent, attend_bias, units):
+    rows, width = hidden.shape
     vmem = pl.BlockSpec(memory_space=pltpu.VMEM)
+    smem = pl.BlockSpec(memory_space=pltpu.SMEM)
     anywhere = pl.BlockSpec(memory_space=pl.ANY)
+    whole = jax.ShapeDtypeStruct((rows, width), jnp.bfloat16)
     return pl.pallas_call(
-        project_kernel,
-        in_specs=[pl.BlockSpec(memory_space=pltpu.SMEM), vmem, vmem] + [anywhere] * 4,
-        out_specs=[vmem] * 3 + [anywhere],
-        out_shape=[jax.ShapeDtypeStruct((rows, width), jnp.bfloat16)] * 3
+        begin_kernel,
+        in_specs=[smem, smem] + [vmem] * 5 + [anywhere] * 4,
+        out_specs=[vmem] * 6 + [anywhere],
+        out_shape=[whole, whole, jax.ShapeDtypeStruct((live.shape[0], 6, width), jnp.float32)]
+        + [whole] * 3
         + [jax.ShapeDtypeStruct((width, width), jnp.bfloat16)],
         scratch_shapes=[
             pltpu.VMEM((4, width, width), jnp.bfloat16),
             pltpu.SemaphoreType.DMA((5,)),
         ],
         compiler_params=pltpu.CompilerParams(vmem_limit_bytes=40 << 20),
-    )(jnp.stack(order).astype(jnp.int32), normed, bias, *units)
-
-
-def start_kernel(
-    live_ref, terms_ref, bias_ref, hidden_ref, cotangent_ref, normed_ref, slope_ref, mod_ref
-):
-    slot = pl.program_id(0)
-    width = hidden_ref.shape[1]
-    modulation = terms_ref[pl.ds(slot, 1), :] + bias_ref[...]
-    cuts = [modulation[:, i * width : (i + 1) * width] for i in range(6)]
-    for i in range(6):
-        mod_ref[0, i : i + 1] = cuts[i]
-    normed = norm_parts(hidden_ref[...].astype(jnp.float32))[0]
-    normed_ref[...] = low(normed * (1.0 + cuts[1]) + cuts[0])
-    slope_ref[...] = low(cotangent_ref[...].astype(jnp.float32) * live_ref[slot] * cuts[5])
+    )(jnp.stack(order).astype(jnp.int32), live, terms, bias, hidden, cotangent, attend_bias, *units)
 
 
 def middle_kernel(attended_ref, weight_ref, bias_ref, hidden_ref, mod_ref, branch_ref, normed_ref):
@@ -291,21 +293,24 @@
     mod_ref,
     *refs,
 ):
-    units, out_ref, slopes_ref, held, sems = refs[:4], refs[4], refs[5], refs[6], refs[7]
-
-    @pl.when(pl.program_id(0) == 0)
-    def _():
-        for copy in fetch(units, held, sems, order_ref):
-            copy.wait()
-
-    scale_one = mod_ref[0, 1:2]
-    back = times_transposed(query_ref[...], held[0])
-    back += times_transposed(key_ref[...], held[1])
-    back += times_transposed(value_ref[...], held[2])
-    normed, inverse = norm_parts(hidden_ref[...].astype(jnp.float32))
-    slopes_ref[0, 0:1] = patch_sums(back)
-    slopes_ref[0, 1:2] = patch_sums(back * normed)
-    out_ref[...] = middle_slope_ref[...] + norm_back(normed, inverse, back * (1.0 + scale_one))
+    units, out_ref, slopes_ref, held, sems = refs[:4], *refs[4:]
+    for copy in fetch(units, held, sems, order_ref):
+        copy.wait()
+    out_ref[...] = times_transposed(query_ref[...], held[0])
+    out_ref[...] += times_transposed(key_ref[...], held[1])
+    out_ref[...] += times_transposed(value_ref[...], held[2])
+    slots = mod_ref.shape[0]
+    patches = hidden_ref.shape[0] // slots
+    for slot in range(slots):
+        rows = slice(slot * patches, (slot + 1) * patches)
+        normed, inverse = norm_parts(hidden_ref[rows, :].astype(jnp.float32))
+        back = out_ref[rows, :]
+        slopes_ref[slot, 0:1] = patch_sums(back)
+        slopes_ref[slot, 1:2] = patch_sums(back * normed)
+        scale_one = mod_ref[slot, 1:2]
+        out_ref[rows, :] = middle_slope_ref[rows, :] + norm_back(
+            normed, inverse, back * (1.0 + scale_one)
+        )
 
 
 def assemble_kernel(place_ref, *refs):
@@ -484,25 +489,12 @@
     def flat(self, values):
         return values.reshape(self.rows, self.width)
 
-    def start(self, terms, bias):
-        return self.per_image(
-            start_kernel,
-            [("rows", jnp.bfloat16), ("rows", jnp.bfloat16), (6, jnp.float32)],
-            [
-                ("scalar", self.live),
-                ("all", terms),
-                ("all", bias),
-                ("rows", self.hidden),
-                ("rows", self.flat(self.cotangent)),
-            ],
-        )
-
-    def attention(self, normed_one, units, order, attend_bias):
-        queries, keys_all, values_all, output_full = project(
-            normed_one, units, order, attend_bias
-        )
-        attended, logs = attend(queries, keys_all, values_all, self.patch_mask)
-        return queries, keys_all, values_all, output_full, attended, logs
+    def begin(self, order, terms, bias, attend_bias, *units):
+        cotangent = self.flat(self.cotangent)
+        return begin(order, self.live, terms, bias, self.hidden, cotangent, attend_bias, units)
+
+    def attention(self, queries, keys_all, values_all):
+        return attend(queries, keys_all, values_all, self.patch_mask)
 
     def per_image(self, kernel, outs, ins, scratch=()):
         rows = pl.BlockSpec((self.patches, self.width), lambda slot: (slot, 0))
@@ -585,18 +577,23 @@
         return attend_back(queries, keys_all, values_all, slopes, self.patch_mask, logs)
 
     def start_back(self, slopes, units, order, middle_slope, modulation):
-        gradient, first_slopes = self.per_image(
+        vmem = pl.BlockSpec(memory_space=pltpu.VMEM)
+        gradient, first_slopes = pl.pallas_call(
             start_back_kernel,
-            [("rows", jnp.float32), (2, jnp.float32)],
-            [("scalar", jnp.stack(order).astype(jnp.int32))]
-            + [("rows", slope) for slope in slopes]
-            + [("rows", middle_slope), ("rows", self.hidden), ("mod", modulation)]
-            + [("any", unit) for unit in units],
-            [
+            in_specs=[pl.BlockSpec(memory_space=pltpu.SMEM)]
+            + [vmem] * 6
+            + [pl.BlockSpec(memory_space=pl.ANY)] * 4,
+            out_specs=[vmem] * 2,
+            out_shape=[
+                jax.ShapeDtypeStruct(self.whole, jnp.float32),
+                jax.ShapeDtypeStruct((self.slots, 2, self.width), jnp.float32),
+            ],
+            scratch_shapes=[
                 pltpu.VMEM((4, self.width, self.width), jnp.bfloat16),
                 pltpu.SemaphoreType.DMA((4,)),
             ],
-        )
+            compiler_params=pltpu.CompilerParams(vmem_limit_bytes=48 << 20),
+        )(jnp.stack(order).astype(jnp.int32), *slopes, middle_slope, self.hidden, modulation, *units)
         return gradient.reshape(self.hidden_in.shape), first_slopes
 
     def condition_back(self, slope):
@@ -728,14 +725,13 @@
     expand_biases = biases[3].reshape(4, dp, shard).transpose(1, 0, 2).reshape(4, width)
     terms = times(act_rows(conditions, here, shard), modulation_weight)
     terms = lax.psum_scatter(terms, "dp", scatter_dimension=0, tiled=True)
-    normed_one, shrink_slope, modulation = layer.start(terms, biases[0])
     weights = whole(jnp.concatenate([attend_weight, output_weight], 1))
     weights = [weights[:, unit * width : (unit + 1) * width] for unit in range(4)]
     natural = [jnp.int32(unit) for unit in range(4)]
     expand_full, shrink_full = whole(expand_weight), whole(shrink_weight)
-    queries, keys_all, values_all, output_full, attended, logs = layer.attention(
-        normed_one, weights, natural, biases[1]
-    )
+    begun = layer.begin(natural, terms, biases[0], biases[1], *weights)
+    normed_one, shrink_slope, modulation, queries, keys_all, values_all, output_full = begun
+    attended, logs = layer.attention(queries, keys_all, values_all)
     branch, normed_two = layer.middle(attended, output_full, biases[2], modulation)
     totals = ()
     expand_terms, shrink_terms, inner_sums = [], [], []
@@ -945,7 +941,7 @@
         )
 
     for name, stream, row, tick in (
-        (n.Aown, n.AB, 0, 4), (n.Bown, n.AB, 1, 5), (n.Cown, n.C, 0, 9)
+        (n.Aown, n.AB, 0, 4), (n.Bown, n.AB, 1, 5)
     ):
         parts = tuple((str(stream) + str(step)) for step in range(4))
         parts += tuple((str(stream) + n.x + str(step)) for step in range(4))
@@ -957,7 +953,6 @@
     at(5, n.Acy, n.Ay, swap_core)
     at(6, n.Bc, n.Bown, swap_core)
     at(7, n.Bcy, n.By, swap_core)
-    at(9, n.Cc, n.Cown, swap_core)
     at(10, n.Ccy, n.Cy, swap_core)
 
     def swap_z(distance, value):
@@ -1017,11 +1012,11 @@
     terms = shrink_terms(3, n.terms, (n.x,))
     terms = shrink_terms(4, terms, (n.near,))
     terms = shrink_terms(5, terms, (n.far,))
-    at(6, (n.n1, n.gm, n.mod), (terms, n.mod_bias), layer.start)
 
     units_a = (n.Aown, n.Ay, n.Ac, n.Acy)
-    at(6, (n.q, n.k, n.v, n.O, n.att, n.logs), (n.n1, n.att_bias) + units_a,
-       lambda n1, bias, *units: layer.attention(n1, units, order, bias))
+    at(6, (n.n1, n.gm, n.mod, n.q, n.k, n.v, n.O), (terms, n.mod_bias, n.att_bias) + units_a,
+       partial(layer.begin, order))
+    at(6, (n.att, n.logs), (n.q, n.k, n.v), layer.attention)
     at(7, (n.branch, n.n2), (n.att, n.O, n.out_bias, n.mod), layer.middle)
 
     def expand(index, n2, weight, biases):
@@ -1033,13 +1028,16 @@
             total = total + value.astype(jnp.float32)
         return low(total)
 
-    for index, (name, tick) in enumerate(((n.own, 7), (n.y, 8), (n.c, 7), (n.cy, 8))):
+    for index, (name, tick) in enumerate(((n.own, 8), (n.y, 8), (n.c, 7), (n.cy, 8))):
         at(tick, ((n.in_ + str(name)), (n.act_ + str(name))), (n.n2, (n.B + str(name)), n.exp_bias), partial(expand, index))
     at(7, n.dC_c, (n.act_c, n.gm), term)
     at(8, n.dC_cy, (n.act_cy, n.gm), term)
     at(9, n.dC_own, (n.act_own, n.gm, n.dC_rc), term)
-    at(10, n.dC_y, (n.act_y, n.gm, n.dC_rcy), term)
-
+    at(11, n.dC_y, (n.act_y, n.gm, n.dC_rcy), term)
+
+    at(9, n.Cown, (n.C0, n.C1, n.C2, n.C3, n.Cx0, n.Cx1, n.Cx2, n.Cx3, n.dC_own),
+       lambda *parts: own_unit(0, *lax.optimization_barrier(parts)[:8]))
+    at(9, n.Cc, n.Cown, swap_core)
     total = ()
     for index, (name, tick) in enumerate(((n.own, 9), (n.c, 10), (n.cy, 11), (n.y, 12))):
         ins = ((n.in_ + str(name)), (n.act_ + str(name)), n.gm, (n.B + str(name)), (n.C + str(name))) + total
@@ -1067,6 +1065,7 @@
 
     at(16, (n.gradient_hidden, n.first), (n.gq, n.gk, n.gv, n.middle_slope, n.mod) + units_a,
        lambda a, b, c, ms, mod, *units: layer.start_back((a, b, c), units, order, ms, mod))
+
 
     def slab(step, moved, count, *values):
         first = below(step) * (2 * shard)

time: 496 us -> 485 us (0.978)
  waiting for transfers between devices: 141 us -> 132 us
    pallas_call x4 -> x2, Pallas kernels: 31 us -> 13.8 us  [per_image(): pl.pallas_call(kernel, grid=(self.slots,), in_specs=[spec(kind, array.sha...]
    pallas_call x1 -> x2, Pallas kernels: 10.1 us -> 23.9 us  [the longest x1 13.5 us: start_back(): pl.pallas_call(start_back_kernel, in_specs=[pl.BlockSpec(memory_space=plt...]
    unnamed x187 -> x195, local copies, waits for them, and re-layouts: 11.8 us -> 14.4 us
  transfers between devices with their start and end apart: 90 -> 90, of which waited for: 29 -> 30; matrix products, arithmetic and copies ran while one was open for 28% -> 28% of each run, Pallas kernels for 16% -> 16%
where the time goes in v5:
time: 485 us; the launch traced here: 478 us
  waiting for transfers between devices  132 us (27%)
  matrix products  95.4 us (20%)
  starting transfers between devices  92.1 us (19%)
  Pallas kernels  83.9 us (17%)
  other arithmetic  40.2 us (8%)
  local copies, waits for them, and re-layouts  31.5 us (6%)
    ppermute x9, waiting for transfers between devices, swap_z(): return lax.ppermute(value, n.dp, [(i, i ^ 2 * distance) for i in range(dp)])  45.8 us
    dot_general x14, matrix products, times(): return jnp.dot(left_side, right_side, preferred_element_type=jnp.float32)  35.7 us
    ppermute x21, waiting for transfers between devices, swap_y(): return lax.ppermute(value, n.rep, [(i, i ^ 2) for i in range(4)])  34.1 us
    dot_general x13, matrix products, inner_rows(): lax.dot_general(left_side, right_side, (((0,), (0,)), ((), ())), preferre...  30.7 us
    ppermute x21, starting transfers between devices, up(): return lax.ppermute(value, n.dp, [(i, (i + 2) % dp) for i in range(dp)])  30.5 us
    dot_general x10, matrix products, times_transposed(): lax.dot_general(left_side, right_side, (((1,), (1,)), ((), ())), preferre...  29 us
    ppermute x19, waiting for transfers between devices, swap_x(): return lax.ppermute(value, n.dp, [(i, i ^ 1) for i in range(dp)])  27.4 us
    convert_element_type x28, other arithmetic, low(): return values.astype(jnp.bfloat16)  26.4 us
  transfers between devices with their start and end apart: 90, of which 30 were waited for; matrix products, arithmetic and copies ran while one was open for 28% of the time, Pallas kernels for 16%

profile of v5, /device:TPU:0, one launch (start us, length us, event | category | flops | bytes accessed | tf_op | source)
XLA Modules:
  0.0 478.3 jit_solution(11059021553889571478)
XLA Ops:
  13.2 12.4 %collective-permute-done.2 = bf16[1,4320]{1,0:T(2,128)(2,1)S(1)} collective-permute-done((bf16[1,4320]{1,0:T(2,128)(2,1)S(1)}, bf16[1,4320]{1,0:T(2,128)(2,1)S(1)}, u32[]{:S(2)}, u32[]{:S(2)}) %collective-permute-start.2) | collective-permute-done | bytes 8672 | tf_op jit(solution)/shard_map/ppermute | solution.py:857
  34.2 13.1 %collective-permute-done.6 = bf16[2,4320]{1,0:T(2,128)(2,1)S(1)} collective-permute-done((bf16[2,4320]{1,0:T(2,128)(2,1)S(1)}, bf16[2,4320]{1,0:T(2,128)(2,1)S(1)}, u32[]{:S(2)}, u32[]{:S(2)}) %collective-permute-start.6) | collective-permute-done | bytes 17312 | tf_op jit(solution)/shard_map/ppermute | solution.py:959
  54.4 14.1 %collective-permute-done.10 = bf16[4,4320]{1,0:T(4,128)(2,1)S(1)} collective-permute-done((bf16[4,4320]{1,0:T(4,128)(2,1)S(1)}, bf16[4,4320]{1,0:T(4,128)(2,1)S(1)}, u32[]{:S(2)}, u32[]{:S(2)}) %collective-permute-start.10) | collective-permute-done | bytes 34592 | tf_op jit(solution)/shard_map/ppermute | solution.py:959
  79.7 10.1 %collective-permute-done.15 = f32[8,6912]{1,0:T(8,128)} collective-permute-done((f32[8,6912]{1,0:T(8,128)}, f32[8,6912]{1,0:T(8,128)}, u32[]{:S(2)}, u32[]{:S(2)}) %collective-permute-start.15) | collective-permute-done | bytes 221216 | tf_op jit(solution)/shard_map/ppermute | solution.py:857
  130.2 10.4 %shard_map.251 = (bf16[512,1152]{1,0:T(8,128)(2,1)S(1)}, bf16[512,1152]{1,0:T(8,128)(2,1)S(1)}, f32[2,6,1152]{2,1,0:T(8,128)S(1)}, bf16[512,1152]{1,0:T(8,128)(2...) custom-call(s32[4]{0:T(128)S(1)} %pad_add_fusion.order_ref, ...), custom_call_target="tpu_custom_call" | custom-call | tf_op jit(solution)/shard_map/pallas_call | solution.py:228
  143.3 5.2 %shard_map.252 = (bf16[512,1152]{1,0:T(8,128)(2,1)S(1)}, f32[512,16]{1,0:T(8,128)S(1)}) custom-call(bf16[512,1152]{1,0:T(8,128)(2,1)S(1)} %get-tuple-element.966.query_ref, bf16[512,1152]{1,0:T(8,128)(2,1)S(1)} %get-tuple-element.967.key_ref, bf16[512,1152]{1,0:T(8,128)(2,1)S(1)} %get-tuple-element.968.value_ref, s32[2,1,256]{2,1,0:T(1,128)S(1)} %broadcast_in_dim.107.mask_ref), custom_call_target="tpu_custom_call" | custom-call | tf_op jit(solution)/shard_map/pallas_call | solution.py:91
  158.2 6.1 %shard_map.254 = (f32[512,1152]{1,0:T(8,128)}, bf16[512,1152]{1,0:T(8,128)(2,1)}) custom-call(bf16[512,1152]{1,0:T(8,128)(2,1)} %copy-done.28, bf16[1152,1152]{1,0:T(8,128)(2,1)} %copy-done.14, f32[1,1152]{1,0:T(1,128)} %get-tuple-element.728.bias_ref, bf16[512,1152]{1,0:T(8,128)(2,1)} %bitcast.133, f32[2,6,1152]{2,1,0:T(8,128)} %copy-done.30), custom_call_target="tpu_custom_call" | custom-call | tf_op jit(solution)/shard_map/pallas_call | solution.py:516
  164.4 5.6 %fusion.39 = (bf16[512,1152]{1,0:T(8,128)(2,1)S(1)}, f32[512,1152]{1,0:T(8,128)}) fusion(f32[1152]{0:T(1024)S(1)} %fusion.119, bf16[512,1152]{1,0:T(8,128)(2,1)} %get-tuple-element.939, bf16[1152,1152]{1,0:T(8,128)(2,1)} %collective-permute-done.25), kind=kOutput, calls=%fused_computation.74 | convolution fusion | flops 1364852736 | bytes 7377408 | tf_op jit(solution)/shard_map/dot_general | solution.py:33
  178.5 4.1 fusion.47
  182.6 5.2 %fusion.63 = (bf16[512,1152]{1,0:T(8,128)(2,1)}, f32[512,1152]{1,0:T(8,128)S(1)}) fusion(f32[1152]{0:T(1024)S(1)} %get-tuple-element.1167, bf16[512,1152]{1,0:T(8,128)(2,1)S(1)} %copy-done.84, bf16[1152,1152]{1,0:T(8,128)(2,1)} %bitcast.29), kind=kOutput, calls=%fused_computation.98 | convolution fusion | flops 1364852736 | bytes 7377408 | tf_op jit(solution)/shard_map/dot_general | solution.py:33
  187.8 3.8 fusion.55
  194.1 3.6 fusion
  210.1 5.0 %fusion.154 = f32[512,1152]{1,0:T(8,128)} fusion(bf16[512,1152]{1,0:T(8,128)(2,1)S(1)} %fusion.10, bf16[1152,1152]{1,0:T(8,128)(2,1)} %bitcast.21), kind=kOutput, calls=%fused_computation.290 | convolution fusion | flops 1358954496 | bytes 6193152 | tf_op jit(solution)/shard_map/dot_general | solution.py:37
  218.2 3.4 collective-permute-start.43
  232.6 3.6 convolution_add_fusion.9
  248.1 3.6 convolution_add_fusion.7
  251.8 4.1 collective-permute-done.45
  263.8 5.1 %convolution_add_fusion.5.back_ref = f32[512,1152]{1,0:T(8,128)} fusion(f32[512,1152]{1,0:T(8,128)S(1)} %convolution_add_fusion.7, bf16[512,1152]{1,0:T(8,128)(2,1)S(1)} %fusion.31, bf16[1152,1152]{1,0:T(8,128)(2,1)} %bitcast.29), kind=kOutput, calls=%fused_computation.29 | convolution fusion | flops 1359544320 | bytes 8552448 | tf_op jit(solution)/shard_map/dot_general | solution.py:37
  280.0 7.7 %shard_map.257 = (bf16[512,1152]{1,0:T(8,128)(2,1)}, f32[512,1152]{1,0:T(8,128)}, bf16[512,1152]{1,0:T(8,128)(2,1)}, f32[2,6,1152]{2,1,0:T(8,128)}) custom-call(f32[2]{0:T(128)} %copy-done.50, bf16[512,1152]{1,0:T(8,128)(2,1)} %bitcast.134, f32[512,1152]{1,0:T(8,128)} %get-tuple-element.932.branch_ref, f32[512,1152]{1,0:T(8,128)} %convolution_add_fusion.4.out_ref, ...), custom_call_target="tpu_custom_call" | custom-call | tf_op jit(solution)/shard_map/pallas_call | solution.py:516
  299.7 4.5 collective-permute-start.51
  304.2 13.6 %shard_map.258 = (bf16[512,1152]{1,0:T(8,128)(2,1)S(1)}, bf16[512,1152]{1,0:T(8,128)(2,1)S(1)}, bf16[512,1152]{1,0:T(8,128)(2,1)S(1)}, f32[2,2,1152]{2,1,0:T(2,128)S(1)}) custom-call(bf16[512,1152]{1,0:T(8,128)(2,1)S(1)} %copy-done.7, bf16[512,1152]{1,0:T(8,128)(2,1)S(1)} %copy-done.9, bf16[512,1152]{1,0:T(8,128)(2,1)S(1)} %copy-done.11, ...), custom_call_target="tpu_custom_call" | custom-call | tf_op jit(solution)/shard_map/pallas_call | solution.py:152
  321.7 4.9 %collective-permute-done.53 = bf16[288,1152]{1,0:T(8,128)(2,1)S(1)} collective-permute-done((bf16[288,1152]{1,0:T(8,128)(2,1)S(1)}, bf16[288,1152]{1,0:T(8,128)(2,1)S(1)}, u32[]{:S(2)}, u32[]{:S(2)}) %collective-permute-start.53) | collective-permute-done | bytes 663584 | tf_op jit(solution)/shard_map/ppermute | solution.py:860
  329.5 4.4 collective-permute-start.57
  337.2 3.5 convolution_convert_fusion.1
  340.6 7.4 %collective-permute-done.57 = bf16[288,1152]{1,0:T(8,128)(2,1)S(1)} collective-permute-done((bf16[288,1152]{1,0:T(8,128)(2,1)S(1)}, bf16[288,1152]{1,0:T(8,128)(2,1)S(1)}, u32[]{:S(2)}, u32[]{:S(2)}) %collective-permute-start.57) | collective-permute-done | bytes 663584 | tf_op jit(solution)/shard_map/ppermute | solution.py:851
  354.6 13.5 %shard_map.259 = (f32[512,1152]{1,0:T(8,128)}, f32[2,2,1152]{2,1,0:T(2,128)S(1)}) custom-call(s32[4]{0:T(128)S(1)} %pad_add_fusion.order_ref, bf16[512,1152]{1,0:T(8,128)(2,1)S(1)} %get-tuple-element.1029.query_ref, bf16[512,1152]{1,0:T(8,128)(2,1)S(1)} %get-tuple-element.1030.key_ref, bf16[512,1152]{1,0:T(8,128)(2,1)S(1)} %get-tuple-element.1031.value_ref, ...), custom_call_target="tpu_custom_call" | custom-call | tf_op jit(solution)/shard_map/pallas_call | solution.py:581
  371.9 3.6 collective-permute-start.66
  382.4 9.5 %collective-permute-done.63 = bf16[288,1152]{1,0:T(8,128)(2,1)S(1)} collective-permute-done((bf16[288,1152]{1,0:T(8,128)(2,1)S(1)}, bf16[288,1152]{1,0:T(8,128)(2,1)S(1)}, u32[]{:S(2)}, u32[]{:S(2)}) %collective-permute-start.63) | collective-permute-done | bytes 663584 | tf_op jit(solution)/shard_map/ppermute | solution.py:860
  392.0 4.7 collective-permute-done.62
  402.0 12.6 %collective-permute-done.70 = bf16[8,12672]{1,0:T(8,128)(2,1)S(1)} collective-permute-done((bf16[8,12672]{1,0:T(8,128)(2,1)S(1)}, bf16[8,12672]{1,0:T(8,128)(2,1)S(1)}, u32[]{:S(2)}, u32[]{:S(2)}) %collective-permute-start.70) | collective-permute-done | bytes 202784 | tf_op jit(solution)/shard_map/ppermute | solution.py:959
  418.0 4.7 collective-permute-done.74
  426.1 7.8 %collective-permute-done.72 = bf16[288,1152]{1,0:T(8,128)(2,1)S(1)} collective-permute-done((bf16[288,1152]{1,0:T(8,128)(2,1)S(1)}, bf16[288,1152]{1,0:T(8,128)(2,1)S(1)}, u32[]{:S(2)}, u32[]{:S(2)}) %collective-permute-start.72) | collective-permute-done | bytes 663584 | tf_op jit(solution)/shard_map/ppermute | solution.py:860
  (505 shorter events, 253.8 us)
Async XLA Ops:
  5.8 20.0 %collective-permute-start = (bf16[2,144,1152]{2,1,0:T(8,128)(2,1)S(1)}, bf16[2,144,1152]{2,1,0:T(8,128)(2,1)S(1)}, u32[]{:S(2)}, u32[]{:S(2)}) collective-permute-start(bf16[2,144,1152]{2,1,0:T(8,128)(2,1)S(1)} %pad_maximum_fusion.1.refs_0_), channel_id=1, source_target_pairs={{0,8},{4,12},{8,16},{12,20},{16,24},{20,28},{24,0},{28,4},{1,9},{5... | collective-permute-start | bytes 1990664 | tf_op jit(solution)/shard_map/ppermute | solution.py:851
  28.0 19.4 %collective-permute-start.5 = (bf16[2,144,1152]{2,1,0:T(8,128)(2,1)}, bf16[2,144,1152]{2,1,0:T(8,128)(2,1)}, u32[]{:S(2)}, u32[]{:S(2)}) collective-permute-start(bf16[2,144,1152]{2,1,0:T(8,128)(2,1)} %broadcast_select_fusion.2), channel_id=1, source_target_pairs={{0,2},{1,3},{2,0},{3,1},{4,6},{5,7},{6,4},{7,5},{8,10},{9,11},{10,... | collective-permute-start | bytes 1990664 | tf_op jit(solution)/shard_map/ppermute | solution.py:860
  48.4 20.7 %collective-permute-start.7 = (bf16[2,144,1152]{2,1,0:T(8,128)(2,1)}, bf16[2,144,1152]{2,1,0:T(8,128)(2,1)}, u32[]{:S(2)}, u32[]{:S(2)}) collective-permute-start(bf16[2,144,1152]{2,1,0:T(8,128)(2,1)} %collective-permute-done.3.refs_2_), channel_id=1, source_target_pairs={{0,8},{4,12},{8,16},{12,20},{16,24},{20,28},{24,0},{28,4},{1,9},{5... | collective-permute-start | bytes 1990664 | tf_op jit(solution)/shard_map/ppermute | solution.py:851
  48.8 20.3 %collective-permute-start.8 = (bf16[2,144,1152]{2,1,0:T(8,128)(2,1)}, bf16[2,144,1152]{2,1,0:T(8,128)(2,1)}, u32[]{:S(2)}, u32[]{:S(2)}) collective-permute-start(bf16[2,144,1152]{2,1,0:T(8,128)(2,1)} %collective-permute-done.3.refs_2_), channel_id=1, source_target_pairs={{0,4},{4,0},{8,12},{12,8},{16,20},{20,16},{24,28},{28,24},{1,5},{5... | collective-permute-start | bytes 1990664 | tf_op jit(solution)/shard_map/ppermute | solution.py:857
  50.3 18.1 %collective-permute-start.10 = (bf16[4,4320]{1,0:T(4,128)(2,1)S(1)}, bf16[4,4320]{1,0:T(4,128)(2,1)S(1)}, u32[]{:S(2)}, u32[]{:S(2)}) collective-permute-start(bf16[4,4320]{1,0:T(4,128)(2,1)S(1)} %maximum_select_fusion.1), channel_id=1, source_target_pairs={{0,16},{4,20},{8,24},{12,28},{16,0},{20,4},{24,8},{28,12},{1,17},{... | collective-permute-start | bytes 103688 | tf_op jit(solution)/shard_map/ppermute | solution.py:959
  70.3 21.0 %collective-permute-start.11 = (bf16[2,144,1152]{2,1,0:T(8,128)(2,1)}, bf16[2,144,1152]{2,1,0:T(8,128)(2,1)}, u32[]{:S(2)}, u32[]{:S(2)}) collective-permute-start(bf16[2,144,1152]{2,1,0:T(8,128)(2,1)} %collective-permute-done.7.refs_3_), channel_id=1, source_target_pairs={{0,4},{4,0},{8,12},{12,8},{16,20},{20,16},{24,28},{28,24},{1,5},{5... | collective-permute-start | bytes 1990664 | tf_op jit(solution)/shard_map/ppermute | solution.py:857
  71.2 18.6 %collective-permute-start.15 = (f32[8,6912]{1,0:T(8,128)}, f32[8,6912]{1,0:T(8,128)}, u32[]{:S(2)}, u32[]{:S(2)}) collective-permute-start(f32[8,6912]{1,0:T(8,128)} %constant_dynamic-slice_fusion.17), channel_id=1, source_target_pairs={{0,4},{4,0},{8,12},{12,8},{16,20},{20,16},{24,28},{28,24},{1,5},{5... | collective-permute-start | bytes 663560 | tf_op jit(solution)/shard_map/ppermute | solution.py:857
  122.7 27.6 %collective-permute-start.25 = (bf16[1152,1152]{1,0:T(8,128)(2,1)}, bf16[1152,1152]{1,0:T(8,128)(2,1)}, u32[]{:S(2)}, u32[]{:S(2)}) collective-permute-start(bf16[1152,1152]{1,0:T(8,128)(2,1)} %bitcast.21), channel_id=1, source_target_pairs={{0,1},{1,0},{2,3},{3,2},{4,5},{5,4},{6,7},{7,6},{8,9},{9,8},{10,11... | collective-permute-start | bytes 7962632 | tf_op jit(solution)/shard_map/ppermute | solution.py:863
  123.7 26.5 %collective-permute-start.29 = (bf16[2,144,1152]{2,1,0:T(8,128)(2,1)}, bf16[2,144,1152]{2,1,0:T(8,128)(2,1)}, u32[]{:S(2)}, u32[]{:S(2)}) collective-permute-start(bf16[2,144,1152]{2,1,0:T(8,128)(2,1)} %pad_maximum_fusion.2), channel_id=1, source_target_pairs={{0,4},{4,0},{8,12},{12,8},{16,20},{20,16},{24,28},{28,24},{1,5},{5... | collective-permute-start | bytes 1990664 | tf_op jit(solution)/shard_map/ppermute | solution.py:857
  125.5 24.8 %collective-permute-start.26 = (bf16[1,144,1152]{2,1,0:T(8,128)(2,1)}, bf16[1,144,1152]{2,1,0:T(8,128)(2,1)}, u32[]{:S(2)}, u32[]{:S(2)}) collective-permute-start(bf16[1,144,1152]{2,1,0:T(8,128)(2,1)} %collective-permute-done.13.refs_1_), channel_id=1, source_target_pairs={{0,2},{1,3},{2,0},{3,1},{4,6},{5,7},{6,4},{7,5},{8,10},{9,11},{10,... | collective-permute-start | bytes 995336 | tf_op jit(solution)/shard_map/ppermute | solution.py:860
  126.8 23.5 %collective-permute-start.27 = (bf16[1,144,1152]{2,1,0:T(8,128)(2,1)}, bf16[1,144,1152]{2,1,0:T(8,128)(2,1)S(1)}, u32[]{:S(2)}, u32[]{:S(2)}) collective-permute-start(bf16[1,144,1152]{2,1,0:T(8,128)(2,1)} %collective-permute-done.13.refs_1_), channel_id=1, source_target_pairs={{0,8},{4,12},{8,16},{12,20},{16,24},{20,28},{24,0},{28,4},{1,9},{5... | collective-permute-start | bytes 995336 | tf_op jit(solution)/shard_map/ppermute | solution.py:851
  126.9 23.3 %collective-permute-start.28 = (bf16[1,144,1152]{2,1,0:T(8,128)(2,1)}, bf16[1,144,1152]{2,1,0:T(8,128)(2,1)}, u32[]{:S(2)}, u32[]{:S(2)}) collective-permute-start(bf16[1,144,1152]{2,1,0:T(8,128)(2,1)} %get-tuple-element.794.refs_0_), channel_id=1, source_target_pairs={{0,4},{4,0},{8,12},{12,8},{16,20},{20,16},{24,28},{28,24},{1,5},{5... | collective-permute-start | bytes 995336 | tf_op jit(solution)/shard_map/ppermute | solution.py:857
  153.3 20.7 %collective-permute-start.30 = (bf16[1152,1152]{1,0:T(8,128)(2,1)}, bf16[1152,1152]{1,0:T(8,128)(2,1)}, u32[]{:S(2)}, u32[]{:S(2)}) collective-permute-start(bf16[1152,1152]{1,0:T(8,128)(2,1)} %bitcast.29), channel_id=1, source_target_pairs={{0,1},{1,0},{2,3},{3,2},{4,5},{5,4},{6,7},{7,6},{8,9},{9,8},{10,11... | collective-permute-start | bytes 7962632 | tf_op jit(solution)/shard_map/ppermute | solution.py:863
  153.4 19.8 %collective-permute-start.31 = (bf16[1,144,1152]{2,1,0:T(8,128)(2,1)S(1)}, bf16[1,144,1152]{2,1,0:T(8,128)(2,1)S(1)}, u32[]{:S(2)}, u32[]{:S(2)}) collective-permute-start(bf16[1,144,1152]{2,1,0:T(8,128)(2,1)S(1)} %collective-permute-done.27.refs_2_), channel_id=1, source_target_pairs={{0,8},{4,12},{8,16},{12,20},{16,24},{20,28},{24,0},{28,4},{1,9},{5... | collective-permute-start | bytes 995336 | tf_op jit(solution)/shard_map/ppermute | solution.py:851
  154.3 18.9 %collective-permute-start.34 = (bf16[1,144,1152]{2,1,0:T(8,128)(2,1)S(1)}, bf16[1,144,1152]{2,1,0:T(8,128)(2,1)S(1)}, u32[]{:S(2)}, u32[]{:S(2)}) collective-permute-start(bf16[1,144,1152]{2,1,0:T(8,128)(2,1)S(1)} %collective-permute-done.27.refs_2_), channel_id=1, source_target_pairs={{0,4},{4,0},{8,12},{12,8},{16,20},{20,16},{24,28},{28,24},{1,5},{5... | collective-permute-start | bytes 995336 | tf_op jit(solution)/shard_map/ppermute | solution.py:857
  174.1 20.0 %collective-permute-start.37 = (bf16[1152,1152]{1,0:T(8,128)(2,1)}, bf16[1152,1152]{1,0:T(8,128)(2,1)}, u32[]{:S(2)}, u32[]{:S(2)}) collective-permute-start(bf16[1152,1152]{1,0:T(8,128)(2,1)} %convolution_convert_fusion.7), channel_id=1, source_target_pairs={{0,1},{1,0},{2,3},{3,2},{4,5},{5,4},{6,7},{7,6},{8,9},{9,8},{10,11... | collective-permute-start | bytes 7962632 | tf_op jit(solution)/shard_map/ppermute | solution.py:863
  174.1 19.2 %collective-permute-start.36 = (bf16[1,144,1152]{2,1,0:T(8,128)(2,1)}, bf16[1,144,1152]{2,1,0:T(8,128)(2,1)S(1)}, u32[]{:S(2)}, u32[]{:S(2)}) collective-permute-start(bf16[1,144,1152]{2,1,0:T(8,128)(2,1)} %copy-done.19), channel_id=1, source_target_pairs={{0,4},{4,0},{8,12},{12,8},{16,20},{20,16},{24,28},{28,24},{1,5},{5... | collective-permute-start | bytes 995336 | tf_op jit(solution)/shard_map/ppermute | solution.py:857
  197.8 18.4 %collective-permute-start.40 = (bf16[288,1152]{1,0:T(8,128)(2,1)S(1)}, bf16[288,1152]{1,0:T(8,128)(2,1)S(1)}, u32[]{:S(2)}, u32[]{:S(2)}) collective-permute-start(bf16[288,1152]{1,0:T(8,128)(2,1)S(1)} %constant_dynamic-slice_fusion.10), channel_id=1, source_target_pairs={{0,8},{4,12},{8,16},{12,20},{16,24},{20,28},{24,0},{28,4},{1,9},{5... | collective-permute-start | bytes 1990664 | tf_op jit(solution)/shard_map/ppermute | solution.py:851
  218.2 18.1 %collective-permute-start.43 = (bf16[288,1152]{1,0:T(8,128)(2,1)S(1)}, bf16[288,1152]{1,0:T(8,128)(2,1)S(1)}, u32[]{:S(2)}, u32[]{:S(2)}) collective-permute-start(bf16[288,1152]{1,0:T(8,128)(2,1)S(1)} %add_convert_fusion.17), channel_id=1, source_target_pairs={{0,8},{4,12},{8,16},{12,20},{16,24},{20,28},{24,0},{28,4},{1,9},{5... | collective-permute-start | bytes 1990664 | tf_op jit(solution)/shard_map/ppermute | solution.py:851
  236.5 19.4 %collective-permute-start.45 = (bf16[288,1152]{1,0:T(8,128)(2,1)S(1)}, bf16[288,1152]{1,0:T(8,128)(2,1)S(1)}, u32[]{:S(2)}, u32[]{:S(2)}) collective-permute-start(bf16[288,1152]{1,0:T(8,128)(2,1)S(1)} %add_convert_fusion.16), channel_id=1, source_target_pairs={{0,8},{4,12},{8,16},{12,20},{16,24},{20,28},{24,0},{28,4},{1,9},{5... | collective-permute-start | bytes 1990664 | tf_op jit(solution)/shard_map/ppermute | solution.py:851
  256.5 18.5 %collective-permute-start.48 = (bf16[288,1152]{1,0:T(8,128)(2,1)S(1)}, bf16[288,1152]{1,0:T(8,128)(2,1)S(1)}, u32[]{:S(2)}, u32[]{:S(2)}) collective-permute-start(bf16[288,1152]{1,0:T(8,128)(2,1)S(1)} %constant_dynamic-slice_fusion.8), channel_id=1, source_target_pairs={{0,8},{4,12},{8,16},{12,20},{16,24},{20,28},{24,0},{28,4},{1,9},{5... | collective-permute-start | bytes 1990664 | tf_op jit(solution)/shard_map/ppermute | solution.py:851
  257.0 18.1 %collective-permute-start.46 = (bf16[1152,1152]{1,0:T(8,128)(2,1)S(1)}, bf16[1152,1152]{1,0:T(8,128)(2,1)S(1)}, u32[]{:S(2)}, u32[]{:S(2)}) collective-permute-start(bf16[1152,1152]{1,0:T(8,128)(2,1)S(1)} %convolution_convert_fusion.4), channel_id=1, source_target_pairs={{0,1},{1,0},{2,3},{3,2},{4,5},{5,4},{6,7},{7,6},{8,9},{9,8},{10,11... | collective-permute-start | bytes 7962632 | tf_op jit(solution)/shard_map/ppermute | solution.py:863
  295.8 25.9 %collective-permute-start.54 = (bf16[288,1152]{1,0:T(8,128)(2,1)S(1)}, bf16[288,1152]{1,0:T(8,128)(2,1)S(1)}, u32[]{:S(2)}, u32[]{:S(2)}) collective-permute-start(bf16[288,1152]{1,0:T(8,128)(2,1)S(1)} %add_convert_fusion.12), channel_id=1, source_target_pairs={{0,8},{4,12},{8,16},{12,20},{16,24},{20,28},{24,0},{28,4},{1,9},{5... | collective-permute-start | bytes 1990664 | tf_op jit(solution)/shard_map/ppermute | solution.py:851
  296.3 25.4 %collective-permute-start.52 = (bf16[288,1152]{1,0:T(8,128)(2,1)S(1)}, bf16[288,1152]{1,0:T(8,128)(2,1)S(1)}, u32[]{:S(2)}, u32[]{:S(2)}) collective-permute-start(bf16[288,1152]{1,0:T(8,128)(2,1)S(1)} %get-tuple-element.1171), channel_id=1, source_target_pairs={{0,2},{1,3},{2,0},{3,1},{4,6},{5,7},{6,4},{7,5},{8,10},{9,11},{10,... | collective-permute-start | bytes 1990664 | tf_op jit(solution)/shard_map/ppermute | solution.py:860
  297.7 28.9 %collective-permute-start.53 = (bf16[288,1152]{1,0:T(8,128)(2,1)S(1)}, bf16[288,1152]{1,0:T(8,128)(2,1)S(1)}, u32[]{:S(2)}, u32[]{:S(2)}) collective-permute-start(bf16[288,1152]{1,0:T(8,128)(2,1)S(1)} %get-tuple-element.1170), channel_id=1, source_target_pairs={{0,2},{1,3},{2,0},{3,1},{4,6},{5,7},{6,4},{7,5},{8,10},{9,11},{10,... | collective-permute-start | bytes 1990664 | tf_op jit(solution)/shard_map/ppermute | solution.py:860
  299.7 26.9 %collective-permute-start.51 = (bf16[288,1152]{1,0:T(8,128)(2,1)S(1)}, bf16[288,1152]{1,0:T(8,128)(2,1)S(1)}, u32[]{:S(2)}, u32[]{:S(2)}) collective-permute-start(bf16[288,1152]{1,0:T(8,128)(2,1)S(1)} %add_convert_fusion.13), channel_id=1, source_target_pairs={{0,8},{4,12},{8,16},{12,20},{16,24},{20,28},{24,0},{28,4},{1,9},{5... | collective-permute-start | bytes 1990664 | tf_op jit(solution)/shard_map/ppermute | solution.py:851
  326.6 23.6 %collective-permute-start.55 = (bf16[1152,1152]{1,0:T(8,128)(2,1)S(1)}, bf16[1152,1152]{1,0:T(8,128)(2,1)S(1)}, u32[]{:S(2)}, u32[]{:S(2)}) collective-permute-start(bf16[1152,1152]{1,0:T(8,128)(2,1)S(1)} %convolution_convert_fusion.3), channel_id=1, source_target_pairs={{0,1},{1,0},{2,3},{3,2},{4,5},{5,4},{6,7},{7,6},{8,9},{9,8},{10,11... | collective-permute-start | bytes 7962632 | tf_op jit(solution)/shard_map/ppermute | solution.py:863
  326.6 23.6 %collective-permute-start.56 = (bf16[1152,1152]{1,0:T(8,128)(2,1)S(1)}, bf16[1152,1152]{1,0:T(8,128)(2,1)S(1)}, u32[]{:S(2)}, u32[]{:S(2)}) collective-permute-start(bf16[1152,1152]{1,0:T(8,128)(2,1)S(1)} %convolution_convert_fusion.2), channel_id=1, source_target_pairs={{0,1},{1,0},{2,3},{3,2},{4,5},{5,4},{6,7},{7,6},{8,9},{9,8},{10,11... | collective-permute-start | bytes 7962632 | tf_op jit(solution)/shard_map/ppermute | solution.py:863
  329.5 18.6 %collective-permute-start.57 = (bf16[288,1152]{1,0:T(8,128)(2,1)S(1)}, bf16[288,1152]{1,0:T(8,128)(2,1)S(1)}, u32[]{:S(2)}, u32[]{:S(2)}) collective-permute-start(bf16[288,1152]{1,0:T(8,128)(2,1)S(1)} %add_convert_fusion.11), channel_id=1, source_target_pairs={{0,8},{4,12},{8,16},{12,20},{16,24},{20,28},{24,0},{28,4},{1,9},{5... | collective-permute-start | bytes 1990664 | tf_op jit(solution)/shard_map/ppermute | solution.py:851
  351.5 19.6 %collective-permute-start.61 = (bf16[288,1152]{1,0:T(8,128)(2,1)}, bf16[288,1152]{1,0:T(8,128)(2,1)}, u32[]{:S(2)}, u32[]{:S(2)}) collective-permute-start(bf16[288,1152]{1,0:T(8,128)(2,1)} %add_convert_fusion.8), channel_id=1, source_target_pairs={{0,8},{4,12},{8,16},{12,20},{16,24},{20,28},{24,0},{28,4},{1,9},{5... | collective-permute-start | bytes 1990664 | tf_op jit(solution)/shard_map/ppermute | solution.py:851
  353.2 17.9 %collective-permute-start.60 = (bf16[288,1152]{1,0:T(8,128)(2,1)}, bf16[288,1152]{1,0:T(8,128)(2,1)}, u32[]{:S(2)}, u32[]{:S(2)}) collective-permute-start(bf16[288,1152]{1,0:T(8,128)(2,1)} %add_convert_fusion.9), channel_id=1, source_target_pairs={{0,2},{1,3},{2,0},{3,1},{4,6},{5,7},{6,4},{7,5},{8,10},{9,11},{10,... | collective-permute-start | bytes 1990664 | tf_op jit(solution)/shard_map/ppermute | solution.py:860
  396.7 17.9 %collective-permute-start.70 = (bf16[8,12672]{1,0:T(8,128)(2,1)S(1)}, bf16[8,12672]{1,0:T(8,128)(2,1)S(1)}, u32[]{:S(2)}, u32[]{:S(2)}) collective-permute-start(bf16[8,12672]{1,0:T(8,128)(2,1)S(1)} %pad_maximum_fusion.7), channel_id=1, source_target_pairs={{0,8},{4,12},{8,0},{12,4},{16,24},{20,28},{24,16},{28,20},{1,9},{5... | collective-permute-start | bytes 608264 | tf_op jit(solution)/shard_map/ppermute | solution.py:959
  (155 other events, 1864.9 us)

commit v6 on v5

--- a/solution.py
+++ b/solution.py
@@ -1031,7 +1031,7 @@
     for index, (name, tick) in enumerate(((n.own, 8), (n.y, 8), (n.c, 7), (n.cy, 8))):
         at(tick, ((n.in_ + str(name)), (n.act_ + str(name))), (n.n2, (n.B + str(name)), n.exp_bias), partial(expand, index))
     at(7, n.dC_c, (n.act_c, n.gm), term)
-    at(8, n.dC_cy, (n.act_cy, n.gm), term)
+    at(9, n.dC_cy, (n.act_cy, n.gm), term)
     at(9, n.dC_own, (n.act_own, n.gm, n.dC_rc), term)
     at(11, n.dC_y, (n.act_y, n.gm, n.dC_rcy), term)
 
@@ -1115,7 +1115,7 @@
         at(late + 1, (str(name) + n._3), (str(name) + n._1), swap_core)
         return late + 2
 
-    for name, tick_one, tick_two in ((n.dC, 8, 9), (n.dB, 11, 12), (n.dA, 15, 15)):
+    for name, tick_one, tick_two in ((n.dC, 8, 10), (n.dB, 11, 12), (n.dA, 15, 15)):
         at(tick_one, (str(name) + n._rc), (str(name) + n._c), swap_core)
         at(tick_two, (str(name) + n._rcy), (str(name) + n._cy), swap_core)
     end_c = wide(n.dC, 9, 12, 20)

time: 485 us -> 496 us (1.023)
  waiting for transfers between devices: 132 us -> 150 us
  starting transfers between devices: 92.1 us -> 75.3 us
  local copies, waits for them, and re-layouts: 31.5 us -> 39.1 us
    ppermute x21, waiting for transfers between devices: 24.6 us -> 37 us  [up(): return lax.ppermute(value, n.dp, [(i, (i + 2) % dp) for i in range(dp)])]
    ppermute x21, starting transfers between devices: 30.5 us -> 19.8 us  [up(): return lax.ppermute(value, n.dp, [(i, (i + 2) % dp) for i in range(dp)])]
    unnamed x195 -> x213, local copies, waits for them, and re-layouts: 14.4 us -> 16.3 us
  transfers between devices with their start and end apart: 90 -> 90, of which waited for: 30 -> 34; matrix products, arithmetic and copies ran while one was open for 28% -> 30% of each run, Pallas kernels for 16% -> 15%
where the time goes in v6:
time: 496 us; the launch traced here: 490 us
  waiting for transfers between devices  150 us (30%)
  matrix products  98.3 us (20%)
  Pallas kernels  83.3 us (17%)
  starting transfers between devices  75.3 us (15%)
  other arithmetic  40.2 us (8%)
  local copies, waits for them, and re-layouts  39.1 us (8%)
    ppermute x9, waiting for transfers between devices, swap_z(): return lax.ppermute(value, n.dp, [(i, i ^ 2 * distance) for i in range(dp)])  44.6 us
    ppermute x21, waiting for transfers between devices, swap_y(): return lax.ppermute(value, n.rep, [(i, i ^ 2) for i in range(4)])  38 us
    ppermute x21, waiting for transfers between devices, up(): return lax.ppermute(value, n.dp, [(i, (i + 2) % dp) for i in range(dp)])  37 us
    dot_general x14, matrix products, times(): return jnp.dot(left_side, right_side, preferred_element_type=jnp.float32)  35.7 us
    dot_general x13, matrix products, inner_rows(): lax.dot_general(left_side, right_side, (((0,), (0,)), ((), ())), preferre...  32.1 us
    dot_general x10, matrix products, times_transposed(): lax.dot_general(left_side, right_side, (((1,), (1,)), ((), ())), preferre...  30.6 us
    ppermute x19, waiting for transfers between devices, swap_x(): return lax.ppermute(value, n.dp, [(i, i ^ 1) for i in range(dp)])  28.2 us
    convert_element_type x28, other arithmetic, low(): return values.astype(jnp.bfloat16)  26.3 us
  transfers between devices with their start and end apart: 90, of which 34 were waited for; matrix products, arithmetic and copies ran while one was open for 30% of the time, Pallas kernels for 15%

profile of v6, /device:TPU:0, one launch (start us, length us, event | category | flops | bytes accessed | tf_op | source)
XLA Modules:
  0.0 489.6 jit_solution(2903477482463557550)
XLA Ops:
  13.2 10.9 %collective-permute-done.2 = bf16[1,4320]{1,0:T(2,128)(2,1)S(1)} collective-permute-done((bf16[1,4320]{1,0:T(2,128)(2,1)S(1)}, bf16[1,4320]{1,0:T(2,128)(2,1)S(1)}, u32[]{:S(2)}, u32[]{:S(2)}) %collective-permute-start.2) | collective-permute-done | bytes 8672 | tf_op jit(solution)/shard_map/ppermute | solution.py:857
  32.9 12.9 %collective-permute-done.6 = bf16[2,4320]{1,0:T(2,128)(2,1)S(1)} collective-permute-done((bf16[2,4320]{1,0:T(2,128)(2,1)S(1)}, bf16[2,4320]{1,0:T(2,128)(2,1)S(1)}, u32[]{:S(2)}, u32[]{:S(2)}) %collective-permute-start.6) | collective-permute-done | bytes 17312 | tf_op jit(solution)/shard_map/ppermute | solution.py:959
  54.4 13.5 %collective-permute-done.10 = bf16[4,4320]{1,0:T(4,128)(2,1)S(1)} collective-permute-done((bf16[4,4320]{1,0:T(4,128)(2,1)S(1)}, bf16[4,4320]{1,0:T(4,128)(2,1)S(1)}, u32[]{:S(2)}, u32[]{:S(2)}) %collective-permute-start.10) | collective-permute-done | bytes 34592 | tf_op jit(solution)/shard_map/ppermute | solution.py:959
  80.3 7.0 %collective-permute-done.15 = f32[8,6912]{1,0:T(8,128)S(1)} collective-permute-done((f32[8,6912]{1,0:T(8,128)S(1)}, f32[8,6912]{1,0:T(8,128)S(1)}, u32[]{:S(2)}, u32[]{:S(2)}) %collective-permute-start.15) | collective-permute-done | bytes 221216 | tf_op jit(solution)/shard_map/ppermute | solution.py:857
  132.0 10.4 %shard_map.251 = (bf16[512,1152]{1,0:T(8,128)(2,1)S(1)}, bf16[512,1152]{1,0:T(8,128)(2,1)S(1)}, f32[2,6,1152]{2,1,0:T(8,128)S(1)}, bf16[512,1152]{1,0:T(8,128)(2...) custom-call(s32[4]{0:T(128)S(1)} %pad_add_fusion.order_ref, ...), custom_call_target="tpu_custom_call" | custom-call | tf_op jit(solution)/shard_map/pallas_call | solution.py:228
  145.1 5.2 %shard_map.252 = (bf16[512,1152]{1,0:T(8,128)(2,1)S(1)}, f32[512,16]{1,0:T(8,128)S(1)}) custom-call(bf16[512,1152]{1,0:T(8,128)(2,1)S(1)} %get-tuple-element.964.query_ref, bf16[512,1152]{1,0:T(8,128)(2,1)S(1)} %get-tuple-element.965.key_ref, bf16[512,1152]{1,0:T(8,128)(2,1)S(1)} %get-tuple-element.966.value_ref, s32[2,1,256]{2,1,0:T(1,128)S(1)} %broadcast_in_dim.107.mask_ref), custom_call_target="tpu_custom_call" | custom-call | tf_op jit(solution)/shard_map/pallas_call | solution.py:91
  159.6 5.9 %shard_map.254 = (f32[512,1152]{1,0:T(8,128)}, bf16[512,1152]{1,0:T(8,128)(2,1)}) custom-call(bf16[512,1152]{1,0:T(8,128)(2,1)} %copy-done.32, bf16[1152,1152]{1,0:T(8,128)(2,1)} %copy-done.16, f32[1,1152]{1,0:T(1,128)} %get-tuple-element.727.bias_ref, bf16[512,1152]{1,0:T(8,128)(2,1)} %bitcast.133, f32[2,6,1152]{2,1,0:T(8,128)} %copy-done.34), custom_call_target="tpu_custom_call" | custom-call | tf_op jit(solution)/shard_map/pallas_call | solution.py:516
  165.6 5.6 %fusion.39 = (bf16[512,1152]{1,0:T(8,128)(2,1)S(1)}, f32[512,1152]{1,0:T(8,128)}) fusion(f32[1152]{0:T(1024)S(1)} %fusion.119, bf16[512,1152]{1,0:T(8,128)(2,1)} %get-tuple-element.937, bf16[1152,1152]{1,0:T(8,128)(2,1)} %collective-permute-done.25), kind=kOutput, calls=%fused_computation.74 | convolution fusion | flops 1364852736 | bytes 7377408 | tf_op jit(solution)/shard_map/dot_general | solution.py:33
  179.2 5.2 %fusion.63 = (bf16[512,1152]{1,0:T(8,128)(2,1)}, f32[512,1152]{1,0:T(8,128)S(1)}) fusion(f32[1152]{0:T(1024)S(1)} %get-tuple-element.1165, bf16[512,1152]{1,0:T(8,128)(2,1)} %get-tuple-element.937, bf16[1152,1152]{1,0:T(8,128)(2,1)} %bitcast.29), kind=kOutput, calls=%fused_computation.98 | convolution fusion | flops 1364852736 | bytes 7377408 | tf_op jit(solution)/shard_map/dot_general | solution.py:33
  184.4 3.7 fusion.55
  188.2 3.8 fusion.47
  196.2 3.5 fusion
  211.2 5.1 %fusion.154 = f32[512,1152]{1,0:T(8,128)} fusion(bf16[512,1152]{1,0:T(8,128)(2,1)S(1)} %fusion.10, bf16[1152,1152]{1,0:T(8,128)(2,1)} %bitcast.21), kind=kOutput, calls=%fused_computation.290 | convolution fusion | flops 1358954496 | bytes 6193152 | tf_op jit(solution)/shard_map/dot_general | solution.py:37
  232.1 5.1 %convolution_add_fusion.9 = f32[512,1152]{1,0:T(8,128)} fusion(f32[512,1152]{1,0:T(8,128)S(1)} %copy-done.104, bf16[512,1152]{1,0:T(8,128)(2,1)S(1)} %fusion.17, bf16[1152,1152]{1,0:T(8,128)(2,1)} %collective-permute-done.25), kind=kOutput, calls=%fused_computation.33 | convolution fusion | flops 1359544320 | bytes 8552448 | tf_op jit(solution)/shard_map/dot_general | solution.py:37
  250.0 3.7 convolution_add_fusion.7
  253.7 4.0 collective-permute-done.45
  267.0 5.1 %convolution_add_fusion.5.back_ref = f32[512,1152]{1,0:T(8,128)} fusion(f32[512,1152]{1,0:T(8,128)S(1)} %convolution_add_fusion.7, bf16[512,1152]{1,0:T(8,128)(2,1)S(1)} %fusion.31, bf16[1152,1152]{1,0:T(8,128)(2,1)} %bitcast.29), kind=kOutput, calls=%fused_computation.29 | convolution fusion | flops 1359544320 | bytes 8552448 | tf_op jit(solution)/shard_map/dot_general | solution.py:37
  282.3 7.7 %shard_map.257 = (bf16[512,1152]{1,0:T(8,128)(2,1)}, f32[512,1152]{1,0:T(8,128)}, bf16[512,1152]{1,0:T(8,128)(2,1)}, f32[2,6,1152]{2,1,0:T(8,128)}) custom-call(f32[2]{0:T(128)} %copy-done.54, bf16[512,1152]{1,0:T(8,128)(2,1)} %bitcast.134, f32[512,1152]{1,0:T(8,128)} %get-tuple-element.930.branch_ref, f32[512,1152]{1,0:T(8,128)} %convolution_add_fusion.4.out_ref, ...), custom_call_target="tpu_custom_call" | custom-call | tf_op jit(solution)/shard_map/pallas_call | solution.py:516
  300.9 4.3 collective-permute-start.51
  307.4 13.6 %shard_map.258 = (bf16[512,1152]{1,0:T(8,128)(2,1)S(1)}, bf16[512,1152]{1,0:T(8,128)(2,1)S(1)}, bf16[512,1152]{1,0:T(8,128)(2,1)S(1)}, f32[2,2,1152]{2,1,0:T(2,128)S(1)}) custom-call(bf16[512,1152]{1,0:T(8,128)(2,1)S(1)} %copy-done.7, bf16[512,1152]{1,0:T(8,128)(2,1)S(1)} %copy-done.9, bf16[512,1152]{1,0:T(8,128)(2,1)S(1)} %copy-done.11, ...), custom_call_target="tpu_custom_call" | custom-call | tf_op jit(solution)/shard_map/pallas_call | solution.py:152
  324.9 5.4 %collective-permute-done.51 = bf16[288,1152]{1,0:T(8,128)(2,1)S(1)} collective-permute-done((bf16[288,1152]{1,0:T(8,128)(2,1)S(1)}, bf16[288,1152]{1,0:T(8,128)(2,1)S(1)}, u32[]{:S(2)}, u32[]{:S(2)}) %collective-permute-start.51) | collective-permute-done | bytes 663584 | tf_op jit(solution)/shard_map/ppermute | solution.py:851
  330.2 5.0 %collective-permute-done.52 = bf16[288,1152]{1,0:T(8,128)(2,1)S(1)} collective-permute-done((bf16[288,1152]{1,0:T(8,128)(2,1)S(1)}, bf16[288,1152]{1,0:T(8,128)(2,1)S(1)}, u32[]{:S(2)}, u32[]{:S(2)}) %collective-permute-start.52) | collective-permute-done | bytes 663584 | tf_op jit(solution)/shard_map/ppermute | solution.py:860
  340.5 3.5 convolution_convert_fusion.1
  345.7 7.5 %collective-permute-done.58 = bf16[288,1152]{1,0:T(8,128)(2,1)S(1)} collective-permute-done((bf16[288,1152]{1,0:T(8,128)(2,1)S(1)}, bf16[288,1152]{1,0:T(8,128)(2,1)S(1)}, u32[]{:S(2)}, u32[]{:S(2)}) %collective-permute-start.58) | collective-permute-done | bytes 663584 | tf_op jit(solution)/shard_map/ppermute | solution.py:860
  359.7 13.5 %shard_map.259 = (f32[512,1152]{1,0:T(8,128)}, f32[2,2,1152]{2,1,0:T(2,128)S(1)}) custom-call(s32[4]{0:T(128)S(1)} %pad_add_fusion.order_ref, bf16[512,1152]{1,0:T(8,128)(2,1)S(1)} %get-tuple-element.1027.query_ref, bf16[512,1152]{1,0:T(8,128)(2,1)S(1)} %get-tuple-element.1028.key_ref, bf16[512,1152]{1,0:T(8,128)(2,1)S(1)} %get-tuple-element.1029.value_ref, ...), custom_call_target="tpu_custom_call" | custom-call | tf_op jit(solution)/shard_map/pallas_call | solution.py:581
  388.3 8.7 %collective-permute-done.63 = bf16[288,1152]{1,0:T(8,128)(2,1)S(1)} collective-permute-done((bf16[288,1152]{1,0:T(8,128)(2,1)S(1)}, bf16[288,1152]{1,0:T(8,128)(2,1)S(1)}, u32[]{:S(2)}, u32[]{:S(2)}) %collective-permute-start.63) | collective-permute-done | bytes 663584 | tf_op jit(solution)/shard_map/ppermute | solution.py:860
  397.0 5.2 %collective-permute-done.62 = bf16[288,1152]{1,0:T(8,128)(2,1)S(1)} collective-permute-done((bf16[288,1152]{1,0:T(8,128)(2,1)S(1)}, bf16[288,1152]{1,0:T(8,128)(2,1)S(1)}, u32[]{:S(2)}, u32[]{:S(2)}) %collective-permute-start.62) | collective-permute-done | bytes 663584 | tf_op jit(solution)/shard_map/ppermute | solution.py:851
  407.7 12.8 %collective-permute-done.70 = bf16[8,12672]{1,0:T(8,128)(2,1)S(1)} collective-permute-done((bf16[8,12672]{1,0:T(8,128)(2,1)S(1)}, bf16[8,12672]{1,0:T(8,128)(2,1)S(1)}, u32[]{:S(2)}, u32[]{:S(2)}) %collective-permute-start.70) | collective-permute-done | bytes 202784 | tf_op jit(solution)/shard_map/ppermute | solution.py:959
  424.2 6.0 %collective-permute-done.74 = bf16[16,12672]{1,0:T(8,128)(2,1)S(1)} collective-permute-done((bf16[16,12672]{1,0:T(8,128)(2,1)S(1)}, bf16[16,12672]{1,0:T(8,128)(2,1)S(1)}, u32[]{:S(2)}, u32[]{:S(2)}) %collective-permute-start.74) | collective-permute-done | bytes 405536 | tf_op jit(solution)/shard_map/ppermute | solution.py:857
  431.4 8.9 %collective-permute-done.72 = bf16[288,1152]{1,0:T(8,128)(2,1)S(1)} collective-permute-done((bf16[288,1152]{1,0:T(8,128)(2,1)S(1)}, bf16[288,1152]{1,0:T(8,128)(2,1)S(1)}, u32[]{:S(2)}, u32[]{:S(2)}) %collective-permute-start.72) | collective-permute-done | bytes 663584 | tf_op jit(solution)/shard_map/ppermute | solution.py:860
  451.8 4.0 fusion.102
  472.5 5.3 %collective-permute-done.87 = f32[2,2,144]{2,1,0:T(2,128)S(1)} collective-permute-done((f32[2,2,144]{2,1,0:T(2,128)S(1)}, f32[2,2,144]{2,1,0:T(2,128)S(1)}, u32[]{:S(2)}, u32[]{:S(2)}) %collective-permute-start.87) | collective-permute-done | bytes 2336 | tf_op jit(solution)/shard_map/ppermute | solution.py:959
  (523 shorter events, 264.1 us)
Async XLA Ops:
  5.8 18.4 %collective-permute-start.1 = (bf16[2,144,1152]{2,1,0:T(8,128)(2,1)S(1)}, bf16[2,144,1152]{2,1,0:T(8,128)(2,1)S(1)}, u32[]{:S(2)}, u32[]{:S(2)}) collective-permute-start(bf16[2,144,1152]{2,1,0:T(8,128)(2,1)S(1)} %pad_maximum_fusion.1.refs_0_), channel_id=1, source_target_pairs={{0,4},{4,0},{8,12},{12,8},{16,20},{20,16},{24,28},{28,24},{1,5},{5... | collective-permute-start | bytes 1990664 | tf_op jit(solution)/shard_map/ppermute | solution.py:857
  8.8 18.4 %collective-permute-start = (bf16[2,144,1152]{2,1,0:T(8,128)(2,1)S(1)}, bf16[2,144,1152]{2,1,0:T(8,128)(2,1)}, u32[]{:S(2)}, u32[]{:S(2)}) collective-permute-start(bf16[2,144,1152]{2,1,0:T(8,128)(2,1)S(1)} %pad_maximum_fusion.1.refs_0_), channel_id=1, source_target_pairs={{0,8},{4,12},{8,16},{12,20},{16,24},{20,28},{24,0},{28,4},{1,9},{5... | collective-permute-start | bytes 1990664 | tf_op jit(solution)/shard_map/ppermute | solution.py:851
  49.6 19.8 %collective-permute-start.8 = (bf16[2,144,1152]{2,1,0:T(8,128)(2,1)}, bf16[2,144,1152]{2,1,0:T(8,128)(2,1)}, u32[]{:S(2)}, u32[]{:S(2)}) collective-permute-start(bf16[2,144,1152]{2,1,0:T(8,128)(2,1)} %collective-permute-done.3.refs_2_), channel_id=1, source_target_pairs={{0,4},{4,0},{8,12},{12,8},{16,20},{20,16},{24,28},{28,24},{1,5},{5... | collective-permute-start | bytes 1990664 | tf_op jit(solution)/shard_map/ppermute | solution.py:857
  71.1 21.9 %collective-permute-start.11 = (bf16[2,144,1152]{2,1,0:T(8,128)(2,1)}, bf16[2,144,1152]{2,1,0:T(8,128)(2,1)}, u32[]{:S(2)}, u32[]{:S(2)}) collective-permute-start(bf16[2,144,1152]{2,1,0:T(8,128)(2,1)} %collective-permute-done.7.refs_3_), channel_id=1, source_target_pairs={{0,4},{4,0},{8,12},{12,8},{16,20},{20,16},{24,28},{28,24},{1,5},{5... | collective-permute-start | bytes 1990664 | tf_op jit(solution)/shard_map/ppermute | solution.py:857
  124.3 27.8 %collective-permute-start.25 = (bf16[1152,1152]{1,0:T(8,128)(2,1)}, bf16[1152,1152]{1,0:T(8,128)(2,1)}, u32[]{:S(2)}, u32[]{:S(2)}) collective-permute-start(bf16[1152,1152]{1,0:T(8,128)(2,1)} %bitcast.21), channel_id=1, source_target_pairs={{0,1},{1,0},{2,3},{3,2},{4,5},{5,4},{6,7},{7,6},{8,9},{9,8},{10,11... | collective-permute-start | bytes 7962632 | tf_op jit(solution)/shard_map/ppermute | solution.py:863
  125.3 26.8 %collective-permute-start.29 = (bf16[2,144,1152]{2,1,0:T(8,128)(2,1)}, bf16[2,144,1152]{2,1,0:T(8,128)(2,1)}, u32[]{:S(2)}, u32[]{:S(2)}) collective-permute-start(bf16[2,144,1152]{2,1,0:T(8,128)(2,1)} %pad_maximum_fusion.2), channel_id=1, source_target_pairs={{0,4},{4,0},{8,12},{12,8},{16,20},{20,16},{24,28},{28,24},{1,5},{5... | collective-permute-start | bytes 1990664 | tf_op jit(solution)/shard_map/ppermute | solution.py:857
  126.3 25.8 %collective-permute-start.28 = (bf16[1,144,1152]{2,1,0:T(8,128)(2,1)S(1)}, bf16[1,144,1152]{2,1,0:T(8,128)(2,1)}, u32[]{:S(2)}, u32[]{:S(2)}) collective-permute-start(bf16[1,144,1152]{2,1,0:T(8,128)(2,1)S(1)} %copy-done.21), channel_id=1, source_target_pairs={{0,4},{4,0},{8,12},{12,8},{16,20},{20,16},{24,28},{28,24},{1,5},{5... | collective-permute-start | bytes 995336 | tf_op jit(solution)/shard_map/ppermute | solution.py:857
  127.3 24.8 %collective-permute-start.27 = (bf16[1,144,1152]{2,1,0:T(8,128)(2,1)}, bf16[1,144,1152]{2,1,0:T(8,128)(2,1)}, u32[]{:S(2)}, u32[]{:S(2)}) collective-permute-start(bf16[1,144,1152]{2,1,0:T(8,128)(2,1)} %collective-permute-done.13.refs_1_), channel_id=1, source_target_pairs={{0,8},{4,12},{8,16},{12,20},{16,24},{20,28},{24,0},{28,4},{1,9},{5... | collective-permute-start | bytes 995336 | tf_op jit(solution)/shard_map/ppermute | solution.py:851
  127.5 24.6 %collective-permute-start.26 = (bf16[1,144,1152]{2,1,0:T(8,128)(2,1)}, bf16[1,144,1152]{2,1,0:T(8,128)(2,1)}, u32[]{:S(2)}, u32[]{:S(2)}) collective-permute-start(bf16[1,144,1152]{2,1,0:T(8,128)(2,1)} %collective-permute-done.13.refs_1_), channel_id=1, source_target_pairs={{0,2},{1,3},{2,0},{3,1},{4,6},{5,7},{6,4},{7,5},{8,10},{9,11},{10,... | collective-permute-start | bytes 995336 | tf_op jit(solution)/shard_map/ppermute | solution.py:860
  155.1 20.4 %collective-permute-start.30 = (bf16[1152,1152]{1,0:T(8,128)(2,1)}, bf16[1152,1152]{1,0:T(8,128)(2,1)}, u32[]{:S(2)}, u32[]{:S(2)}) collective-permute-start(bf16[1152,1152]{1,0:T(8,128)(2,1)} %bitcast.29), channel_id=1, source_target_pairs={{0,1},{1,0},{2,3},{3,2},{4,5},{5,4},{6,7},{7,6},{8,9},{9,8},{10,11... | collective-permute-start | bytes 7962632 | tf_op jit(solution)/shard_map/ppermute | solution.py:863
  155.2 19.3 %collective-permute-start.34 = (bf16[1,144,1152]{2,1,0:T(8,128)(2,1)}, bf16[1,144,1152]{2,1,0:T(8,128)(2,1)S(1)}, u32[]{:S(2)}, u32[]{:S(2)}) collective-permute-start(bf16[1,144,1152]{2,1,0:T(8,128)(2,1)} %collective-permute-done.27.refs_2_), channel_id=1, source_target_pairs={{0,4},{4,0},{8,12},{12,8},{16,20},{20,16},{24,28},{28,24},{1,5},{5... | collective-permute-start | bytes 995336 | tf_op jit(solution)/shard_map/ppermute | solution.py:857
  155.7 18.7 %collective-permute-start.31 = (bf16[1,144,1152]{2,1,0:T(8,128)(2,1)}, bf16[1,144,1152]{2,1,0:T(8,128)(2,1)S(1)}, u32[]{:S(2)}, u32[]{:S(2)}) collective-permute-start(bf16[1,144,1152]{2,1,0:T(8,128)(2,1)} %collective-permute-done.27.refs_2_), channel_id=1, source_target_pairs={{0,8},{4,12},{8,16},{12,20},{16,24},{20,28},{24,0},{28,4},{1,9},{5... | collective-permute-start | bytes 995336 | tf_op jit(solution)/shard_map/ppermute | solution.py:851
  175.4 19.4 %collective-permute-start.37 = (bf16[1152,1152]{1,0:T(8,128)(2,1)}, bf16[1152,1152]{1,0:T(8,128)(2,1)}, u32[]{:S(2)}, u32[]{:S(2)}) collective-permute-start(bf16[1152,1152]{1,0:T(8,128)(2,1)} %convolution_convert_fusion.7), channel_id=1, source_target_pairs={{0,1},{1,0},{2,3},{3,2},{4,5},{5,4},{6,7},{7,6},{8,9},{9,8},{10,11... | collective-permute-start | bytes 7962632 | tf_op jit(solution)/shard_map/ppermute | solution.py:863
  194.9 21.4 %collective-permute-start.39 = (bf16[2,144,1152]{2,1,0:T(8,128)(2,1)S(1)}, bf16[2,144,1152]{2,1,0:T(8,128)(2,1)S(1)}, u32[]{:S(2)}, u32[]{:S(2)}) collective-permute-start(bf16[2,144,1152]{2,1,0:T(8,128)(2,1)S(1)} %pad_maximum_fusion.5), channel_id=1, source_target_pairs={{0,2},{1,3},{2,0},{3,1},{4,6},{5,7},{6,4},{7,5},{8,10},{9,11},{10,... | collective-permute-start | bytes 1990664 | tf_op jit(solution)/shard_map/ppermute | solution.py:860
  218.0 19.2 %collective-permute-start.42 = (bf16[288,1152]{1,0:T(8,128)(2,1)S(1)}, bf16[288,1152]{1,0:T(8,128)(2,1)S(1)}, u32[]{:S(2)}, u32[]{:S(2)}) collective-permute-start(bf16[288,1152]{1,0:T(8,128)(2,1)S(1)} %add_convert_fusion.17), channel_id=1, source_target_pairs={{0,8},{4,12},{8,16},{12,20},{16,24},{20,28},{24,0},{28,4},{1,9},{5... | collective-permute-start | bytes 1990664 | tf_op jit(solution)/shard_map/ppermute | solution.py:851
  238.7 19.0 %collective-permute-start.45 = (bf16[288,1152]{1,0:T(8,128)(2,1)S(1)}, bf16[288,1152]{1,0:T(8,128)(2,1)S(1)}, u32[]{:S(2)}, u32[]{:S(2)}) collective-permute-start(bf16[288,1152]{1,0:T(8,128)(2,1)S(1)} %add_convert_fusion.16), channel_id=1, source_target_pairs={{0,8},{4,12},{8,16},{12,20},{16,24},{20,28},{24,0},{28,4},{1,9},{5... | collective-permute-start | bytes 1990664 | tf_op jit(solution)/shard_map/ppermute | solution.py:851
  258.0 18.3 %collective-permute-start.47 = (bf16[144,1152]{1,0:T(8,128)(2,1)S(1)}, bf16[144,1152]{1,0:T(8,128)(2,1)S(1)}, u32[]{:S(2)}, u32[]{:S(2)}) collective-permute-start(bf16[144,1152]{1,0:T(8,128)(2,1)S(1)} %constant_dynamic-slice_fusion.9), channel_id=1, source_target_pairs={{0,4},{4,0},{8,12},{12,8},{16,20},{20,16},{24,28},{28,24},{1,5},{5... | collective-permute-start | bytes 995336 | tf_op jit(solution)/shard_map/ppermute | solution.py:857
  278.8 18.2 %collective-permute-start.50 = (bf16[288,1152]{1,0:T(8,128)(2,1)}, bf16[288,1152]{1,0:T(8,128)(2,1)}, u32[]{:S(2)}, u32[]{:S(2)}) collective-permute-start(bf16[288,1152]{1,0:T(8,128)(2,1)} %add_convert_fusion.14), channel_id=1, source_target_pairs={{0,8},{4,12},{8,16},{12,20},{16,24},{20,28},{24,0},{28,4},{1,9},{5... | collective-permute-start | bytes 1990664 | tf_op jit(solution)/shard_map/ppermute | solution.py:851
  299.0 25.8 %collective-permute-start.54 = (bf16[288,1152]{1,0:T(8,128)(2,1)S(1)}, bf16[288,1152]{1,0:T(8,128)(2,1)S(1)}, u32[]{:S(2)}, u32[]{:S(2)}) collective-permute-start(bf16[288,1152]{1,0:T(8,128)(2,1)S(1)} %add_convert_fusion.12), channel_id=1, source_target_pairs={{0,8},{4,12},{8,16},{12,20},{16,24},{20,28},{24,0},{28,4},{1,9},{5... | collective-permute-start | bytes 1990664 | tf_op jit(solution)/shard_map/ppermute | solution.py:851
  300.9 29.4 %collective-permute-start.51 = (bf16[288,1152]{1,0:T(8,128)(2,1)S(1)}, bf16[288,1152]{1,0:T(8,128)(2,1)S(1)}, u32[]{:S(2)}, u32[]{:S(2)}) collective-permute-start(bf16[288,1152]{1,0:T(8,128)(2,1)S(1)} %add_convert_fusion.13), channel_id=1, source_target_pairs={{0,8},{4,12},{8,16},{12,20},{16,24},{20,28},{24,0},{28,4},{1,9},{5... | collective-permute-start | bytes 1990664 | tf_op jit(solution)/shard_map/ppermute | solution.py:851
  305.3 24.9 %collective-permute-start.53 = (bf16[288,1152]{1,0:T(8,128)(2,1)S(1)}, bf16[288,1152]{1,0:T(8,128)(2,1)S(1)}, u32[]{:S(2)}, u32[]{:S(2)}) collective-permute-start(bf16[288,1152]{1,0:T(8,128)(2,1)S(1)} %get-tuple-element.1168), channel_id=1, source_target_pairs={{0,2},{1,3},{2,0},{3,1},{4,6},{5,7},{6,4},{7,5},{8,10},{9,11},{10,... | collective-permute-start | bytes 1990664 | tf_op jit(solution)/shard_map/ppermute | solution.py:860
  306.2 29.1 %collective-permute-start.52 = (bf16[288,1152]{1,0:T(8,128)(2,1)S(1)}, bf16[288,1152]{1,0:T(8,128)(2,1)S(1)}, u32[]{:S(2)}, u32[]{:S(2)}) collective-permute-start(bf16[288,1152]{1,0:T(8,128)(2,1)S(1)} %get-tuple-element.1169), channel_id=1, source_target_pairs={{0,2},{1,3},{2,0},{3,1},{4,6},{5,7},{6,4},{7,5},{8,10},{9,11},{10,... | collective-permute-start | bytes 1990664 | tf_op jit(solution)/shard_map/ppermute | solution.py:860
  335.2 21.0 %collective-permute-start.55 = (bf16[1152,1152]{1,0:T(8,128)(2,1)S(1)}, bf16[1152,1152]{1,0:T(8,128)(2,1)S(1)}, u32[]{:S(2)}, u32[]{:S(2)}) collective-permute-start(bf16[1152,1152]{1,0:T(8,128)(2,1)S(1)} %convolution_convert_fusion.3), channel_id=1, source_target_pairs={{0,1},{1,0},{2,3},{3,2},{4,5},{5,4},{6,7},{7,6},{8,9},{9,8},{10,11... | collective-permute-start | bytes 7962632 | tf_op jit(solution)/shard_map/ppermute | solution.py:863
  335.2 21.0 %collective-permute-start.56 = (bf16[1152,1152]{1,0:T(8,128)(2,1)S(1)}, bf16[1152,1152]{1,0:T(8,128)(2,1)S(1)}, u32[]{:S(2)}, u32[]{:S(2)}) collective-permute-start(bf16[1152,1152]{1,0:T(8,128)(2,1)S(1)} %convolution_convert_fusion.2), channel_id=1, source_target_pairs={{0,1},{1,0},{2,3},{3,2},{4,5},{5,4},{6,7},{7,6},{8,9},{9,8},{10,11... | collective-permute-start | bytes 7962632 | tf_op jit(solution)/shard_map/ppermute | solution.py:863
  337.9 18.3 %collective-permute-start.57 = (bf16[288,1152]{1,0:T(8,128)(2,1)S(1)}, bf16[288,1152]{1,0:T(8,128)(2,1)S(1)}, u32[]{:S(2)}, u32[]{:S(2)}) collective-permute-start(bf16[288,1152]{1,0:T(8,128)(2,1)S(1)} %add_convert_fusion.11), channel_id=1, source_target_pairs={{0,8},{4,12},{8,16},{12,20},{16,24},{20,28},{24,0},{28,4},{1,9},{5... | collective-permute-start | bytes 1990664 | tf_op jit(solution)/shard_map/ppermute | solution.py:851
  357.5 18.7 %collective-permute-start.60 = (bf16[288,1152]{1,0:T(8,128)(2,1)}, bf16[288,1152]{1,0:T(8,128)(2,1)}, u32[]{:S(2)}, u32[]{:S(2)}) collective-permute-start(bf16[288,1152]{1,0:T(8,128)(2,1)} %add_convert_fusion.9), channel_id=1, source_target_pairs={{0,2},{1,3},{2,0},{3,1},{4,6},{5,7},{6,4},{7,5},{8,10},{9,11},{10,... | collective-permute-start | bytes 1990664 | tf_op jit(solution)/shard_map/ppermute | solution.py:860
  402.1 18.3 %collective-permute-start.70 = (bf16[8,12672]{1,0:T(8,128)(2,1)S(1)}, bf16[8,12672]{1,0:T(8,128)(2,1)S(1)}, u32[]{:S(2)}, u32[]{:S(2)}) collective-permute-start(bf16[8,12672]{1,0:T(8,128)(2,1)S(1)} %pad_maximum_fusion.7), channel_id=1, source_target_pairs={{0,8},{4,12},{8,0},{12,4},{16,24},{20,28},{24,16},{28,20},{1,9},{5... | collective-permute-start | bytes 608264 | tf_op jit(solution)/shard_map/ppermute | solution.py:959
  402.2 18.3 %collective-permute-start.69 = (bf16[144,1152]{1,0:T(8,128)(2,1)S(1)}, bf16[144,1152]{1,0:T(8,128)(2,1)S(1)}, u32[]{:S(2)}, u32[]{:S(2)}) collective-permute-start(bf16[144,1152]{1,0:T(8,128)(2,1)S(1)} %constant_dynamic-slice_fusion.2), channel_id=1, source_target_pairs={{0,4},{4,0},{8,12},{12,8},{16,20},{20,16},{24,28},{28,24},{1,5},{5... | collective-permute-start | bytes 995336 | tf_op jit(solution)/shard_map/ppermute | solution.py:857
  442.1 22.9 %collective-permute-start.77 = (bf16[144,1152]{1,0:T(8,128)(2,1)S(1)}, bf16[144,1152]{1,0:T(8,128)(2,1)S(1)}, u32[]{:S(2)}, u32[]{:S(2)}) collective-permute-start(bf16[144,1152]{1,0:T(8,128)(2,1)S(1)} %add_convert_fusion.21.refs_0_), channel_id=1, source_target_pairs={{0,1},{1,0},{2,3},{3,2},{4,5},{5,4},{6,7},{7,6},{8,9},{9,8},{10,11... | collective-permute-start | bytes 995336 | tf_op jit(solution)/shard_map/ppermute | solution.py:863
  442.1 22.9 %collective-permute-start.78 = (bf16[144,1152]{1,0:T(8,128)(2,1)S(1)}, bf16[144,1152]{1,0:T(8,128)(2,1)S(1)}, u32[]{:S(2)}, u32[]{:S(2)}) collective-permute-start(bf16[144,1152]{1,0:T(8,128)(2,1)S(1)} %collective-permute-done.73.refs_1_), channel_id=1, source_target_pairs={{0,1},{1,0},{2,3},{3,2},{4,5},{5,4},{6,7},{7,6},{8,9},{9,8},{10,11... | collective-permute-start | bytes 995336 | tf_op jit(solution)/shard_map/ppermute | solution.py:863
  442.6 22.4 %collective-permute-start.80 = (bf16[144,1152]{1,0:T(8,128)(2,1)}, bf16[144,1152]{1,0:T(8,128)(2,1)}, u32[]{:S(2)}, u32[]{:S(2)}) collective-permute-start(bf16[144,1152]{1,0:T(8,128)(2,1)} %add_convert_fusion.23), channel_id=1, source_target_pairs={{0,2},{1,3},{2,0},{3,1},{4,6},{5,7},{6,4},{7,5},{8,10},{9,11},{10,... | collective-permute-start | bytes 995336 | tf_op jit(solution)/shard_map/ppermute | solution.py:860
  446.1 18.9 %collective-permute-start.79 = (bf16[144,1152]{1,0:T(8,128)(2,1)}, bf16[144,1152]{1,0:T(8,128)(2,1)}, u32[]{:S(2)}, u32[]{:S(2)}) collective-permute-start(bf16[144,1152]{1,0:T(8,128)(2,1)} %add_convert_fusion.22), channel_id=1, source_target_pairs={{0,2},{1,3},{2,0},{3,1},{4,6},{5,7},{6,4},{7,5},{8,10},{9,11},{10,... | collective-permute-start | bytes 995336 | tf_op jit(solution)/shard_map/ppermute | solution.py:860
  (164 other events, 1936.1 us)
